TPU v7x, 256 devices: a whole 4x4x8 slice. The times are simulated.
256 devices in a mesh: rep: 16 (over y_lo, z), fsdp: 16 (over y_hi, x, core).
Axes of the slice: x: 4, y: 4 (y_hi: 2, y_lo: 2; y = y_hi * 2 + y_lo), z: 8, core: 2. Of those that a mesh axis runs over, the one named last changes fastest.
Arguments:
- grads: bfloat16 [16, 16, 4, 128, 5120], P('rep', 'fsdp'), may hold values from -6 to 6
- momentum: float32 [16, 4, 128, 5120], P('rep', None, 'fsdp'), may hold values from -6 to 6
- params: float32 [4, 128, 5120], P(None, 'fsdp'), may hold values from -6 to 6
- band: int32 [4, 128, 80, 16], P(None, 'fsdp'), may hold values from 0 to 63, as said below
Outputs:
- new_momentum: float32 [16, 4, 128, 5120], P('rep', None, 'fsdp')
- new_params: float32 [4, 128, 5120], P(None, 'fsdp')
Inputs may be any that keep to these rules, and one draw needn't show every extreme that they name: `band`: the 16 indices of one block are distinct.
All inputs are finite; a program needn't handle non-finite values.
Results may differ from a plain program's by a relative error of at most 0.0003.
Values sent between devices are 32-bit elements; how exact they have to be, the bound alone decides.
No kernel may reach another device: no remote copies, remote signals or barrier semaphores. Data moves between devices by JAX's collectives and lax.ppermute only.
A program may use at most 64 MiB of HBM per device.

v0:
```python
import jax
import jax.numpy as jnp
from jax import lax
from jax.sharding import PartitionSpec as P

SPAN = 64


def dct_table(width):
    index = jnp.arange(width, dtype=jnp.float32)
    angle = jnp.pi * (2.0 * index[None, :] + 1.0) * index[:, None] / (2.0 * width)
    scales = jnp.where(index == 0.0, jnp.sqrt(1.0 / width), jnp.sqrt(2.0 / width)).astype(
        jnp.float32
    )
    return scales[:, None] * jnp.cos(angle)


def band_inverse(values, select, table):
    dense = jnp.einsum("icj,icjk->ick", values, select, precision=lax.Precision.HIGHEST)
    blocks = jnp.einsum("ick,kn->icn", dense, table, precision=lax.Precision.HIGHEST)
    return blocks.reshape(blocks.shape[0], -1)


def layer_step(summed, moment, indices, table):
    width = table.shape[0]
    row_count = summed.shape[0]
    count = summed.shape[1] // width
    select = (indices[..., None] == jnp.arange(width, dtype=jnp.int32)).astype(jnp.float32)
    pre = 0.9 * moment + summed
    blocks = pre.reshape(row_count, count, width)
    coeffs = jnp.einsum("icn,kn->ick", blocks, table, precision=lax.Precision.HIGHEST)
    values = jnp.einsum("ick,icjk->icj", coeffs, select, precision=lax.Precision.HIGHEST)
    kept = pre - band_inverse(values, select, table)
    return (kept, values, select)


def shards(grads, momentum, params, band):
    table = dct_table(SPAN)
    moment = momentum[0]
    layer_count = grads.shape[2]
    results = []
    summed = lax.psum_scatter(
        grads[0, 0].astype(jnp.float32), "fsdp", scatter_dimension=1, tiled=True
    )
    for layer in range(layer_count):
        results.append(layer_step(summed[layer], moment[layer], band[layer], table))
    kept = jnp.stack([item[0] for item in results])
    values = jnp.stack([item[1] for item in results])
    flat_shape = (values.shape[0], values.shape[1], values.shape[2] * values.shape[3])
    flat_values = values.reshape(flat_shape)
    total = jnp.sum(lax.all_gather(flat_values[None], "rep", axis=0, tiled=True), axis=0)
    mean_values = (total / lax.axis_size("rep")).reshape(values.shape)
    updates = [
        band_inverse(mean_values[layer], results[layer][2], table) for layer in range(layer_count)
    ]
    new_params = params - 0.5 * jnp.stack(updates)
    return (kept[None], new_params)


def solution(mesh):
    placed = (
        P("rep", "fsdp", None, None, None),
        P("rep", None, "fsdp", None),
        P(None, "fsdp", None),
        P(None, "fsdp", None, None),
    )
    return jax.shard_map(
        shards,
        mesh=mesh,
        in_specs=placed,
        out_specs=(P("rep", None, "fsdp", None), P(None, "fsdp", None)),
        check_vma=False,
    )
```

profile of v0, /device:TPU:32, one launch (start us, length us, event | category | flops | bytes accessed | tf_op | source)
XLA Modules:
  0.0 271.6 jit_solution(10023196552845389403)
XLA Ops:
  7.2 7.9 %bitcast_convert_fusion = f32[4,128,5120]{2,1,0:T(8,128)} fusion(bf16[1,1,4,128,5120]{4,3,2,1,0:T(8,128)(2,1)} %param.4), kind=kLoop, calls=%fused_computation | loop fusion | flops 2621440 | bytes 15728640 | tf_op jit(solution)/shard_map/convert_element_type | solution.py:43
  15.1 1.0 copy-done
  16.4 0.9 copy.28
  17.3 0.9 copy.32
  18.6 0.9 copy.24
  19.5 118.1 %reduce-scatter.2.cloned.1.call-done = f32[4,8,5120]{2,1,0:T(8,128)} async-done(((f32[4,128,5120]{2,1,0:T(8,128)}), f32[4,8,5120]{2,1,0:T(8,128)}) %reduce-scatter.2.cloned.1.call-update) | async-done | bytes 655376 | tf_op jit(solution)/shard_map/reduce_scatter | solution.py:42
  137.6 1.2 fusion.109
  139.5 6.8 %fusion.8 = f32[8,80,1,16]{3,2,1,0:T(1,128)S(1)} fusion(f32[8,80,64,1]{2,3,1,0:T(1,128)S(1)} %bitcast.143, s32[8,80,16]{2,1,0:T(8,128)} %copy.28), kind=kOutput, calls=%fused_computation.12 | convolution fusion | flops 8519680 | bytes 245760 | tf_op jit(solution)/shard_map/ick,icjk->icj/dot_general | solution.py:32
  147.8 5.7 %fusion.5 = f32[8,80,1,16]{3,2,1,0:T(1,128)S(1)} fusion(f32[8,80,64,1]{2,3,1,0:T(1,128)S(1)} %bitcast.144, s32[8,80,16]{2,1,0:T(8,128)S(1)} %copy-done.3), kind=kOutput, calls=%fused_computation.8 | convolution fusion | flops 8519680 | bytes 245760 | tf_op jit(solution)/shard_map/ick,icjk->icj/dot_general | solution.py:32
  155.0 5.7 %fusion.2 = f32[8,80,1,16]{3,2,1,0:T(1,128)S(1)} fusion(f32[8,80,64,1]{2,3,1,0:T(1,128)S(1)} %bitcast.145, s32[8,80,16]{2,1,0:T(8,128)S(1)} %copy.36), kind=kOutput, calls=%fused_computation.4 | convolution fusion | flops 8519680 | bytes 245760 | tf_op jit(solution)/shard_map/ick,icjk->icj/dot_general | solution.py:32
  162.1 5.7 %fusion.11 = f32[8,80,1,16]{3,2,1,0:T(1,128)S(1)} fusion(f32[8,80,64,1]{2,3,1,0:T(1,128)S(1)} %bitcast.146, s32[8,80,16]{2,1,0:T(8,128)S(1)} %copy-done.6), kind=kOutput, calls=%fused_computation.16 | convolution fusion | flops 8519680 | bytes 245760 | tf_op jit(solution)/shard_map/ick,icjk->icj/dot_general | solution.py:32
  167.7 0.7 copy-done.13
  168.6 0.7 pad_maximum_fusion
  169.4 4.3 %fusion.7 = f32[8,80,1,64]{3,2,1,0:T(1,128)S(1)} fusion(s32[8,80,16]{2,1,0:T(8,128)S(1)} %copy-done.5, f32[8,80,1,16]{3,2,1,0:T(1,128)S(1)} %copy-done.8), kind=kOutput, calls=%fused_computation.11 | convolution fusion | flops 8519680 | bytes 245760 | tf_op jit(solution)/shard_map/icj,icjk->ick/dot_general | solution.py:19
  173.6 0.6 fusion.56
  174.4 4.3 %fusion.4 = f32[8,80,1,64]{3,2,1,0:T(1,128)S(1)} fusion(s32[8,80,16]{2,1,0:T(8,128)S(1)} %copy-done.3, f32[8,80,1,16]{3,2,1,0:T(1,128)S(1)} %copy-done.10), kind=kOutput, calls=%fused_computation.7 | convolution fusion | flops 8519680 | bytes 245760 | tf_op jit(solution)/shard_map/icj,icjk->ick/dot_general | solution.py:19
  178.7 0.6 fusion.54
  179.5 4.3 %fusion.1 = f32[8,80,1,64]{3,2,1,0:T(1,128)S(1)} fusion(s32[8,80,16]{2,1,0:T(8,128)S(1)} %copy.36, f32[8,80,1,16]{3,2,1,0:T(1,128)S(1)} %copy-done.12), kind=kOutput, calls=%fused_computation.3 | convolution fusion | flops 8519680 | bytes 245760 | tf_op jit(solution)/shard_map/icj,icjk->ick/dot_general | solution.py:19
  183.7 0.6 fusion.52
  184.5 4.5 %fusion.10 = f32[8,80,1,64]{3,2,1,0:T(1,128)S(1)} fusion(s32[8,80,16]{2,1,0:T(8,128)S(1)} %copy-done.6, f32[8,80,1,16]{3,2,1,0:T(1,128)} %copy-done.13), kind=kOutput, calls=%fused_computation.15 | convolution fusion | flops 8519680 | bytes 245760 | tf_op jit(solution)/shard_map/icj,icjk->ick/dot_general | solution.py:19
  189.0 0.6 fusion.58
  189.8 0.9 maximum_bitcast_fusion
  190.7 50.2 %all-gather.2.cloned.1.call-done = f32[16,4,8,1280]{3,2,1,0:T(8,128)} async-done(((f32[1,4,8,1280]{3,2,1,0:T(8,128)}), f32[16,4,8,1280]{3,2,1,0:T(8,128)}) %all-gather.2.cloned.1.call-update) | async-done | bytes 2621456 | tf_op jit(solution)/shard_map/all_gather | solution.py:51
  240.9 1.9 reduce_sum.9
  243.0 4.3 %fusion.9 = f32[8,80,1,64]{3,2,1,0:T(1,128)S(1)} fusion(f32[8,80,16,1]{2,3,1,0:T(1,128)S(1)} %bitcast.147, s32[8,80,16]{2,1,0:T(8,128)S(1)} %copy-done.6), kind=kOutput, calls=%fused_computation.14 | convolution fusion | flops 8519680 | bytes 245760 | tf_op jit(solution)/shard_map/icj,icjk->ick/dot_general | solution.py:19
  247.3 0.6 fusion.50
  248.2 4.5 %fusion.6 = f32[8,80,1,64]{3,2,1,0:T(1,128)S(1)} fusion(f32[8,80,16,1]{2,3,1,0:T(1,128)S(1)} %bitcast.149, s32[8,80,16]{2,1,0:T(8,128)S(1)} %copy-done.5), kind=kOutput, calls=%fused_computation.10 | convolution fusion | flops 8519680 | bytes 245760 | tf_op jit(solution)/shard_map/icj,icjk->ick/dot_general | solution.py:19
  252.7 0.6 fusion.48
  253.6 4.3 %fusion.3 = f32[8,80,1,64]{3,2,1,0:T(1,128)S(1)} fusion(f32[8,80,16,1]{2,3,1,0:T(1,128)S(1)} %bitcast.151, s32[8,80,16]{2,1,0:T(8,128)S(1)} %copy-done.4), kind=kOutput, calls=%fused_computation.6 | convolution fusion | flops 8519680 | bytes 245760 | tf_op jit(solution)/shard_map/icj,icjk->ick/dot_general | solution.py:19
  258.8 4.3 %fusion = f32[8,80,1,64]{3,2,1,0:T(1,128)S(1)} fusion(f32[8,80,16,1]{2,3,1,0:T(1,128)S(1)} %bitcast.153, s32[8,80,16]{2,1,0:T(8,128)S(1)} %copy.36), kind=kOutput, calls=%fused_computation.2 | convolution fusion | flops 8519680 | bytes 245760 | tf_op jit(solution)/shard_map/icj,icjk->ick/dot_general | solution.py:19
  263.1 0.6 fusion.44
  263.8 0.9 fusion.24
  (68 shorter events, 8.4 us)
Async XLA Ops:
  7.2 130.5 %reduce-scatter.2.cloned.1.call-start = ((), (), s32[]{:S(2)}) async-start(), calls=%async_computation.1 | async-start | bytes 11141120 | tf_op jit(solution)/shard_map/reduce_scatter | solution.py:42
  15.1 1.1 copy-start
  15.1 1.3 copy-start.14
  15.1 225.8 %all-gather.2.cloned.1.call-start = ((), (), s32[]{:S(2)}) async-start(), calls=%async_computation.2 | async-start | bytes 2785280 | tf_op jit(solution)/shard_map/all_gather | solution.py:51
  139.5 8.3 %copy-start.3 = (s32[8,80,16]{2,1,0:T(8,128)S(1)}, s32[8,80,16]{2,1,0:T(8,128)}, u32[]{:S(2)}) copy-start(s32[8,80,16]{2,1,0:T(8,128)} %copy.32) | copy-start | bytes 122884
  146.4 0.7 copy-start.7
  153.5 0.7 copy-start.9
  154.9 7.1 %copy-start.6 = (s32[8,80,16]{2,1,0:T(8,128)S(1)}, s32[8,80,16]{2,1,0:T(8,128)}, u32[]{:S(2)}) copy-start(s32[8,80,16]{2,1,0:T(8,128)} %copy.24) | copy-start | bytes 122884
  160.6 0.7 copy-start.11
  161.4 7.9 %copy-start.5 = (s32[8,80,16]{2,1,0:T(8,128)S(1)}, s32[8,80,16]{2,1,0:T(8,128)}, u32[]{:S(2)}) copy-start(s32[8,80,16]{2,1,0:T(8,128)} %copy.28) | copy-start | bytes 122884
  161.4 7.9 %copy-start.8 = (f32[8,80,1,16]{3,2,1,0:T(1,128)S(1)}, f32[8,80,1,16]{3,2,1,0:T(1,128)}, u32[]{:S(2)}) copy-start(f32[8,80,1,16]{3,2,1,0:T(1,128)} %copy-done.7) | copy-start | bytes 122884
  167.7 0.7 copy-start.13
  168.6 5.8 %copy-start.10 = (f32[8,80,1,16]{3,2,1,0:T(1,128)S(1)}, f32[8,80,1,16]{3,2,1,0:T(1,128)}, u32[]{:S(2)}) copy-start(f32[8,80,1,16]{3,2,1,0:T(1,128)} %copy-done.9) | copy-start | bytes 122884
  174.3 5.2 %copy-start.12 = (f32[8,80,1,16]{3,2,1,0:T(1,128)S(1)}, f32[8,80,1,16]{3,2,1,0:T(1,128)}, u32[]{:S(2)}) copy-start(f32[8,80,1,16]{3,2,1,0:T(1,128)} %copy-done.11) | copy-start | bytes 122884
  184.4 5.4 %copy-start.1 = (f32[4,8,5120]{2,1,0:T(8,128)S(1)}, f32[4,8,5120]{2,1,0:T(8,128)}, u32[]{:S(2)}) copy-start(f32[4,8,5120]{2,1,0:T(8,128)} %reduce-scatter.2.cloned.1.call-done) | copy-start | bytes 1966084
  248.0 5.6 %copy-start.4 = (s32[8,80,16]{2,1,0:T(8,128)S(1)}, s32[8,80,16]{2,1,0:T(8,128)}, u32[]{:S(2)}) copy-start(s32[8,80,16]{2,1,0:T(8,128)} %copy.32) | copy-start | bytes 122884
  258.5 5.3 %copy-start.2 = (f32[4,8,5120]{2,1,0:T(8,128)S(1)}, f32[4,8,5120]{2,1,0:T(8,128)}, u32[]{:S(2)}) copy-start(f32[4,8,5120]{2,1,0:T(8,128)} %param.6) | copy-start | bytes 1966084
Sparse Core Ops, SparseCore 0:
  15.2 122.3 reduce-scatter.1
  169.5 71.4 all-gather.1
where the time goes:
time: 273 us; the launch traced here: 272 us
  waiting for transfers between devices  168 us (62%)
  matrix products  65.6 us (24%)
  between operations  14.5 us (5%)
  other arithmetic  12.4 us (5%)
  local copies, waits for them, and re-layouts  10.6 us (4%)
    reduce_scatter x1, waiting for transfers between devices, shards(): lax.psum_scatter(grads[0, 0].astype(jnp.float32), 'fsdp', scatter_dimensi...  118 us
    all_gather x1, waiting for transfers between devices, shards(): lax.all_gather(flat_values[None], 'rep', axis=0, tiled=True)  50.2 us
    dot_general x8, matrix products, band_inverse(): jnp.einsum('icj,icjk->ick', values, select, precision=lax.Precision.HIGHEST)  34.7 us
    dot_general x4, matrix products, layer_step(): jnp.einsum('ick,icjk->icj', coeffs, select, precision=lax.Precision.HIGHEST)  23.8 us
    convert_element_type x1, other arithmetic, shards(): grads[0, 0].astype(jnp.float32)  7.85 us
  transfers between devices with their start and end apart: 2, of which 2 were waited for; matrix products, arithmetic and copies ran while one was open for 9% of the time, Pallas kernels for 0%

commit v1 on v0

v1 whole, which is shorter than its diff:
```python
import jax
import jax.numpy as jnp
import numpy as np
from jax import lax
from jax.experimental import pallas as pl
from jax.experimental.pallas import tpu as pltpu
from jax.sharding import PartitionSpec as P

SPAN = 64
BAND = 16
LANES = 128
EXACT = lax.Precision.HIGHEST
CHUNKS = ((0, 2), (2, 2))
ORDERS = ((1, 2, 0), (2, 0, 1), (0, 1, 2))


def table128():
    k = np.arange(SPAN, dtype=np.float64)[:, None]
    n = np.arange(SPAN, dtype=np.float64)[None, :]
    scale = np.where(k == 0, np.sqrt(1.0 / SPAN), np.sqrt(2.0 / SPAN))
    table = (scale * np.cos(np.pi * (2 * n + 1) * k / (2 * SPAN))).astype(np.float32)
    wide = np.zeros((LANES, LANES), np.float32)
    wide[:SPAN, :SPAN] = table
    wide[SPAN:, SPAN:] = table
    return jnp.asarray(wide)


def fsdp_index(y, x, c):
    return (y * 4 + x) * 2 + c


def fsdp_pairs(step):
    return [
        (fsdp_index(y, x, c), fsdp_index(*step(y, x, c)))
        for y in range(2)
        for x in range(4)
        for c in range(2)
    ]


CORE = fsdp_pairs(lambda y, x, c: (y, x, 1 - c))
HALVES = (
    fsdp_pairs(lambda y, x, c: (1 - y, x, c)),
    fsdp_pairs(lambda y, x, c: (y, x ^ 1, c)),
    fsdp_pairs(lambda y, x, c: (y, 3 - x, c)),
)


def rep_pairs(mask):
    return [(i, i ^ mask) for i in range(16)]


def split_cores(grads, chips, core, first, count):
    width = grads.shape[2]

    def kernel(chips_ref, core_ref, grads_ref, other_ref, own_ref):
        both = grads_ref[...].astype(jnp.float32)
        low, high = both[:, :8], both[:, 8:]
        is_low = core_ref[0] == 0
        own_ref[0] = jnp.where(is_low, low, high)
        other_ref[0] = jnp.where(is_low, high, low)

    out = jax.ShapeDtypeStruct((8, count, 8, width), jnp.float32)
    spec = pl.BlockSpec((1, count, 8, width), lambda i, chips, core: (i, 0, 0, 0))
    return pl.pallas_call(
        kernel,
        grid_spec=pltpu.PrefetchScalarGridSpec(
            num_scalar_prefetch=2,
            grid=(8,),
            in_specs=[
                pl.BlockSpec(
                    (count, 16, width), lambda i, chips, core: (first // count, chips[i], 0)
                )
            ],
            out_specs=[spec, spec],
        ),
        out_shape=[out, out],
        compiler_params=pltpu.CompilerParams(vmem_limit_bytes=24 * 2**20),
        name="split_cores",
    )(chips, core, grads)


def padded(count):
    return -(-count // LANES) * LANES


def to_blocks(rows):
    high, wide = rows.shape
    tiles = [rows[:, t * LANES : (t + 1) * LANES] for t in range(wide // LANES)]
    total = high * len(tiles)
    if padded(total) > total:
        tiles.append(jnp.zeros((padded(total) - total, LANES), rows.dtype))
    return jnp.concatenate(tiles, axis=0)


def forward(keeps, recvs, momentum, band, table, first, count):
    rows = 8 * count
    width = momentum.shape[2]
    blocks = band.shape[1]
    parts = len(keeps)

    def kernel(*refs):
        keep_refs, recv_refs = refs[:parts], refs[parts : 2 * parts]
        mom_ref, band_ref, table_ref, values_ref, dense_ref, pre_ref = refs[2 * parts :]
        at = 0
        for k_ref, r_ref in zip(keep_refs, recv_refs):
            wide = k_ref.shape[2]
            part = 0.9 * mom_ref[first : first + count, :, at : at + wide] + (
                k_ref[...] + r_ref[...]
            )
            pre_ref[:, at : at + wide] = part.reshape(rows, wide)
            at += wide
        cut = to_blocks(pre_ref[...])
        coeffs = lax.dot_general(
            table_ref[...],
            cut,
            (((1,), (1,)), ((), ())),
            precision=EXACT,
            preferred_element_type=jnp.float32,
        )
        index = lax.broadcasted_iota(jnp.int32, (SPAN, LANES), 0)
        for tile in range(blocks // LANES):
            lanes = slice(tile * LANES, (tile + 1) * LANES)
            for h in range(2):
                block = coeffs[h * SPAN : (h + 1) * SPAN, lanes]
                kept = jnp.zeros((SPAN, LANES), jnp.float32)
                picked = []
                for j in range(BAND):
                    hit = index == band_ref[h * BAND + j : h * BAND + j + 1, lanes]
                    one = jnp.where(hit, block, 0.0)
                    kept = kept + one
                    picked.append(jnp.sum(one, axis=0, keepdims=True))
                dense_ref[h * SPAN : (h + 1) * SPAN, lanes] = kept
                values_ref[h * BAND : (h + 1) * BAND, lanes] = jnp.concatenate(picked, axis=0)

    shapes = [
        jax.ShapeDtypeStruct((2 * BAND, blocks), jnp.float32),
        jax.ShapeDtypeStruct((LANES, blocks), jnp.float32),
        jax.ShapeDtypeStruct((rows, width), jnp.float32),
    ]
    return pl.pallas_call(
        kernel,
        out_shape=shapes,
        compiler_params=pltpu.CompilerParams(vmem_limit_bytes=24 * 2**20),
        name="forward_dct",
    )(*keeps, *recvs, momentum, band, table)


def inverse(dense, table):
    return lax.dot_general(
        dense,
        table,
        (((0,), (0,)), ((), ())),
        precision=EXACT,
        preferred_element_type=jnp.float32,
    )


def residual(pre, dense, table):
    rows, width = pre.shape

    def kernel(pre_ref, dense_ref, table_ref, out_ref):
        blocks = inverse(dense_ref[...], table_ref[...])
        for t in range(width // LANES):
            lanes = slice(t * LANES, (t + 1) * LANES)
            out_ref[:, lanes] = pre_ref[:, lanes] - blocks[t * rows : (t + 1) * rows]

    return pl.pallas_call(
        kernel,
        out_shape=jax.ShapeDtypeStruct((rows, width), jnp.float32),
        compiler_params=pltpu.CompilerParams(vmem_limit_bytes=24 * 2**20),
        name="residual",
    )(pre, dense, table)


def step_params(params, sums, band, table, replicas, first, count):
    rows = 8 * count
    width = params.shape[2]
    blocks = band.shape[1]

    def kernel(params_ref, s0_ref, s1_ref, s2_ref, s3_ref, band_ref, table_ref, out_ref, dense):
        index = lax.broadcasted_iota(jnp.int32, (SPAN, LANES), 0)
        for tile in range(blocks // LANES):
            lanes = slice(tile * LANES, (tile + 1) * LANES)
            total = (s0_ref[:, lanes] + s1_ref[:, lanes]) + (s2_ref[:, lanes] + s3_ref[:, lanes])
            mean = total / replicas
            for h in range(2):
                spread = jnp.zeros((SPAN, LANES), jnp.float32)
                for j in range(BAND):
                    row = h * BAND + j
                    hit = index == band_ref[row : row + 1, lanes]
                    spread = jnp.where(hit, mean[row : row + 1], spread)
                dense[h * SPAN : (h + 1) * SPAN, lanes] = spread
        update = inverse(dense[...], table_ref[...])
        for t in range(width // LANES):
            lanes = slice(t * LANES, (t + 1) * LANES)
            old = params_ref[first : first + count, :, lanes].reshape(rows, LANES)
            new = old - 0.5 * update[t * rows : (t + 1) * rows]
            out_ref[:, :, lanes] = new.reshape(count, 8, LANES)

    return pl.pallas_call(
        kernel,
        out_shape=jax.ShapeDtypeStruct((count, 8, width), jnp.float32),
        scratch_shapes=[pltpu.VMEM((LANES, blocks), jnp.float32)],
        compiler_params=pltpu.CompilerParams(vmem_limit_bytes=24 * 2**20),
        name="step_params",
    )(params, *sums, band, table)


def band_rows(band, first, count):
    part = band[first : first + count].reshape(count, 8, -1, 2, BAND)
    part = part.transpose(3, 4, 2, 0, 1).reshape(2 * BAND, -1)
    total = part.shape[1]
    return jnp.pad(part, ((0, 0), (0, padded(total) - total)), constant_values=SPAN)


def halve(piece, order):
    left = [0, 1, 2]
    for step, dim in enumerate(order):
        axis = left.index(dim)
        left.remove(dim)
        keep = lax.index_in_dim(piece, 0, axis, keepdims=False)
        send = lax.index_in_dim(piece, 1, axis, keepdims=False)
        recv = lax.ppermute(send, "fsdp", HALVES[dim])
        if step == 2:
            return keep, recv
        piece = keep + recv


def shards(grads, momentum, params, band):
    table = table128()
    grads = grads[0, 0]
    moment = momentum[0]
    width = grads.shape[2]
    replicas = lax.axis_size("rep")
    me = lax.axis_index("fsdp").astype(jnp.int32)
    core = (me % 2).reshape(1)
    x, y = (me // 2) % 4, me // 8
    chips = jnp.stack(
        [
            (y ^ dy) * 4 + column
            for dy in range(2)
            for column in (x, 3 - x, x ^ 1, x ^ 2)
        ]
    )
    tiles = width // LANES
    cuts = [0, (tiles + 2) // 3 * LANES, ((tiles + 2) // 3 + (tiles + 1) // 3) * LANES, width]
    kept, updated = [], []
    for first, count in CHUNKS:
        other, own = split_cores(grads, chips, core, first, count)
        got = lax.ppermute(other, "fsdp", CORE)
        bands = band_rows(band, first, count)
        keeps, recvs = [], []
        for third, order in enumerate(ORDERS):
            cols = slice(cuts[third], cuts[third + 1])
            piece = own[..., cols] + got[..., cols]
            keep, recv = halve(piece.reshape(2, 2, 2, *piece.shape[1:]), order)
            keeps.append(keep)
            recvs.append(recv)
        values, dense, pre = forward(keeps, recvs, moment, bands, table, first, count)
        near = [lax.ppermute(values, "rep", rep_pairs(m)) for m in (1, 2, 3)]
        four = (values + near[0]) + (near[1] + near[2])
        far = [lax.ppermute(four, "rep", rep_pairs(m)) for m in (4, 8, 12)]
        kept.append(residual(pre, dense, table).reshape(count, 8, width))
        updated.append(
            step_params(params, [four] + far, bands, table, replicas, first, count)
        )
    return jnp.concatenate(kept)[None], jnp.concatenate(updated)


def solution(mesh):
    placed = (
        P("rep", "fsdp", None, None, None),
        P("rep", None, "fsdp", None),
        P(None, "fsdp", None),
        P(None, "fsdp", None, None),
    )
    return jax.shard_map(
        shards,
        mesh=mesh,
        in_specs=placed,
        out_specs=(P("rep", None, "fsdp", None), P(None, "fsdp", None)),
        check_vma=False,
    )
```

time: 273 us -> 105 us (0.38)
  waiting for transfers between devices: 168 us -> 25.9 us
  matrix products: 65.6 us -> 0 us
  starting transfers between devices: 0.08 us -> 54.7 us
  between operations: 14.5 us -> 1.08 us
  other arithmetic: 12.4 us -> 2.97 us
  Pallas kernels: 0 us -> 8.29 us
    reduce_scatter x1 -> x0, waiting for transfers between devices: 118 us -> none  [shards(): lax.psum_scatter(grads[0, 0].astype(jnp.float32), 'fsdp', scatter_dimensi...]
    dot_general x24 -> x0, matrix products: 65.6 us -> none  [the longest x8 34.7 us: band_inverse(): jnp.einsum('icj,icjk->ick', values, select, precision=lax.Precision.HIGHEST)]
    ppermute x0 -> x32, starting transfers between devices: none -> 54.7 us  [the longest x18 27.9 us: halve(): recv = lax.ppermute(send, 'fsdp', HALVES[dim])]
    all_gather x1 -> x0, waiting for transfers between devices: 50.2 us -> none  [shards(): lax.all_gather(flat_values[None], 'rep', axis=0, tiled=True)]
    ppermute x0 -> x32, waiting for transfers between devices: none -> 25.9 us  [the longest x18 16.8 us: halve(): recv = lax.ppermute(send, 'fsdp', HALVES[dim])]
    pallas_call x0 -> x8, Pallas kernels: none -> 8.29 us  [the longest x2 2.99 us: split_cores(): pl.pallas_call(kernel, grid_spec=pltpu.PrefetchScalarGridSpec(num_scalar_...]
    convert_element_type x1 -> x0, other arithmetic: 7.85 us -> none  [shards(): grads[0, 0].astype(jnp.float32)]
    eq x5 -> x0, local copies, waits for them, and re-layouts: 2.78 us -> none  [layer_step(): indices[..., None] == jnp.arange(width, dtype=jnp.int32)]
  transfers between devices with their start and end apart: 2 -> 32, of which waited for: 2 -> 6; matrix products, arithmetic and copies ran while one was open for 9% -> 11% of each run, Pallas kernels for 0% -> 6%
where the time goes in v1:
time: 105 us
  starting transfers between devices  54.7 us (52%)
  waiting for transfers between devices  25.9 us (25%)
  local copies, waits for them, and re-layouts  12.1 us (12%)
  Pallas kernels  8.29 us (8%)
  other arithmetic  2.97 us (3%)
  between operations  1.08 us (1%)
    ppermute x18, starting transfers between devices, halve(): recv = lax.ppermute(send, 'fsdp', HALVES[dim])  27.9 us
    ppermute x18, waiting for transfers between devices, halve(): recv = lax.ppermute(send, 'fsdp', HALVES[dim])  16.8 us
    ppermute x6, starting transfers between devices, shards(): far = [lax.ppermute(four, 'rep', rep_pairs(m)) for m in (4, 8, 12)]  16.7 us
    ppermute x6, starting transfers between devices, shards(): near = [lax.ppermute(values, 'rep', rep_pairs(m)) for m in (1, 2, 3)]  9.48 us
    ppermute x6, waiting for transfers between devices, shards(): far = [lax.ppermute(four, 'rep', rep_pairs(m)) for m in (4, 8, 12)]  6.23 us
    squeeze x14, local copies, waits for them, and re-layouts, halve(): send = lax.index_in_dim(piece, 1, axis, keepdims=False)  3.46 us
    pallas_call x2, Pallas kernels, split_cores(): pl.pallas_call(kernel, grid_spec=pltpu.PrefetchScalarGridSpec(num_scalar_...  2.99 us
    ppermute x2, waiting for transfers between devices, shards(): got = lax.ppermute(other, 'fsdp', CORE)  2.81 us
  transfers between devices with their start and end apart: 32, of which 6 were waited for; matrix products, arithmetic and copies ran while one was open for 11% of the time, Pallas kernels for 6%

profile of v1, /device:TPU:32, one launch (start us, length us, event | category | flops | bytes accessed | tf_op | source)
XLA Modules:
  0.0 105.0 jit_solution(15492046901813511965)
XLA Ops:
  0.8 2.5 %copy-done = bf16[1,1,4,128,5120]{4,3,2,1,0:T(8,128)(2,1)S(1)} copy-done((bf16[1,1,4,128,5120]{4,3,2,1,0:T(8,128)(2,1)S(1)}, bf16[1,1,4,128,5120]{4,3,2,1,0:T(8,128)(2,1)}, u32[]{:S(2)}) %copy-start) | copy-done | bytes 5242904
  3.3 1.5 %split_cores.3 = (f32[8,2,8,5120]{3,2,1,0:T(8,128)S(1)}, f32[8,2,8,5120]{3,2,1,0:T(8,128)S(1)}) custom-call(s32[8]{0:T(128)S(1)} %stack.35.chips_ref, s32[1]{0:T(128)} %bitcast.8.core_ref, bf16[4,128,5120]{2,1,0:T(8,128)(2,1)S(1)} %bitcast.127), custom_call_target="tpu_custom_call" | custom-call | tf_op jit(solution)/shard_map/split_cores/pallas_call | solution.py:65
  4.9 1.5 %split_cores.2 = (f32[8,2,8,5120]{3,2,1,0:T(8,128)S(1)}, f32[8,2,8,5120]{3,2,1,0:T(8,128)S(1)}) custom-call(s32[8]{0:T(128)S(1)} %stack.35.chips_ref, s32[1]{0:T(128)} %bitcast.8.core_ref, bf16[4,128,5120]{2,1,0:T(8,128)(2,1)S(1)} %bitcast.128), custom_call_target="tpu_custom_call" | custom-call | tf_op jit(solution)/shard_map/split_cores/pallas_call | solution.py:65
  6.9 2.8 %collective-permute-done.10 = f32[8,2,8,5120]{3,2,1,0:T(8,128)S(1)} collective-permute-done((f32[8,2,8,5120]{3,2,1,0:T(8,128)S(1)}, f32[8,2,8,5120]{3,2,1,0:T(8,128)S(1)}, u32[]{:S(2)}, u32[]{:S(2)}) %collective-permute-start.10) | collective-permute-done | bytes 2621472 | tf_op jit(solution)/shard_map/ppermute | solution.py:251
  10.0 1.6 %collective-permute-start.11 = (f32[2,2,2,8,1792]{4,3,2,0,1:T(8,128)S(1)}, f32[2,2,2,8,1792]{4,3,2,0,1:T(8,128)S(1)}, u32[]{:S(2)}, u32[]{:S(2)}) collective-permute-start(f32[2,2,2,8,1792]{4,3,2,0,1:T(8,128)S(1)} %bitcast.143), channel_id=1, source_target_pairs={{0,2},{1,3},{2,0},{3,1},{4,6},{5,7},{6,4},{7,5},{8,10},{9,11},{10,... | collective-permute-start | bytes 1376264 | tf_op jit(solution)/shard_map/ppermute | solution.py:224
  11.8 2.2 %collective-permute-start.13 = (f32[2,2,2,8,1664]{4,3,2,1,0:T(8,128)S(1)}, f32[2,2,2,8,1664]{4,3,2,1,0:T(8,128)S(1)}, u32[]{:S(2)}, u32[]{:S(2)}) collective-permute-start(f32[2,2,2,8,1664]{4,3,2,1,0:T(8,128)S(1)} %slice_bitcast_fusion), channel_id=1, source_target_pairs={{0,6},{1,7},{2,4},{3,5},{4,2},{5,3},{6,0},{7,1},{8,14},{9,15},{10,... | collective-permute-start | bytes 1277960 | tf_op jit(solution)/shard_map/ppermute | solution.py:224
  14.0 3.3 %collective-permute-start.15 = (f32[2,2,2,8,1664]{4,3,2,1,0:T(8,128)S(1)}, f32[2,2,2,8,1664]{4,3,2,1,0:T(8,128)S(1)}, u32[]{:S(2)}, u32[]{:S(2)}) collective-permute-start(f32[2,2,2,8,1664]{4,3,2,1,0:T(8,128)S(1)} %bitcast.145), channel_id=1, source_target_pairs={{0,8},{1,9},{2,10},{3,11},{4,12},{5,13},{6,14},{7,15},{8,0},{9,1},... | collective-permute-start | bytes 1277960 | tf_op jit(solution)/shard_map/ppermute | solution.py:224
  19.2 6.6 %collective-permute-done.13 = f32[2,2,2,8,1664]{4,3,2,1,0:T(8,128)S(1)} collective-permute-done((f32[2,2,2,8,1664]{4,3,2,1,0:T(8,128)S(1)}, f32[2,2,2,8,1664]{4,3,2,1,0:T(8,128)S(1)}, u32[]{:S(2)}, u32[]{:S(2)}) %collective-permute-start.13) | collective-permute-done | bytes 426016 | tf_op jit(solution)/shard_map/ppermute | solution.py:224
  25.8 3.2 %collective-permute-start.5 = (f32[2,2,2,8,1664]{4,3,2,1,0:T(8,128)S(1)}, f32[2,2,2,8,1664]{4,3,2,1,0:T(8,128)S(1)}, u32[]{:S(2)}, u32[]{:S(2)}) collective-permute-start(f32[2,2,2,8,1664]{4,3,2,1,0:T(8,128)S(1)} %bitcast.146), channel_id=1, source_target_pairs={{0,8},{1,9},{2,10},{3,11},{4,12},{5,13},{6,14},{7,15},{8,0},{9,1},... | collective-permute-start | bytes 1277960 | tf_op jit(solution)/shard_map/ppermute | solution.py:224
  30.2 3.6 %collective-permute-done.3 = f32[2,2,2,8,1664]{4,3,2,1,0:T(8,128)S(1)} collective-permute-done((f32[2,2,2,8,1664]{4,3,2,1,0:T(8,128)S(1)}, f32[2,2,2,8,1664]{4,3,2,1,0:T(8,128)S(1)}, u32[]{:S(2)}, u32[]{:S(2)}) %collective-permute-start.3) | collective-permute-done | bytes 426016 | tf_op jit(solution)/shard_map/ppermute | solution.py:224
  33.9 6.2 %collective-permute-done.5 = f32[2,2,2,8,1664]{4,3,2,1,0:T(8,128)S(1)} collective-permute-done((f32[2,2,2,8,1664]{4,3,2,1,0:T(8,128)S(1)}, f32[2,2,2,8,1664]{4,3,2,1,0:T(8,128)S(1)}, u32[]{:S(2)}, u32[]{:S(2)}) %collective-permute-start.5) | collective-permute-done | bytes 426016 | tf_op jit(solution)/shard_map/ppermute | solution.py:224
  40.1 3.2 %collective-permute-start.4 = (f32[2,2,8,1664]{3,2,1,0:T(8,128)S(1)}, f32[2,2,8,1664]{3,2,1,0:T(8,128)S(1)}, u32[]{:S(2)}, u32[]{:S(2)}) collective-permute-start(f32[2,2,8,1664]{3,2,1,0:T(8,128)S(1)} %slice_bitcast_fusion.14), channel_id=1, source_target_pairs={{0,8},{1,9},{2,10},{3,11},{4,12},{5,13},{6,14},{7,15},{8,0},{9,1},... | collective-permute-start | bytes 638984 | tf_op jit(solution)/shard_map/ppermute | solution.py:224
  43.6 2.2 %collective-permute-start.12 = (f32[2,2,8,1792]{3,2,1,0:T(8,128)S(1)}, f32[2,2,8,1792]{3,2,1,0:T(8,128)S(1)}, u32[]{:S(2)}, u32[]{:S(2)}) collective-permute-start(f32[2,2,8,1792]{3,2,1,0:T(8,128)S(1)} %slice_bitcast_fusion.4), channel_id=1, source_target_pairs={{0,6},{1,7},{2,4},{3,5},{4,2},{5,3},{6,0},{7,1},{8,14},{9,15},{10,... | collective-permute-start | bytes 688136 | tf_op jit(solution)/shard_map/ppermute | solution.py:224
  45.8 1.2 %collective-permute-start.2 = (f32[2,2,8,1792]{3,2,1,0:T(8,128)S(1)}, f32[2,2,8,1792]{3,2,1,0:T(8,128)S(1)}, u32[]{:S(2)}, u32[]{:S(2)}) collective-permute-start(f32[2,2,8,1792]{3,2,1,0:T(8,128)S(1)} %slice_bitcast_fusion.6), channel_id=1, source_target_pairs={{0,6},{1,7},{2,4},{3,5},{4,2},{5,3},{6,0},{7,1},{8,14},{9,15},{10,... | collective-permute-start | bytes 688136 | tf_op jit(solution)/shard_map/ppermute | solution.py:224
  48.6 2.1 %collective-permute-start.19 = (f32[2,8,1664]{2,1,0:T(8,128)}, f32[2,8,1664]{2,1,0:T(8,128)S(1)}, u32[]{:S(2)}, u32[]{:S(2)}) collective-permute-start(f32[2,8,1664]{2,1,0:T(8,128)} %get-tuple-element.44), channel_id=1, source_target_pairs={{0,6},{1,7},{2,4},{3,5},{4,2},{5,3},{6,0},{7,1},{8,14},{9,15},{10,... | collective-permute-start | bytes 319496 | tf_op jit(solution)/shard_map/ppermute | solution.py:224
  52.7 1.4 %collective-permute-start.9 = (f32[2,8,1664]{2,1,0:T(8,128)}, f32[2,8,1664]{2,1,0:T(8,128)S(1)}, u32[]{:S(2)}, u32[]{:S(2)}) collective-permute-start(f32[2,8,1664]{2,1,0:T(8,128)} %get-tuple-element.40), channel_id=1, source_target_pairs={{0,6},{1,7},{2,4},{3,5},{4,2},{5,3},{6,0},{7,1},{8,14},{9,15},{10,... | collective-permute-start | bytes 319496 | tf_op jit(solution)/shard_map/ppermute | solution.py:224
  54.8 1.8 %collective-permute-start.17 = (f32[2,8,1792]{2,1,0:T(8,128)}, f32[2,8,1792]{2,1,0:T(8,128)S(1)}, u32[]{:S(2)}, u32[]{:S(2)}) collective-permute-start(f32[2,8,1792]{2,1,0:T(8,128)} %get-tuple-element.38), channel_id=1, source_target_pairs={{0,8},{1,9},{2,10},{3,11},{4,12},{5,13},{6,14},{7,15},{8,0},{9,1},... | collective-permute-start | bytes 344072 | tf_op jit(solution)/shard_map/ppermute | solution.py:224
  57.3 1.8 %collective-permute-start.7 = (f32[2,8,1792]{2,1,0:T(8,128)}, f32[2,8,1792]{2,1,0:T(8,128)S(1)}, u32[]{:S(2)}, u32[]{:S(2)}) collective-permute-start(f32[2,8,1792]{2,1,0:T(8,128)} %get-tuple-element.36), channel_id=1, source_target_pairs={{0,8},{1,9},{2,10},{3,11},{4,12},{5,13},{6,14},{7,15},{8,0},{9,1},... | collective-permute-start | bytes 344072 | tf_op jit(solution)/shard_map/ppermute | solution.py:224
  61.4 1.3 %forward_dct.3 = (f32[32,640]{1,0:T(8,128)S(1)}, f32[128,640]{1,0:T(8,128)S(1)}, f32[16,5120]{1,0:T(8,128)S(1)}) custom-call(f32[2,8,1792]{2,1,0:T(8,128)S(1)} %get-tuple-element.39.refs_0_, f32[2,8,1664]{2,1,0:T(8,128)S(1)} %get-tuple-element.47.refs_1_, f32[2,8,1664]{2,1,0:T(8,128)S(1)} %get-tuple-element.45.refs_2_, ...), custom_call_target="tpu_custom_call" | custom-call | tf_op jit(solution)/shard_map/forward_dct/pallas_call | solution.py:141
  62.7 3.4 %collective-permute-start.27 = (f32[32,640]{1,0:T(8,128)S(1)}, f32[32,640]{1,0:T(8,128)S(1)}, u32[]{:S(2)}, u32[]{:S(2)}) collective-permute-start(f32[32,640]{1,0:T(8,128)S(1)} %get-tuple-element.21), channel_id=1, source_target_pairs={{0,32},{16,48},{32,0},{48,16},{64,96},{80,112},{96,64},{112,80},{1... | collective-permute-start | bytes 245768 | tf_op jit(solution)/shard_map/ppermute | solution.py:261
  66.0 1.6 %collective-permute-start.26 = (f32[32,640]{1,0:T(8,128)S(1)}, f32[32,640]{1,0:T(8,128)S(1)}, u32[]{:S(2)}, u32[]{:S(2)}) collective-permute-start(f32[32,640]{1,0:T(8,128)S(1)} %get-tuple-element.21), channel_id=1, source_target_pairs={{0,16},{16,0},{32,48},{48,32},{64,80},{80,64},{96,112},{112,96},{1... | collective-permute-start | bytes 245768 | tf_op jit(solution)/shard_map/ppermute | solution.py:261
  68.8 1.2 %copy.14 = s32[2,16,40,2,8]{1,0,4,3,2:T(2,128)} copy(s32[2,16,40,2,8]{1,4,0,2,3:T(8,128)S(1)} %bitcast.140) | data formatting | bytes 163840 | tf_op jit(solution)/shard_map/transpose | solution.py:212
  70.0 1.5 %reshape.51 = s32[32,640]{0,1:T(8,128)S(1)} reshape(s32[2,16,40,2,8]{1,0,4,3,2:T(2,128)} %copy.14) | data formatting | bytes 163840 | tf_op jit(solution)/shard_map/reshape | solution.py:212
  71.6 1.3 %forward_dct.2 = (f32[32,640]{1,0:T(8,128)S(1)}, f32[128,640]{1,0:T(8,128)S(1)}, f32[16,5120]{1,0:T(8,128)S(1)}) custom-call(f32[2,8,1792]{2,1,0:T(8,128)S(1)} %get-tuple-element.37.refs_0_, f32[2,8,1664]{2,1,0:T(8,128)S(1)} %get-tuple-element.43.refs_1_, f32[2,8,1664]{2,1,0:T(8,128)S(1)} %get-tuple-element.41.refs_2_, ...), custom_call_target="tpu_custom_call" | custom-call | tf_op jit(solution)/shard_map/forward_dct/pallas_call | solution.py:141
  72.9 2.0 %collective-permute-start.21 = (f32[32,640]{1,0:T(8,128)S(1)}, f32[32,640]{1,0:T(8,128)S(1)}, u32[]{:S(2)}, u32[]{:S(2)}) collective-permute-start(f32[32,640]{1,0:T(8,128)S(1)} %get-tuple-element.20), channel_id=1, source_target_pairs={{0,32},{16,48},{32,0},{48,16},{64,96},{80,112},{96,64},{112,80},{1... | collective-permute-start | bytes 245768 | tf_op jit(solution)/shard_map/ppermute | solution.py:261
  75.9 2.5 %collective-permute-start.20 = (f32[32,640]{1,0:T(8,128)S(1)}, f32[32,640]{1,0:T(8,128)S(1)}, u32[]{:S(2)}, u32[]{:S(2)}) collective-permute-start(f32[32,640]{1,0:T(8,128)S(1)} %get-tuple-element.20), channel_id=1, source_target_pairs={{0,16},{16,0},{32,48},{48,32},{64,80},{80,64},{96,112},{112,96},{1... | collective-permute-start | bytes 245768 | tf_op jit(solution)/shard_map/ppermute | solution.py:261
  78.4 5.9 %collective-permute-start.29 = (f32[32,640]{1,0:T(8,128)S(1)}, f32[32,640]{1,0:T(8,128)S(1)}, u32[]{:S(2)}, u32[]{:S(2)}) collective-permute-start(f32[32,640]{1,0:T(8,128)S(1)} %add_add_fusion.s0_ref), channel_id=1, source_target_pairs={{0,64},{16,80},{32,96},{48,112},{64,0},{80,16},{96,32},{112,48},{1... | collective-permute-start | bytes 245768 | tf_op jit(solution)/shard_map/ppermute | solution.py:263
  84.4 1.3 %collective-permute-start.30 = (f32[32,640]{1,0:T(8,128)S(1)}, f32[32,640]{1,0:T(8,128)S(1)}, u32[]{:S(2)}, u32[]{:S(2)}) collective-permute-start(f32[32,640]{1,0:T(8,128)S(1)} %add_add_fusion.s0_ref), channel_id=1, source_target_pairs={{0,128},{16,144},{32,160},{48,176},{64,192},{80,208},{96,224},{112... | collective-permute-start | bytes 245768 | tf_op jit(solution)/shard_map/ppermute | solution.py:263
  86.4 5.5 %collective-permute-start.23 = (f32[32,640]{1,0:T(8,128)S(1)}, f32[32,640]{1,0:T(8,128)S(1)}, u32[]{:S(2)}, u32[]{:S(2)}) collective-permute-start(f32[32,640]{1,0:T(8,128)S(1)} %add_add_fusion.1.s0_ref), channel_id=1, source_target_pairs={{0,64},{16,80},{32,96},{48,112},{64,0},{80,16},{96,32},{112,48},{1... | collective-permute-start | bytes 245768 | tf_op jit(solution)/shard_map/ppermute | solution.py:263
  91.9 1.3 %collective-permute-start.24 = (f32[32,640]{1,0:T(8,128)S(1)}, f32[32,640]{1,0:T(8,128)S(1)}, u32[]{:S(2)}, u32[]{:S(2)}) collective-permute-start(f32[32,640]{1,0:T(8,128)S(1)} %add_add_fusion.1.s0_ref), channel_id=1, source_target_pairs={{0,128},{16,144},{32,160},{48,176},{64,192},{80,208},{96,224},{112... | collective-permute-start | bytes 245768 | tf_op jit(solution)/shard_map/ppermute | solution.py:263
  93.1 2.0 %collective-permute-start.25 = (f32[32,640]{1,0:T(8,128)S(1)}, f32[32,640]{1,0:T(8,128)S(1)}, u32[]{:S(2)}, u32[]{:S(2)}) collective-permute-start(f32[32,640]{1,0:T(8,128)S(1)} %add_add_fusion.1.s0_ref), channel_id=1, source_target_pairs={{0,192},{16,208},{32,224},{48,240},{64,128},{80,144},{96,160},{112... | collective-permute-start | bytes 245768 | tf_op jit(solution)/shard_map/ppermute | solution.py:263
  97.0 6.2 %collective-permute-done.25.s3_ref = f32[32,640]{1,0:T(8,128)S(1)} collective-permute-done((f32[32,640]{1,0:T(8,128)S(1)}, f32[32,640]{1,0:T(8,128)S(1)}, u32[]{:S(2)}, u32[]{:S(2)}) %collective-permute-start.25) | collective-permute-done | bytes 81952 | tf_op jit(solution)/shard_map/ppermute | solution.py:263
  (100 shorter events, 18.5 us)
Async XLA Ops:
  4.8 5.0 %collective-permute-start.10 = (f32[8,2,8,5120]{3,2,1,0:T(8,128)S(1)}, f32[8,2,8,5120]{3,2,1,0:T(8,128)S(1)}, u32[]{:S(2)}, u32[]{:S(2)}) collective-permute-start(f32[8,2,8,5120]{3,2,1,0:T(8,128)S(1)} %get-tuple-element.17), channel_id=1, source_target_pairs={{0,1},{1,0},{2,3},{3,2},{4,5},{5,4},{6,7},{7,6},{8,9},{9,8},{10,11... | collective-permute-start | bytes 7864328 | tf_op jit(solution)/shard_map/ppermute | solution.py:251
  6.4 11.0 %collective-permute-start = (f32[8,2,8,5120]{3,2,1,0:T(8,128)S(1)}, f32[8,2,8,5120]{3,2,1,0:T(8,128)S(1)}, u32[]{:S(2)}, u32[]{:S(2)}) collective-permute-start(f32[8,2,8,5120]{3,2,1,0:T(8,128)S(1)} %get-tuple-element.13), channel_id=1, source_target_pairs={{0,1},{1,0},{2,3},{3,2},{4,5},{5,4},{6,7},{7,6},{8,9},{9,8},{10,11... | collective-permute-start | bytes 7864328 | tf_op jit(solution)/shard_map/ppermute | solution.py:251
  10.0 33.4 %collective-permute-start.11 = (f32[2,2,2,8,1792]{4,3,2,0,1:T(8,128)S(1)}, f32[2,2,2,8,1792]{4,3,2,0,1:T(8,128)S(1)}, u32[]{:S(2)}, u32[]{:S(2)}) collective-permute-start(f32[2,2,2,8,1792]{4,3,2,0,1:T(8,128)S(1)} %bitcast.143), channel_id=1, source_target_pairs={{0,2},{1,3},{2,0},{3,1},{4,6},{5,7},{6,4},{7,5},{8,10},{9,11},{10,... | collective-permute-start | bytes 1376264 | tf_op jit(solution)/shard_map/ppermute | solution.py:224
  11.8 14.0 %collective-permute-start.13 = (f32[2,2,2,8,1664]{4,3,2,1,0:T(8,128)S(1)}, f32[2,2,2,8,1664]{4,3,2,1,0:T(8,128)S(1)}, u32[]{:S(2)}, u32[]{:S(2)}) collective-permute-start(f32[2,2,2,8,1664]{4,3,2,1,0:T(8,128)S(1)} %slice_bitcast_fusion), channel_id=1, source_target_pairs={{0,6},{1,7},{2,4},{3,5},{4,2},{5,3},{6,0},{7,1},{8,14},{9,15},{10,... | collective-permute-start | bytes 1277960 | tf_op jit(solution)/shard_map/ppermute | solution.py:224
  14.0 15.0 %collective-permute-start.15 = (f32[2,2,2,8,1664]{4,3,2,1,0:T(8,128)S(1)}, f32[2,2,2,8,1664]{4,3,2,1,0:T(8,128)S(1)}, u32[]{:S(2)}, u32[]{:S(2)}) collective-permute-start(f32[2,2,2,8,1664]{4,3,2,1,0:T(8,128)S(1)} %bitcast.145), channel_id=1, source_target_pairs={{0,8},{1,9},{2,10},{3,11},{4,12},{5,13},{6,14},{7,15},{8,0},{9,1},... | collective-permute-start | bytes 1277960 | tf_op jit(solution)/shard_map/ppermute | solution.py:224
  17.5 26.0 %collective-permute-start.1 = (f32[2,2,2,8,1792]{4,3,2,0,1:T(8,128)S(1)}, f32[2,2,2,8,1792]{4,3,2,0,1:T(8,128)S(1)}, u32[]{:S(2)}, u32[]{:S(2)}) collective-permute-start(f32[2,2,2,8,1792]{4,3,2,0,1:T(8,128)S(1)} %bitcast.144), channel_id=1, source_target_pairs={{0,2},{1,3},{2,0},{3,1},{4,6},{5,7},{6,4},{7,5},{8,10},{9,11},{10,... | collective-permute-start | bytes 1376264 | tf_op jit(solution)/shard_map/ppermute | solution.py:224
  18.5 15.3 %collective-permute-start.3 = (f32[2,2,2,8,1664]{4,3,2,1,0:T(8,128)S(1)}, f32[2,2,2,8,1664]{4,3,2,1,0:T(8,128)S(1)}, u32[]{:S(2)}, u32[]{:S(2)}) collective-permute-start(f32[2,2,2,8,1664]{4,3,2,1,0:T(8,128)S(1)} %slice_bitcast_fusion.2), channel_id=1, source_target_pairs={{0,6},{1,7},{2,4},{3,5},{4,2},{5,3},{6,0},{7,1},{8,14},{9,15},{10,... | collective-permute-start | bytes 1277960 | tf_op jit(solution)/shard_map/ppermute | solution.py:224
  25.8 14.3 %collective-permute-start.5 = (f32[2,2,2,8,1664]{4,3,2,1,0:T(8,128)S(1)}, f32[2,2,2,8,1664]{4,3,2,1,0:T(8,128)S(1)}, u32[]{:S(2)}, u32[]{:S(2)}) collective-permute-start(f32[2,2,2,8,1664]{4,3,2,1,0:T(8,128)S(1)} %bitcast.146), channel_id=1, source_target_pairs={{0,8},{1,9},{2,10},{3,11},{4,12},{5,13},{6,14},{7,15},{8,0},{9,1},... | collective-permute-start | bytes 1277960 | tf_op jit(solution)/shard_map/ppermute | solution.py:224
  29.1 16.8 %collective-permute-start.14 = (f32[2,2,8,1664]{3,2,1,0:T(8,128)S(1)}, f32[2,2,8,1664]{3,2,1,0:T(8,128)S(1)}, u32[]{:S(2)}, u32[]{:S(2)}) collective-permute-start(f32[2,2,8,1664]{3,2,1,0:T(8,128)S(1)} %slice_bitcast_fusion.10), channel_id=1, source_target_pairs={{0,8},{1,9},{2,10},{3,11},{4,12},{5,13},{6,14},{7,15},{8,0},{9,1},... | collective-permute-start | bytes 638984 | tf_op jit(solution)/shard_map/ppermute | solution.py:224
  33.8 13.3 %collective-permute-start.16 = (f32[2,2,8,1664]{3,2,1,0:T(8,128)S(1)}, f32[2,2,8,1664]{3,2,1,0:T(8,128)S(1)}, u32[]{:S(2)}, u32[]{:S(2)}) collective-permute-start(f32[2,2,8,1664]{3,2,1,0:T(8,128)S(1)} %slice_bitcast_fusion.8), channel_id=1, source_target_pairs={{0,2},{1,3},{2,0},{3,1},{4,6},{5,7},{6,4},{7,5},{8,10},{9,11},{10,... | collective-permute-start | bytes 638984 | tf_op jit(solution)/shard_map/ppermute | solution.py:224
  40.1 8.6 %collective-permute-start.4 = (f32[2,2,8,1664]{3,2,1,0:T(8,128)S(1)}, f32[2,2,8,1664]{3,2,1,0:T(8,128)S(1)}, u32[]{:S(2)}, u32[]{:S(2)}) collective-permute-start(f32[2,2,8,1664]{3,2,1,0:T(8,128)S(1)} %slice_bitcast_fusion.14), channel_id=1, source_target_pairs={{0,8},{1,9},{2,10},{3,11},{4,12},{5,13},{6,14},{7,15},{8,0},{9,1},... | collective-permute-start | bytes 638984 | tf_op jit(solution)/shard_map/ppermute | solution.py:224
  43.3 8.1 %collective-permute-start.6 = (f32[2,2,8,1664]{3,2,1,0:T(8,128)S(1)}, f32[2,2,8,1664]{3,2,1,0:T(8,128)S(1)}, u32[]{:S(2)}, u32[]{:S(2)}) collective-permute-start(f32[2,2,8,1664]{3,2,1,0:T(8,128)S(1)} %slice_bitcast_fusion.12), channel_id=1, source_target_pairs={{0,2},{1,3},{2,0},{3,1},{4,6},{5,7},{6,4},{7,5},{8,10},{9,11},{10,... | collective-permute-start | bytes 638984 | tf_op jit(solution)/shard_map/ppermute | solution.py:224
  43.6 9.2 %collective-permute-start.12 = (f32[2,2,8,1792]{3,2,1,0:T(8,128)S(1)}, f32[2,2,8,1792]{3,2,1,0:T(8,128)S(1)}, u32[]{:S(2)}, u32[]{:S(2)}) collective-permute-start(f32[2,2,8,1792]{3,2,1,0:T(8,128)S(1)} %slice_bitcast_fusion.4), channel_id=1, source_target_pairs={{0,6},{1,7},{2,4},{3,5},{4,2},{5,3},{6,0},{7,1},{8,14},{9,15},{10,... | collective-permute-start | bytes 688136 | tf_op jit(solution)/shard_map/ppermute | solution.py:224
  45.8 9.0 %collective-permute-start.2 = (f32[2,2,8,1792]{3,2,1,0:T(8,128)S(1)}, f32[2,2,8,1792]{3,2,1,0:T(8,128)S(1)}, u32[]{:S(2)}, u32[]{:S(2)}) collective-permute-start(f32[2,2,8,1792]{3,2,1,0:T(8,128)S(1)} %slice_bitcast_fusion.6), channel_id=1, source_target_pairs={{0,6},{1,7},{2,4},{3,5},{4,2},{5,3},{6,0},{7,1},{8,14},{9,15},{10,... | collective-permute-start | bytes 688136 | tf_op jit(solution)/shard_map/ppermute | solution.py:224
  47.8 9.5 %collective-permute-start.18 = (f32[2,8,1664]{2,1,0:T(8,128)S(1)}, f32[2,8,1664]{2,1,0:T(8,128)S(1)}, u32[]{:S(2)}, u32[]{:S(2)}) collective-permute-start(f32[2,8,1664]{2,1,0:T(8,128)S(1)} %get-tuple-element.46), channel_id=1, source_target_pairs={{0,2},{1,3},{2,0},{3,1},{4,6},{5,7},{6,4},{7,5},{8,10},{9,11},{10,... | collective-permute-start | bytes 319496 | tf_op jit(solution)/shard_map/ppermute | solution.py:224
  48.6 12.3 %collective-permute-start.19 = (f32[2,8,1664]{2,1,0:T(8,128)}, f32[2,8,1664]{2,1,0:T(8,128)S(1)}, u32[]{:S(2)}, u32[]{:S(2)}) collective-permute-start(f32[2,8,1664]{2,1,0:T(8,128)} %get-tuple-element.44), channel_id=1, source_target_pairs={{0,6},{1,7},{2,4},{3,5},{4,2},{5,3},{6,0},{7,1},{8,14},{9,15},{10,... | collective-permute-start | bytes 319496 | tf_op jit(solution)/shard_map/ppermute | solution.py:224
  51.4 14.6 %collective-permute-start.8 = (f32[2,8,1664]{2,1,0:T(8,128)}, f32[2,8,1664]{2,1,0:T(8,128)S(1)}, u32[]{:S(2)}, u32[]{:S(2)}) collective-permute-start(f32[2,8,1664]{2,1,0:T(8,128)} %get-tuple-element.42), channel_id=1, source_target_pairs={{0,2},{1,3},{2,0},{3,1},{4,6},{5,7},{6,4},{7,5},{8,10},{9,11},{10,... | collective-permute-start | bytes 319496 | tf_op jit(solution)/shard_map/ppermute | solution.py:224
  52.7 18.8 %collective-permute-start.9 = (f32[2,8,1664]{2,1,0:T(8,128)}, f32[2,8,1664]{2,1,0:T(8,128)S(1)}, u32[]{:S(2)}, u32[]{:S(2)}) collective-permute-start(f32[2,8,1664]{2,1,0:T(8,128)} %get-tuple-element.40), channel_id=1, source_target_pairs={{0,6},{1,7},{2,4},{3,5},{4,2},{5,3},{6,0},{7,1},{8,14},{9,15},{10,... | collective-permute-start | bytes 319496 | tf_op jit(solution)/shard_map/ppermute | solution.py:224
  54.8 6.6 %collective-permute-start.17 = (f32[2,8,1792]{2,1,0:T(8,128)}, f32[2,8,1792]{2,1,0:T(8,128)S(1)}, u32[]{:S(2)}, u32[]{:S(2)}) collective-permute-start(f32[2,8,1792]{2,1,0:T(8,128)} %get-tuple-element.38), channel_id=1, source_target_pairs={{0,8},{1,9},{2,10},{3,11},{4,12},{5,13},{6,14},{7,15},{8,0},{9,1},... | collective-permute-start | bytes 344072 | tf_op jit(solution)/shard_map/ppermute | solution.py:224
  57.3 14.3 %collective-permute-start.7 = (f32[2,8,1792]{2,1,0:T(8,128)}, f32[2,8,1792]{2,1,0:T(8,128)S(1)}, u32[]{:S(2)}, u32[]{:S(2)}) collective-permute-start(f32[2,8,1792]{2,1,0:T(8,128)} %get-tuple-element.36), channel_id=1, source_target_pairs={{0,8},{1,9},{2,10},{3,11},{4,12},{5,13},{6,14},{7,15},{8,0},{9,1},... | collective-permute-start | bytes 344072 | tf_op jit(solution)/shard_map/ppermute | solution.py:224
  62.7 13.2 %collective-permute-start.27 = (f32[32,640]{1,0:T(8,128)S(1)}, f32[32,640]{1,0:T(8,128)S(1)}, u32[]{:S(2)}, u32[]{:S(2)}) collective-permute-start(f32[32,640]{1,0:T(8,128)S(1)} %get-tuple-element.21), channel_id=1, source_target_pairs={{0,32},{16,48},{32,0},{48,16},{64,96},{80,112},{96,64},{112,80},{1... | collective-permute-start | bytes 245768 | tf_op jit(solution)/shard_map/ppermute | solution.py:261
  66.0 12.4 %collective-permute-start.28 = (f32[32,640]{1,0:T(8,128)S(1)}, f32[32,640]{1,0:T(8,128)S(1)}, u32[]{:S(2)}, u32[]{:S(2)}) collective-permute-start(f32[32,640]{1,0:T(8,128)S(1)} %get-tuple-element.21), channel_id=1, source_target_pairs={{0,48},{16,32},{32,16},{48,0},{64,112},{80,96},{96,80},{112,64},{1... | collective-permute-start | bytes 245768 | tf_op jit(solution)/shard_map/ppermute | solution.py:261
  66.0 12.4 %collective-permute-start.26 = (f32[32,640]{1,0:T(8,128)S(1)}, f32[32,640]{1,0:T(8,128)S(1)}, u32[]{:S(2)}, u32[]{:S(2)}) collective-permute-start(f32[32,640]{1,0:T(8,128)S(1)} %get-tuple-element.21), channel_id=1, source_target_pairs={{0,16},{16,0},{32,48},{48,32},{64,80},{80,64},{96,112},{112,96},{1... | collective-permute-start | bytes 245768 | tf_op jit(solution)/shard_map/ppermute | solution.py:261
  72.9 12.7 %collective-permute-start.21 = (f32[32,640]{1,0:T(8,128)S(1)}, f32[32,640]{1,0:T(8,128)S(1)}, u32[]{:S(2)}, u32[]{:S(2)}) collective-permute-start(f32[32,640]{1,0:T(8,128)S(1)} %get-tuple-element.20), channel_id=1, source_target_pairs={{0,32},{16,48},{32,0},{48,16},{64,96},{80,112},{96,64},{112,80},{1... | collective-permute-start | bytes 245768 | tf_op jit(solution)/shard_map/ppermute | solution.py:261
  74.9 11.4 %collective-permute-start.22 = (f32[32,640]{1,0:T(8,128)S(1)}, f32[32,640]{1,0:T(8,128)S(1)}, u32[]{:S(2)}, u32[]{:S(2)}) collective-permute-start(f32[32,640]{1,0:T(8,128)S(1)} %get-tuple-element.20), channel_id=1, source_target_pairs={{0,48},{16,32},{32,16},{48,0},{64,112},{80,96},{96,80},{112,64},{1... | collective-permute-start | bytes 245768 | tf_op jit(solution)/shard_map/ppermute | solution.py:261
  75.9 10.5 %collective-permute-start.20 = (f32[32,640]{1,0:T(8,128)S(1)}, f32[32,640]{1,0:T(8,128)S(1)}, u32[]{:S(2)}, u32[]{:S(2)}) collective-permute-start(f32[32,640]{1,0:T(8,128)S(1)} %get-tuple-element.20), channel_id=1, source_target_pairs={{0,16},{16,0},{32,48},{48,32},{64,80},{80,64},{96,112},{112,96},{1... | collective-permute-start | bytes 245768 | tf_op jit(solution)/shard_map/ppermute | solution.py:261
  78.4 14.7 %collective-permute-start.29 = (f32[32,640]{1,0:T(8,128)S(1)}, f32[32,640]{1,0:T(8,128)S(1)}, u32[]{:S(2)}, u32[]{:S(2)}) collective-permute-start(f32[32,640]{1,0:T(8,128)S(1)} %add_add_fusion.s0_ref), channel_id=1, source_target_pairs={{0,64},{16,80},{32,96},{48,112},{64,0},{80,16},{96,32},{112,48},{1... | collective-permute-start | bytes 245768 | tf_op jit(solution)/shard_map/ppermute | solution.py:263
  84.4 11.7 %collective-permute-start.30 = (f32[32,640]{1,0:T(8,128)S(1)}, f32[32,640]{1,0:T(8,128)S(1)}, u32[]{:S(2)}, u32[]{:S(2)}) collective-permute-start(f32[32,640]{1,0:T(8,128)S(1)} %add_add_fusion.s0_ref), channel_id=1, source_target_pairs={{0,128},{16,144},{32,160},{48,176},{64,192},{80,208},{96,224},{112... | collective-permute-start | bytes 245768 | tf_op jit(solution)/shard_map/ppermute | solution.py:263
  85.6 10.4 %collective-permute-start.31 = (f32[32,640]{1,0:T(8,128)S(1)}, f32[32,640]{1,0:T(8,128)S(1)}, u32[]{:S(2)}, u32[]{:S(2)}) collective-permute-start(f32[32,640]{1,0:T(8,128)S(1)} %add_add_fusion.s0_ref), channel_id=1, source_target_pairs={{0,192},{16,208},{32,224},{48,240},{64,128},{80,144},{96,160},{112... | collective-permute-start | bytes 245768 | tf_op jit(solution)/shard_map/ppermute | solution.py:263
  86.4 10.6 %collective-permute-start.23 = (f32[32,640]{1,0:T(8,128)S(1)}, f32[32,640]{1,0:T(8,128)S(1)}, u32[]{:S(2)}, u32[]{:S(2)}) collective-permute-start(f32[32,640]{1,0:T(8,128)S(1)} %add_add_fusion.1.s0_ref), channel_id=1, source_target_pairs={{0,64},{16,80},{32,96},{48,112},{64,0},{80,16},{96,32},{112,48},{1... | collective-permute-start | bytes 245768 | tf_op jit(solution)/shard_map/ppermute | solution.py:263
  91.9 5.1 %collective-permute-start.24 = (f32[32,640]{1,0:T(8,128)S(1)}, f32[32,640]{1,0:T(8,128)S(1)}, u32[]{:S(2)}, u32[]{:S(2)}) collective-permute-start(f32[32,640]{1,0:T(8,128)S(1)} %add_add_fusion.1.s0_ref), channel_id=1, source_target_pairs={{0,128},{16,144},{32,160},{48,176},{64,192},{80,208},{96,224},{112... | collective-permute-start | bytes 245768 | tf_op jit(solution)/shard_map/ppermute | solution.py:263
  93.1 10.0 %collective-permute-start.25 = (f32[32,640]{1,0:T(8,128)S(1)}, f32[32,640]{1,0:T(8,128)S(1)}, u32[]{:S(2)}, u32[]{:S(2)}) collective-permute-start(f32[32,640]{1,0:T(8,128)S(1)} %add_add_fusion.1.s0_ref), channel_id=1, source_target_pairs={{0,192},{16,208},{32,224},{48,240},{64,128},{80,144},{96,160},{112... | collective-permute-start | bytes 245768 | tf_op jit(solution)/shard_map/ppermute | solution.py:263
  (5 other events, 52.2 us)

commit v2 on v1

--- a/solution.py
+++ b/solution.py
@@ -9,6 +9,7 @@
 SPAN = 64
 BAND = 16
 LANES = 128
+VMEM_LIMIT = 12 * 2**20
 EXACT = lax.Precision.HIGHEST
 CHUNKS = ((0, 2), (2, 2))
 ORDERS = ((1, 2, 0), (2, 0, 1), (0, 1, 2))
@@ -52,30 +53,38 @@
 
 def split_cores(grads, chips, core, first, count):
     width = grads.shape[2]
-
-    def kernel(chips_ref, core_ref, grads_ref, other_ref, own_ref):
-        both = grads_ref[...].astype(jnp.float32)
-        low, high = both[:, :8], both[:, 8:]
+    chip_count = 8
+
+    def kernel(chips_ref, core_ref, grads_ref, other_ref, own_ref, held, sems):
+        def fetch(i):
+            start = pl.multiple_of(chips_ref[i] * 16, 16)
+            return pltpu.make_async_copy(
+                grads_ref.at[pl.ds(first, count), pl.ds(start, 16)], held.at[i], sems.at[i]
+            )
+
+        for i in range(chip_count):
+            fetch(i).start()
         is_low = core_ref[0] == 0
-        own_ref[0] = jnp.where(is_low, low, high)
-        other_ref[0] = jnp.where(is_low, high, low)
-
-    out = jax.ShapeDtypeStruct((8, count, 8, width), jnp.float32)
-    spec = pl.BlockSpec((1, count, 8, width), lambda i, chips, core: (i, 0, 0, 0))
-    return pl.pallas_call(
-        kernel,
-        grid_spec=pltpu.PrefetchScalarGridSpec(
-            num_scalar_prefetch=2,
-            grid=(8,),
-            in_specs=[
-                pl.BlockSpec(
-                    (count, 16, width), lambda i, chips, core: (first // count, chips[i], 0)
-                )
-            ],
-            out_specs=[spec, spec],
+        for i in range(chip_count):
+            fetch(i).wait()
+            for layer in range(count):
+                both = held[i, layer].astype(jnp.float32)
+                own_ref[i, layer] = jnp.where(is_low, both[:8], both[8:])
+                other_ref[i, layer] = jnp.where(is_low, both[8:], both[:8])
+
+    out = jax.ShapeDtypeStruct((chip_count, count, 8, width), jnp.float32)
+    smem = pl.BlockSpec(memory_space=pltpu.SMEM)
+    return pl.pallas_call(
+        kernel,
+        in_specs=[smem, smem, pl.BlockSpec(memory_space=pltpu.HBM)],
+        out_shape=[out, out],
+        scratch_shapes=[
+            pltpu.VMEM((chip_count, count, 16, width), grads.dtype),
+            pltpu.SemaphoreType.DMA((chip_count,)),
+        ],
+        compiler_params=pltpu.CompilerParams(
+            vmem_limit_bytes=chip_count * count * width * 8 * 12 + 2**20
         ),
-        out_shape=[out, out],
-        compiler_params=pltpu.CompilerParams(vmem_limit_bytes=24 * 2**20),
         name="split_cores",
     )(chips, core, grads)
 
@@ -141,7 +150,7 @@
     return pl.pallas_call(
         kernel,
         out_shape=shapes,
-        compiler_params=pltpu.CompilerParams(vmem_limit_bytes=24 * 2**20),
+        compiler_params=pltpu.CompilerParams(vmem_limit_bytes=VMEM_LIMIT),
         name="forward_dct",
     )(*keeps, *recvs, momentum, band, table)
 
@@ -156,29 +165,37 @@
     )
 
 
-def residual(pre, dense, table):
-    rows, width = pre.shape
-
-    def kernel(pre_ref, dense_ref, table_ref, out_ref):
-        blocks = inverse(dense_ref[...], table_ref[...])
-        for t in range(width // LANES):
-            lanes = slice(t * LANES, (t + 1) * LANES)
-            out_ref[:, lanes] = pre_ref[:, lanes] - blocks[t * rows : (t + 1) * rows]
-
-    return pl.pallas_call(
-        kernel,
-        out_shape=jax.ShapeDtypeStruct((rows, width), jnp.float32),
-        compiler_params=pltpu.CompilerParams(vmem_limit_bytes=24 * 2**20),
+def residual(pres, denses, table, layers, width):
+    parts = len(CHUNKS)
+
+    def kernel(*refs):
+        pre_refs, dense_refs = refs[:parts], refs[parts : 2 * parts]
+        table_ref, out_ref = refs[2 * parts :]
+        for (first, count), pre_ref, dense_ref in zip(CHUNKS, pre_refs, dense_refs):
+            rows = 8 * count
+            blocks = inverse(dense_ref[...], table_ref[...])
+            for t in range(width // LANES):
+                lanes = slice(t * LANES, (t + 1) * LANES)
+                new = pre_ref[:, lanes] - blocks[t * rows : (t + 1) * rows]
+                out_ref[first : first + count, :, lanes] = new.reshape(count, 8, LANES)
+
+    return pl.pallas_call(
+        kernel,
+        out_shape=jax.ShapeDtypeStruct((layers, 8, width), jnp.float32),
+        compiler_params=pltpu.CompilerParams(vmem_limit_bytes=VMEM_LIMIT),
         name="residual",
-    )(pre, dense, table)
-
-
-def step_params(params, sums, band, table, replicas, first, count):
+    )(*pres, *denses, table)
+
+
+def step_params(params, sums, band, table, before, replicas, first, count):
+    width = params.shape[2]
     rows = 8 * count
-    width = params.shape[2]
     blocks = band.shape[1]
 
-    def kernel(params_ref, s0_ref, s1_ref, s2_ref, s3_ref, band_ref, table_ref, out_ref, dense):
+    def kernel(params_ref, s0_ref, s1_ref, s2_ref, s3_ref, band_ref, table_ref, *rest):
+        out_ref, dense = rest[-2:]
+        if before is not None:
+            out_ref[:first] = rest[0][...]
         index = lax.broadcasted_iota(jnp.int32, (SPAN, LANES), 0)
         for tile in range(blocks // LANES):
             lanes = slice(tile * LANES, (tile + 1) * LANES)
@@ -196,76 +213,113 @@
             lanes = slice(t * LANES, (t + 1) * LANES)
             old = params_ref[first : first + count, :, lanes].reshape(rows, LANES)
             new = old - 0.5 * update[t * rows : (t + 1) * rows]
-            out_ref[:, :, lanes] = new.reshape(count, 8, LANES)
-
-    return pl.pallas_call(
-        kernel,
-        out_shape=jax.ShapeDtypeStruct((count, 8, width), jnp.float32),
+            out_ref[first : first + count, :, lanes] = new.reshape(count, 8, LANES)
+
+    extra = [] if before is None else [before]
+    return pl.pallas_call(
+        kernel,
+        out_shape=jax.ShapeDtypeStruct((first + count, 8, width), jnp.float32),
         scratch_shapes=[pltpu.VMEM((LANES, blocks), jnp.float32)],
-        compiler_params=pltpu.CompilerParams(vmem_limit_bytes=24 * 2**20),
+        compiler_params=pltpu.CompilerParams(vmem_limit_bytes=VMEM_LIMIT),
         name="step_params",
-    )(params, *sums, band, table)
-
-
-def band_rows(band, first, count):
-    part = band[first : first + count].reshape(count, 8, -1, 2, BAND)
-    part = part.transpose(3, 4, 2, 0, 1).reshape(2 * BAND, -1)
-    total = part.shape[1]
-    return jnp.pad(part, ((0, 0), (0, padded(total) - total)), constant_values=SPAN)
-
-
-def halve(piece, order):
-    left = [0, 1, 2]
-    for step, dim in enumerate(order):
-        axis = left.index(dim)
-        left.remove(dim)
-        keep = lax.index_in_dim(piece, 0, axis, keepdims=False)
+    )(params, *sums, band, table, *extra)
+
+
+def band_rows(band):
+    layers, _, _, spans = band.shape
+    tiles = spans // 2
+
+    def kernel(band_ref, *outs):
+        for (first, count), out_ref in zip(CHUNKS, outs):
+            rows = 8 * count
+            blocks = out_ref.shape[1]
+            index = band_ref[first : first + count].reshape(rows * BAND, spans)
+            index = index.astype(jnp.float32).astype(jnp.bfloat16)
+            lane = lax.broadcasted_iota(jnp.int32, (spans, blocks), 1)
+            chunk = lax.broadcasted_iota(jnp.int32, (spans, blocks), 0)
+            row_of = lax.broadcasted_iota(jnp.int32, (BAND, blocks), 1) % rows
+            for h in range(2):
+                place = (chunk == 2 * (lane // rows) + h).astype(jnp.float32).astype(jnp.bfloat16)
+                spread = jnp.dot(index, place, preferred_element_type=jnp.float32)
+                found = jnp.zeros((BAND, blocks), jnp.float32)
+                for r in range(rows):
+                    found = jnp.where(row_of == r, spread[r * BAND : (r + 1) * BAND], found)
+                out_ref[h * BAND : (h + 1) * BAND] = found.astype(jnp.int32)
+
+    return pl.pallas_call(
+        kernel,
+        out_shape=[
+            jax.ShapeDtypeStruct((2 * BAND, padded(8 * count * tiles)), jnp.int32)
+            for _, count in CHUNKS
+        ],
+        compiler_params=pltpu.CompilerParams(vmem_limit_bytes=VMEM_LIMIT),
+        name="band_rows",
+    )(band)
+
+
+def halve(pieces, step):
+    keeps, recvs = [], []
+    for piece, order in zip(pieces, ORDERS):
+        dim = order[step]
+        axis = sorted(order[step:]).index(dim)
+        keeps.append(lax.index_in_dim(piece, 0, axis, keepdims=False))
         send = lax.index_in_dim(piece, 1, axis, keepdims=False)
-        recv = lax.ppermute(send, "fsdp", HALVES[dim])
-        if step == 2:
-            return keep, recv
-        piece = keep + recv
+        recvs.append(lax.ppermute(send, "fsdp", HALVES[dim]))
+    return keeps, list(lax.optimization_barrier(tuple(recvs)))
+
+
+def ring_pairs(even, odd):
+    return [
+        (y * 8 + z, y * 8 + (z + (odd if z % 2 else even)) % 8) for y in range(2) for z in range(8)
+    ]
+
+
+OPPOSITE, BESIDE, BEYOND = ring_pairs(-3, 3), ring_pairs(-1, 1), ring_pairs(-2, 2)
 
 
 def shards(grads, momentum, params, band):
     table = table128()
     grads = grads[0, 0]
     moment = momentum[0]
-    width = grads.shape[2]
+    layers, _, width = params.shape
     replicas = lax.axis_size("rep")
     me = lax.axis_index("fsdp").astype(jnp.int32)
     core = (me % 2).reshape(1)
     x, y = (me // 2) % 4, me // 8
     chips = jnp.stack(
-        [
-            (y ^ dy) * 4 + column
-            for dy in range(2)
-            for column in (x, 3 - x, x ^ 1, x ^ 2)
-        ]
+        [(y ^ dy) * 4 + column for dy in range(2) for column in (x, 3 - x, x ^ 1, x ^ 2)]
     )
     tiles = width // LANES
     cuts = [0, (tiles + 2) // 3 * LANES, ((tiles + 2) // 3 + (tiles + 1) // 3) * LANES, width]
-    kept, updated = [], []
+    bands = band_rows(band.transpose(0, 1, 3, 2))
+    source = pltpu.with_memory_space_constraint(grads, pltpu.HBM)
+    pieces = []
     for first, count in CHUNKS:
-        other, own = split_cores(grads, chips, core, first, count)
+        other, own = split_cores(source, chips, core, first, count)
         got = lax.ppermute(other, "fsdp", CORE)
-        bands = band_rows(band, first, count)
-        keeps, recvs = [], []
-        for third, order in enumerate(ORDERS):
-            cols = slice(cuts[third], cuts[third + 1])
-            piece = own[..., cols] + got[..., cols]
-            keep, recv = halve(piece.reshape(2, 2, 2, *piece.shape[1:]), order)
-            keeps.append(keep)
-            recvs.append(recv)
-        values, dense, pre = forward(keeps, recvs, moment, bands, table, first, count)
-        near = [lax.ppermute(values, "rep", rep_pairs(m)) for m in (1, 2, 3)]
+        both = [
+            own[..., low:high] + got[..., low:high] for low, high in zip(cuts[:-1], cuts[1:])
+        ]
+        pieces.append([p.reshape(2, 2, 2, *p.shape[1:]) for p in both])
+    for step in range(3):
+        halved = [halve(p, step) for p in pieces]
+        if step < 2:
+            pieces = [[k + r for k, r in zip(*h)] for h in halved]
+    forwards = []
+    for (first, count), (keeps, recvs), bands_here in zip(CHUNKS, halved, bands):
+        forwards.append(forward(keeps, recvs, moment, bands_here, table, first, count))
+    updated = None
+    for (first, count), (values, _, _), bands_here in zip(CHUNKS, forwards, bands):
+        near = [lax.ppermute(values, "rep", rep_pairs(m)) for m in (1, 8, 9)]
         four = (values + near[0]) + (near[1] + near[2])
-        far = [lax.ppermute(four, "rep", rep_pairs(m)) for m in (4, 8, 12)]
-        kept.append(residual(pre, dense, table).reshape(count, 8, width))
-        updated.append(
-            step_params(params, [four] + far, bands, table, replicas, first, count)
+        far = [lax.ppermute(four, "rep", p) for p in (OPPOSITE, BESIDE, BEYOND)]
+        updated = step_params(
+            params, [four] + far, bands_here, table, updated, replicas, first, count
         )
-    return jnp.concatenate(kept)[None], jnp.concatenate(updated)
+    kept = residual(
+        [f[2] for f in forwards], [f[1] for f in forwards], table, layers, width
+    )
+    return kept[None], updated
 
 
 def solution(mesh):

time: 105 us -> 86.3 us (0.82)
  local copies, waits for them, and re-layouts: 12.1 us -> 0.66 us
  waiting for transfers between devices: 25.9 us -> 20.2 us
  starting transfers between devices: 54.7 us -> 50.9 us
  Pallas kernels: 8.29 us -> 12 us
  other arithmetic: 2.97 us -> 1.12 us
    ppermute x30, waiting for transfers between devices: 23.1 us -> 18.2 us  [the longest x18 14.6 us: halve(): recvs.append(lax.ppermute(send, 'fsdp', HALVES[dim]))]
    ppermute x30, starting transfers between devices: 54 us -> 50.3 us  [the longest x18 30 us: halve(): recvs.append(lax.ppermute(send, 'fsdp', HALVES[dim]))]
    pallas_call x6, Pallas kernels: 5.75 us -> 9.47 us  [the longest x2 4.69 us: split_cores(): pl.pallas_call(kernel, in_specs=[smem, smem, pl.BlockSpec(memory_space=pl...]
    squeeze x14, local copies, waits for them, and re-layouts: 3.46 us -> 0.25 us  [halve(): send = lax.index_in_dim(piece, 1, axis, keepdims=False)]
    unnamed x12 -> x10, local copies, waits for them, and re-layouts: 2.57 us -> 0.09 us
    slice x7 -> x4, local copies, waits for them, and re-layouts: 2.36 us -> 0.23 us  [halve(): keeps.append(lax.index_in_dim(piece, 0, axis, keepdims=False))]
    reshape x4 -> x0, local copies, waits for them, and re-layouts: 2.08 us -> none  [band_rows(): part = part.transpose(3, 4, 2, 0, 1).reshape(2 * BAND, -1)]
    transpose x2 -> x0, local copies, waits for them, and re-layouts: 1.54 us -> none  [band_rows(): part = part.transpose(3, 4, 2, 0, 1).reshape(2 * BAND, -1)]
  transfers between devices with their start and end apart: 32 -> 32, of which waited for: 6 -> 7; matrix products, arithmetic and copies ran while one was open for 11% -> 2% of each run, Pallas kernels for 6% -> 9%
where the time goes in v2:
time: 86.3 us; the launch traced here: 86 us
  starting transfers between devices  50.9 us (59%)
  waiting for transfers between devices  20.2 us (23%)
  Pallas kernels  12 us (14%)
  other arithmetic  1.12 us (1%)
  between operations  1.09 us (1%)
    ppermute x18, starting transfers between devices, halve(): recvs.append(lax.ppermute(send, 'fsdp', HALVES[dim]))  30 us
    ppermute x18, waiting for transfers between devices, halve(): recvs.append(lax.ppermute(send, 'fsdp', HALVES[dim]))  14.6 us
    ppermute x6, starting transfers between devices, shards(): far = [lax.ppermute(four, 'rep', p) for p in (OPPOSITE, BESIDE, BEYOND)]  13.1 us
    ppermute x6, starting transfers between devices, shards(): near = [lax.ppermute(values, 'rep', rep_pairs(m)) for m in (1, 8, 9)]  7.15 us
    pallas_call x2, Pallas kernels, split_cores(): pl.pallas_call(kernel, in_specs=[smem, smem, pl.BlockSpec(memory_space=pl...  4.69 us
    ppermute x6, waiting for transfers between devices, shards(): far = [lax.ppermute(four, 'rep', p) for p in (OPPOSITE, BESIDE, BEYOND)]  3.55 us
    pallas_call x2, Pallas kernels, step_params(): pl.pallas_call(kernel, out_shape=jax.ShapeDtypeStruct((first + count, 8,...  2.67 us
    pallas_call x2, Pallas kernels, forward(): pl.pallas_call(kernel, out_shape=shapes, compiler_params=pltpu.CompilerPa...  2.54 us
  transfers between devices with their start and end apart: 32, of which 7 were waited for; matrix products, arithmetic and copies ran while one was open for 2% of the time, Pallas kernels for 9%

profile of v2, /device:TPU:32, one launch (start us, length us, event | category | flops | bytes accessed | tf_op | source)
XLA Modules:
  0.0 86.0 jit_solution(8316800908448077459)
XLA Ops:
  0.8 2.3 %split_cores.2 = (f32[8,2,8,5120]{3,2,1,0:T(8,128)S(1)}, f32[8,2,8,5120]{3,2,1,0:T(8,128)S(1)}) custom-call(s32[8]{0:T(128)S(1)} %stack.35.chips_ref, s32[1]{0:T(128)} %bitcast.8.core_ref, bf16[4,128,5120]{2,1,0:T(8,128)(2,1)} %bitcast.118), custom_call_target="tpu_custom_call" | custom-call | tf_op jit(solution)/shard_map/split_cores/pallas_call | solution.py:77
  3.2 2.3 %split_cores.3 = (f32[8,2,8,5120]{3,2,1,0:T(8,128)S(1)}, f32[8,2,8,5120]{3,2,1,0:T(8,128)S(1)}) custom-call(s32[8]{0:T(128)S(1)} %stack.35.chips_ref, s32[1]{0:T(128)} %bitcast.8.core_ref, bf16[4,128,5120]{2,1,0:T(8,128)(2,1)} %bitcast.119), custom_call_target="tpu_custom_call" | custom-call | tf_op jit(solution)/shard_map/split_cores/pallas_call | solution.py:77
  6.1 2.0 %collective-permute-done = f32[8,2,8,5120]{3,2,1,0:T(8,128)S(1)} collective-permute-done((f32[8,2,8,5120]{3,2,1,0:T(8,128)S(1)}, f32[8,2,8,5120]{3,2,1,0:T(8,128)S(1)}, u32[]{:S(2)}, u32[]{:S(2)}) %collective-permute-start) | collective-permute-done | bytes 2621472 | tf_op jit(solution)/shard_map/ppermute | solution.py:299
  8.3 1.6 %collective-permute-start.1 = (f32[2,2,2,8,1792]{4,3,2,0,1:T(8,128)S(1)}, f32[2,2,2,8,1792]{4,3,2,0,1:T(8,128)S(1)}, u32[]{:S(2)}, u32[]{:S(2)}) collective-permute-start(f32[2,2,2,8,1792]{4,3,2,0,1:T(8,128)S(1)} %bitcast.130), channel_id=1, source_target_pairs={{0,2},{1,3},{2,0},{3,1},{4,6},{5,7},{6,4},{7,5},{8,10},{9,11},{10,... | collective-permute-start | bytes 1376264 | tf_op jit(solution)/shard_map/ppermute | solution.py:267
  10.2 2.2 %collective-permute-start.2 = (f32[2,2,2,8,1664]{4,3,2,1,0:T(8,128)S(1)}, f32[2,2,2,8,1664]{4,3,2,1,0:T(8,128)S(1)}, u32[]{:S(2)}, u32[]{:S(2)}) collective-permute-start(f32[2,2,2,8,1664]{4,3,2,1,0:T(8,128)S(1)} %slice_bitcast_fusion.3), channel_id=1, source_target_pairs={{0,6},{1,7},{2,4},{3,5},{4,2},{5,3},{6,0},{7,1},{8,14},{9,15},{10,... | collective-permute-start | bytes 1277960 | tf_op jit(solution)/shard_map/ppermute | solution.py:267
  12.4 3.3 %collective-permute-start.3 = (f32[2,2,2,8,1664]{4,3,2,1,0:T(8,128)S(1)}, f32[2,2,2,8,1664]{4,3,2,1,0:T(8,128)S(1)}, u32[]{:S(2)}, u32[]{:S(2)}) collective-permute-start(f32[2,2,2,8,1664]{4,3,2,1,0:T(8,128)S(1)} %bitcast.132), channel_id=1, source_target_pairs={{0,8},{1,9},{2,10},{3,11},{4,12},{5,13},{6,14},{7,15},{8,0},{9,1},... | collective-permute-start | bytes 1277960 | tf_op jit(solution)/shard_map/ppermute | solution.py:267
  17.6 6.6 %collective-permute-done.2 = f32[2,2,2,8,1664]{4,3,2,1,0:T(8,128)S(1)} collective-permute-done((f32[2,2,2,8,1664]{4,3,2,1,0:T(8,128)S(1)}, f32[2,2,2,8,1664]{4,3,2,1,0:T(8,128)S(1)}, u32[]{:S(2)}, u32[]{:S(2)}) %collective-permute-start.2) | collective-permute-done | bytes 426016 | tf_op jit(solution)/shard_map/ppermute | solution.py:267
  24.2 3.2 %collective-permute-start.13 = (f32[2,2,2,8,1664]{4,3,2,1,0:T(8,128)S(1)}, f32[2,2,2,8,1664]{4,3,2,1,0:T(8,128)S(1)}, u32[]{:S(2)}, u32[]{:S(2)}) collective-permute-start(f32[2,2,2,8,1664]{4,3,2,1,0:T(8,128)S(1)} %bitcast.131), channel_id=1, source_target_pairs={{0,8},{1,9},{2,10},{3,11},{4,12},{5,13},{6,14},{7,15},{8,0},{9,1},... | collective-permute-start | bytes 1277960 | tf_op jit(solution)/shard_map/ppermute | solution.py:267
  27.4 2.2 %collective-permute-start.4 = (f32[2,2,8,1792]{3,2,1,0:T(8,128)S(1)}, f32[2,2,8,1792]{3,2,1,0:T(8,128)S(1)}, u32[]{:S(2)}, u32[]{:S(2)}) collective-permute-start(f32[2,2,8,1792]{3,2,1,0:T(8,128)S(1)} %slice_bitcast_fusion.6), channel_id=1, source_target_pairs={{0,6},{1,7},{2,4},{3,5},{4,2},{5,3},{6,0},{7,1},{8,14},{9,15},{10,... | collective-permute-start | bytes 688136 | tf_op jit(solution)/shard_map/ppermute | solution.py:267
  30.2 3.1 %collective-permute-done.12 = f32[2,2,2,8,1664]{4,3,2,1,0:T(8,128)S(1)} collective-permute-done((f32[2,2,2,8,1664]{4,3,2,1,0:T(8,128)S(1)}, f32[2,2,2,8,1664]{4,3,2,1,0:T(8,128)S(1)}, u32[]{:S(2)}, u32[]{:S(2)}) %collective-permute-start.12) | collective-permute-done | bytes 426016 | tf_op jit(solution)/shard_map/ppermute | solution.py:267
  33.3 4.2 %collective-permute-done.13 = f32[2,2,2,8,1664]{4,3,2,1,0:T(8,128)S(1)} collective-permute-done((f32[2,2,2,8,1664]{4,3,2,1,0:T(8,128)S(1)}, f32[2,2,2,8,1664]{4,3,2,1,0:T(8,128)S(1)}, u32[]{:S(2)}, u32[]{:S(2)}) %collective-permute-start.13) | collective-permute-done | bytes 426016 | tf_op jit(solution)/shard_map/ppermute | solution.py:267
  37.6 2.2 %collective-permute-start.14 = (f32[2,2,8,1792]{3,2,1,0:T(8,128)S(1)}, f32[2,2,8,1792]{3,2,1,0:T(8,128)S(1)}, u32[]{:S(2)}, u32[]{:S(2)}) collective-permute-start(f32[2,2,8,1792]{3,2,1,0:T(8,128)S(1)} %slice_bitcast_fusion.4), channel_id=1, source_target_pairs={{0,6},{1,7},{2,4},{3,5},{4,2},{5,3},{6,0},{7,1},{8,14},{9,15},{10,... | collective-permute-start | bytes 688136 | tf_op jit(solution)/shard_map/ppermute | solution.py:267
  39.9 3.3 %collective-permute-start.15 = (f32[2,2,8,1664]{3,2,1,0:T(8,128)S(1)}, f32[2,2,8,1664]{3,2,1,0:T(8,128)S(1)}, u32[]{:S(2)}, u32[]{:S(2)}) collective-permute-start(f32[2,2,8,1664]{3,2,1,0:T(8,128)S(1)} %slice_bitcast_fusion.11), channel_id=1, source_target_pairs={{0,8},{1,9},{2,10},{3,11},{4,12},{5,13},{6,14},{7,15},{8,0},{9,1},... | collective-permute-start | bytes 638984 | tf_op jit(solution)/shard_map/ppermute | solution.py:267
  43.6 1.0 %collective-permute-start.7 = (f32[2,8,1792]{2,1,0:T(8,128)S(1)}, f32[2,8,1792]{2,1,0:T(8,128)S(1)}, u32[]{:S(2)}, u32[]{:S(2)}) collective-permute-start(f32[2,8,1792]{2,1,0:T(8,128)S(1)} %get-tuple-element.76), channel_id=1, source_target_pairs={{0,8},{1,9},{2,10},{3,11},{4,12},{5,13},{6,14},{7,15},{8,0},{9,1},... | collective-permute-start | bytes 344072 | tf_op jit(solution)/shard_map/ppermute | solution.py:267
  44.6 2.0 %collective-permute-start.8 = (f32[2,8,1664]{2,1,0:T(8,128)S(1)}, f32[2,8,1664]{2,1,0:T(8,128)S(1)}, u32[]{:S(2)}, u32[]{:S(2)}) collective-permute-start(f32[2,8,1664]{2,1,0:T(8,128)S(1)} %get-tuple-element.84), channel_id=1, source_target_pairs={{0,2},{1,3},{2,0},{3,1},{4,6},{5,7},{6,4},{7,5},{8,10},{9,11},{10,... | collective-permute-start | bytes 319496 | tf_op jit(solution)/shard_map/ppermute | solution.py:267
  47.3 2.4 %collective-permute-start.9 = (f32[2,8,1664]{2,1,0:T(8,128)S(1)}, f32[2,8,1664]{2,1,0:T(8,128)S(1)}, u32[]{:S(2)}, u32[]{:S(2)}) collective-permute-start(f32[2,8,1664]{2,1,0:T(8,128)S(1)} %get-tuple-element.82), channel_id=1, source_target_pairs={{0,6},{1,7},{2,4},{3,5},{4,2},{5,3},{6,0},{7,1},{8,14},{9,15},{10,... | collective-permute-start | bytes 319496 | tf_op jit(solution)/shard_map/ppermute | solution.py:267
  49.8 2.1 %collective-permute-start.17 = (f32[2,8,1792]{2,1,0:T(8,128)S(1)}, f32[2,8,1792]{2,1,0:T(8,128)S(1)}, u32[]{:S(2)}, u32[]{:S(2)}) collective-permute-start(f32[2,8,1792]{2,1,0:T(8,128)S(1)} %get-tuple-element.74), channel_id=1, source_target_pairs={{0,8},{1,9},{2,10},{3,11},{4,12},{5,13},{6,14},{7,15},{8,0},{9,1},... | collective-permute-start | bytes 344072 | tf_op jit(solution)/shard_map/ppermute | solution.py:267
  51.9 2.8 %collective-permute-start.19 = (f32[2,8,1664]{2,1,0:T(8,128)S(1)}, f32[2,8,1664]{2,1,0:T(8,128)S(1)}, u32[]{:S(2)}, u32[]{:S(2)}) collective-permute-start(f32[2,8,1664]{2,1,0:T(8,128)S(1)} %get-tuple-element.78), channel_id=1, source_target_pairs={{0,6},{1,7},{2,4},{3,5},{4,2},{5,3},{6,0},{7,1},{8,14},{9,15},{10,... | collective-permute-start | bytes 319496 | tf_op jit(solution)/shard_map/ppermute | solution.py:267
  55.2 1.3 %forward_dct.2 = (f32[32,640]{1,0:T(8,128)S(1)}, f32[128,640]{1,0:T(8,128)S(1)}, f32[16,5120]{1,0:T(8,128)S(1)}) custom-call(f32[2,8,1792]{2,1,0:T(8,128)S(1)} %get-tuple-element.77.refs_0_, f32[2,8,1664]{2,1,0:T(8,128)S(1)} %get-tuple-element.85.refs_1_, f32[2,8,1664]{2,1,0:T(8,128)S(1)} %get-tuple-element.83.refs_2_, ...), custom_call_target="tpu_custom_call" | custom-call | tf_op jit(solution)/shard_map/forward_dct/pallas_call | solution.py:150
  57.3 0.9 %collective-permute-start.28 = (f32[32,640]{1,0:T(8,128)S(1)}, f32[32,640]{1,0:T(8,128)S(1)}, u32[]{:S(2)}, u32[]{:S(2)}) collective-permute-start(f32[32,640]{1,0:T(8,128)S(1)} %get-tuple-element.61), channel_id=1, source_target_pairs={{0,144},{16,128},{32,176},{48,160},{64,208},{80,192},{96,240},{112... | collective-permute-start | bytes 245768 | tf_op jit(solution)/shard_map/ppermute | solution.py:313
  58.2 1.9 %collective-permute-start.26 = (f32[32,640]{1,0:T(8,128)S(1)}, f32[32,640]{1,0:T(8,128)S(1)}, u32[]{:S(2)}, u32[]{:S(2)}) collective-permute-start(f32[32,640]{1,0:T(8,128)S(1)} %get-tuple-element.61), channel_id=1, source_target_pairs={{0,16},{16,0},{32,48},{48,32},{64,80},{80,64},{96,112},{112,96},{1... | collective-permute-start | bytes 245768 | tf_op jit(solution)/shard_map/ppermute | solution.py:313
  60.1 1.3 %forward_dct.3 = (f32[32,640]{1,0:T(8,128)S(1)}, f32[128,640]{1,0:T(8,128)S(1)}, f32[16,5120]{1,0:T(8,128)S(1)}) custom-call(f32[2,8,1792]{2,1,0:T(8,128)S(1)} %get-tuple-element.75.refs_0_, f32[2,8,1664]{2,1,0:T(8,128)S(1)} %get-tuple-element.81.refs_1_, f32[2,8,1664]{2,1,0:T(8,128)S(1)} %get-tuple-element.79.refs_2_, ...), custom_call_target="tpu_custom_call" | custom-call | tf_op jit(solution)/shard_map/forward_dct/pallas_call | solution.py:150
  63.0 1.9 %collective-permute-start.20 = (f32[32,640]{1,0:T(8,128)S(1)}, f32[32,640]{1,0:T(8,128)S(1)}, u32[]{:S(2)}, u32[]{:S(2)}) collective-permute-start(f32[32,640]{1,0:T(8,128)S(1)} %get-tuple-element.60), channel_id=1, source_target_pairs={{0,16},{16,0},{32,48},{48,32},{64,80},{80,64},{96,112},{112,96},{1... | collective-permute-start | bytes 245768 | tf_op jit(solution)/shard_map/ppermute | solution.py:313
  65.0 5.9 %collective-permute-start.29 = (f32[32,640]{1,0:T(8,128)S(1)}, f32[32,640]{1,0:T(8,128)S(1)}, u32[]{:S(2)}, u32[]{:S(2)}) collective-permute-start(f32[32,640]{1,0:T(8,128)S(1)} %add_add_fusion.s0_ref), channel_id=1, source_target_pairs={{0,80},{16,64},{32,112},{48,96},{64,16},{80,0},{96,48},{112,32},{1... | collective-permute-start | bytes 245768 | tf_op jit(solution)/shard_map/ppermute | solution.py:315
  70.9 1.0 %collective-permute-start.30 = (f32[32,640]{1,0:T(8,128)S(1)}, f32[32,640]{1,0:T(8,128)S(1)}, u32[]{:S(2)}, u32[]{:S(2)}) collective-permute-start(f32[32,640]{1,0:T(8,128)S(1)} %add_add_fusion.s0_ref), channel_id=1, source_target_pairs={{0,112},{16,32},{32,16},{48,64},{64,48},{80,96},{96,80},{112,0},{1... | collective-permute-start | bytes 245768 | tf_op jit(solution)/shard_map/ppermute | solution.py:315
  72.4 4.2 %collective-permute-start.23 = (f32[32,640]{1,0:T(8,128)S(1)}, f32[32,640]{1,0:T(8,128)S(1)}, u32[]{:S(2)}, u32[]{:S(2)}) collective-permute-start(f32[32,640]{1,0:T(8,128)S(1)} %add_add_fusion.1.s0_ref), channel_id=1, source_target_pairs={{0,80},{16,64},{32,112},{48,96},{64,16},{80,0},{96,48},{112,32},{1... | collective-permute-start | bytes 245768 | tf_op jit(solution)/shard_map/ppermute | solution.py:315
  76.6 1.0 %collective-permute-start.24 = (f32[32,640]{1,0:T(8,128)S(1)}, f32[32,640]{1,0:T(8,128)S(1)}, u32[]{:S(2)}, u32[]{:S(2)}) collective-permute-start(f32[32,640]{1,0:T(8,128)S(1)} %add_add_fusion.1.s0_ref), channel_id=1, source_target_pairs={{0,112},{16,32},{32,16},{48,64},{64,48},{80,96},{96,80},{112,0},{1... | collective-permute-start | bytes 245768 | tf_op jit(solution)/shard_map/ppermute | solution.py:315
  78.1 1.6 %residual.1 = f32[4,8,5120]{2,1,0:T(8,128)} custom-call(f32[16,5120]{1,0:T(8,128)S(1)} %get-tuple-element.44.refs_0_, f32[16,5120]{1,0:T(8,128)S(1)} %get-tuple-element.57.refs_1_, f32[128,640]{1,0:T(8,128)S(1)} %get-tuple-element.58.refs_2_, f32[128,640]{1,0:T(8,128)S(1)} %get-tuple-element.59.refs_3_, f32[128,128]{1,0:T(8,128)S(1)} %copy-done.2), custom_call_target="tpu_custom_call" | custom-call | tf_op jit(solution)/shard_map/residual/pallas_call | solution.py:182
  79.7 0.9 %step_params.2.rest_0_ = f32[2,8,5120]{2,1,0:T(8,128)S(1)} custom-call(f32[4,8,5120]{2,1,0:T(8,128)S(1)} %copy-done.1, f32[32,640]{1,0:T(8,128)S(1)} %add_add_fusion.s0_ref, f32[32,640]{1,0:T(8,128)S(1)} %collective-permute-done.29.s1_ref, f32[32,640]{1,0:T(8,128)S(1)} %collective-permute-done.30.s2_ref, f32[32,640]{1,0:T(8,128)S(1)} %collective-permute-done.31.s3_ref, ...), custom_call_target="tpu_custom_call" | custom-call | tf_op jit(solution)/shard_map/step_params/pallas_call | solution.py:219
  80.7 1.0 %collective-permute-done.24.s2_ref = f32[32,640]{1,0:T(8,128)S(1)} collective-permute-done((f32[32,640]{1,0:T(8,128)S(1)}, f32[32,640]{1,0:T(8,128)S(1)}, u32[]{:S(2)}, u32[]{:S(2)}) %collective-permute-start.24) | collective-permute-done | bytes 81952 | tf_op jit(solution)/shard_map/ppermute | solution.py:315
  81.7 2.5 %collective-permute-done.25.s3_ref = f32[32,640]{1,0:T(8,128)S(1)} collective-permute-done((f32[32,640]{1,0:T(8,128)S(1)}, f32[32,640]{1,0:T(8,128)S(1)}, u32[]{:S(2)}, u32[]{:S(2)}) %collective-permute-start.25) | collective-permute-done | bytes 81952 | tf_op jit(solution)/shard_map/ppermute | solution.py:315
  84.2 1.8 %step_params.3 = f32[4,8,5120]{2,1,0:T(8,128)} custom-call(f32[4,8,5120]{2,1,0:T(8,128)S(1)} %copy-done.1, f32[32,640]{1,0:T(8,128)S(1)} %add_add_fusion.1.s0_ref, f32[32,640]{1,0:T(8,128)S(1)} %collective-permute-done.23.s1_ref, f32[32,640]{1,0:T(8,128)S(1)} %collective-permute-done.24.s2_ref, f32[32,640]{1,0:T(8,128)S(1)} %collective-permute-done.25.s3_ref, ...), custom_call_target="tpu_custom_call" | custom-call | tf_op jit(solution)/shard_map/step_params/pallas_call | solution.py:219
  (85 shorter events, 8.9 us)
Async XLA Ops:
  3.1 5.0 %collective-permute-start = (f32[8,2,8,5120]{3,2,1,0:T(8,128)S(1)}, f32[8,2,8,5120]{3,2,1,0:T(8,128)S(1)}, u32[]{:S(2)}, u32[]{:S(2)}) collective-permute-start(f32[8,2,8,5120]{3,2,1,0:T(8,128)S(1)} %get-tuple-element.33), channel_id=1, source_target_pairs={{0,1},{1,0},{2,3},{3,2},{4,5},{5,4},{6,7},{7,6},{8,9},{9,8},{10,11... | collective-permute-start | bytes 7864328 | tf_op jit(solution)/shard_map/ppermute | solution.py:299
  5.6 10.1 %collective-permute-start.10 = (f32[8,2,8,5120]{3,2,1,0:T(8,128)S(1)}, f32[8,2,8,5120]{3,2,1,0:T(8,128)S(1)}, u32[]{:S(2)}, u32[]{:S(2)}) collective-permute-start(f32[8,2,8,5120]{3,2,1,0:T(8,128)S(1)} %get-tuple-element.46), channel_id=1, source_target_pairs={{0,1},{1,0},{2,3},{3,2},{4,5},{5,4},{6,7},{7,6},{8,9},{9,8},{10,11... | collective-permute-start | bytes 7864328 | tf_op jit(solution)/shard_map/ppermute | solution.py:299
  8.3 19.0 %collective-permute-start.1 = (f32[2,2,2,8,1792]{4,3,2,0,1:T(8,128)S(1)}, f32[2,2,2,8,1792]{4,3,2,0,1:T(8,128)S(1)}, u32[]{:S(2)}, u32[]{:S(2)}) collective-permute-start(f32[2,2,2,8,1792]{4,3,2,0,1:T(8,128)S(1)} %bitcast.130), channel_id=1, source_target_pairs={{0,2},{1,3},{2,0},{3,1},{4,6},{5,7},{6,4},{7,5},{8,10},{9,11},{10,... | collective-permute-start | bytes 1376264 | tf_op jit(solution)/shard_map/ppermute | solution.py:267
  10.2 14.0 %collective-permute-start.2 = (f32[2,2,2,8,1664]{4,3,2,1,0:T(8,128)S(1)}, f32[2,2,2,8,1664]{4,3,2,1,0:T(8,128)S(1)}, u32[]{:S(2)}, u32[]{:S(2)}) collective-permute-start(f32[2,2,2,8,1664]{4,3,2,1,0:T(8,128)S(1)} %slice_bitcast_fusion.3), channel_id=1, source_target_pairs={{0,6},{1,7},{2,4},{3,5},{4,2},{5,3},{6,0},{7,1},{8,14},{9,15},{10,... | collective-permute-start | bytes 1277960 | tf_op jit(solution)/shard_map/ppermute | solution.py:267
  12.4 15.0 %collective-permute-start.3 = (f32[2,2,2,8,1664]{4,3,2,1,0:T(8,128)S(1)}, f32[2,2,2,8,1664]{4,3,2,1,0:T(8,128)S(1)}, u32[]{:S(2)}, u32[]{:S(2)}) collective-permute-start(f32[2,2,2,8,1664]{4,3,2,1,0:T(8,128)S(1)} %bitcast.132), channel_id=1, source_target_pairs={{0,8},{1,9},{2,10},{3,11},{4,12},{5,13},{6,14},{7,15},{8,0},{9,1},... | collective-permute-start | bytes 1277960 | tf_op jit(solution)/shard_map/ppermute | solution.py:267
  15.9 21.6 %collective-permute-start.11 = (f32[2,2,2,8,1792]{4,3,2,0,1:T(8,128)S(1)}, f32[2,2,2,8,1792]{4,3,2,0,1:T(8,128)S(1)}, u32[]{:S(2)}, u32[]{:S(2)}) collective-permute-start(f32[2,2,2,8,1792]{4,3,2,0,1:T(8,128)S(1)} %bitcast.129), channel_id=1, source_target_pairs={{0,2},{1,3},{2,0},{3,1},{4,6},{5,7},{6,4},{7,5},{8,10},{9,11},{10,... | collective-permute-start | bytes 1376264 | tf_op jit(solution)/shard_map/ppermute | solution.py:267
  16.8 16.5 %collective-permute-start.12 = (f32[2,2,2,8,1664]{4,3,2,1,0:T(8,128)S(1)}, f32[2,2,2,8,1664]{4,3,2,1,0:T(8,128)S(1)}, u32[]{:S(2)}, u32[]{:S(2)}) collective-permute-start(f32[2,2,2,8,1664]{4,3,2,1,0:T(8,128)S(1)} %slice_bitcast_fusion.1), channel_id=1, source_target_pairs={{0,6},{1,7},{2,4},{3,5},{4,2},{5,3},{6,0},{7,1},{8,14},{9,15},{10,... | collective-permute-start | bytes 1277960 | tf_op jit(solution)/shard_map/ppermute | solution.py:267
  24.2 13.4 %collective-permute-start.13 = (f32[2,2,2,8,1664]{4,3,2,1,0:T(8,128)S(1)}, f32[2,2,2,8,1664]{4,3,2,1,0:T(8,128)S(1)}, u32[]{:S(2)}, u32[]{:S(2)}) collective-permute-start(f32[2,2,2,8,1664]{4,3,2,1,0:T(8,128)S(1)} %bitcast.131), channel_id=1, source_target_pairs={{0,8},{1,9},{2,10},{3,11},{4,12},{5,13},{6,14},{7,15},{8,0},{9,1},... | collective-permute-start | bytes 1277960 | tf_op jit(solution)/shard_map/ppermute | solution.py:267
  27.4 15.9 %collective-permute-start.4 = (f32[2,2,8,1792]{3,2,1,0:T(8,128)S(1)}, f32[2,2,8,1792]{3,2,1,0:T(8,128)S(1)}, u32[]{:S(2)}, u32[]{:S(2)}) collective-permute-start(f32[2,2,8,1792]{3,2,1,0:T(8,128)S(1)} %slice_bitcast_fusion.6), channel_id=1, source_target_pairs={{0,6},{1,7},{2,4},{3,5},{4,2},{5,3},{6,0},{7,1},{8,14},{9,15},{10,... | collective-permute-start | bytes 688136 | tf_op jit(solution)/shard_map/ppermute | solution.py:267
  29.7 13.6 %collective-permute-start.5 = (f32[2,2,8,1664]{3,2,1,0:T(8,128)S(1)}, f32[2,2,8,1664]{3,2,1,0:T(8,128)S(1)}, u32[]{:S(2)}, u32[]{:S(2)}) collective-permute-start(f32[2,2,8,1664]{3,2,1,0:T(8,128)S(1)} %slice_bitcast_fusion.15), channel_id=1, source_target_pairs={{0,8},{1,9},{2,10},{3,11},{4,12},{5,13},{6,14},{7,15},{8,0},{9,1},... | collective-permute-start | bytes 638984 | tf_op jit(solution)/shard_map/ppermute | solution.py:267
  33.3 10.1 %collective-permute-start.6 = (f32[2,2,8,1664]{3,2,1,0:T(8,128)S(1)}, f32[2,2,8,1664]{3,2,1,0:T(8,128)S(1)}, u32[]{:S(2)}, u32[]{:S(2)}) collective-permute-start(f32[2,2,8,1664]{3,2,1,0:T(8,128)S(1)} %slice_bitcast_fusion.14), channel_id=1, source_target_pairs={{0,2},{1,3},{2,0},{3,1},{4,6},{5,7},{6,4},{7,5},{8,10},{9,11},{10,... | collective-permute-start | bytes 638984 | tf_op jit(solution)/shard_map/ppermute | solution.py:267
  37.6 12.1 %collective-permute-start.14 = (f32[2,2,8,1792]{3,2,1,0:T(8,128)S(1)}, f32[2,2,8,1792]{3,2,1,0:T(8,128)S(1)}, u32[]{:S(2)}, u32[]{:S(2)}) collective-permute-start(f32[2,2,8,1792]{3,2,1,0:T(8,128)S(1)} %slice_bitcast_fusion.4), channel_id=1, source_target_pairs={{0,6},{1,7},{2,4},{3,5},{4,2},{5,3},{6,0},{7,1},{8,14},{9,15},{10,... | collective-permute-start | bytes 688136 | tf_op jit(solution)/shard_map/ppermute | solution.py:267
  39.9 7.4 %collective-permute-start.15 = (f32[2,2,8,1664]{3,2,1,0:T(8,128)S(1)}, f32[2,2,8,1664]{3,2,1,0:T(8,128)S(1)}, u32[]{:S(2)}, u32[]{:S(2)}) collective-permute-start(f32[2,2,8,1664]{3,2,1,0:T(8,128)S(1)} %slice_bitcast_fusion.11), channel_id=1, source_target_pairs={{0,8},{1,9},{2,10},{3,11},{4,12},{5,13},{6,14},{7,15},{8,0},{9,1},... | collective-permute-start | bytes 638984 | tf_op jit(solution)/shard_map/ppermute | solution.py:267
  43.3 6.4 %collective-permute-start.16 = (f32[2,2,8,1664]{3,2,1,0:T(8,128)S(1)}, f32[2,2,8,1664]{3,2,1,0:T(8,128)S(1)}, u32[]{:S(2)}, u32[]{:S(2)}) collective-permute-start(f32[2,2,8,1664]{3,2,1,0:T(8,128)S(1)} %slice_bitcast_fusion.10), channel_id=1, source_target_pairs={{0,2},{1,3},{2,0},{3,1},{4,6},{5,7},{6,4},{7,5},{8,10},{9,11},{10,... | collective-permute-start | bytes 638984 | tf_op jit(solution)/shard_map/ppermute | solution.py:267
  43.6 11.6 %collective-permute-start.7 = (f32[2,8,1792]{2,1,0:T(8,128)S(1)}, f32[2,8,1792]{2,1,0:T(8,128)S(1)}, u32[]{:S(2)}, u32[]{:S(2)}) collective-permute-start(f32[2,8,1792]{2,1,0:T(8,128)S(1)} %get-tuple-element.76), channel_id=1, source_target_pairs={{0,8},{1,9},{2,10},{3,11},{4,12},{5,13},{6,14},{7,15},{8,0},{9,1},... | collective-permute-start | bytes 344072 | tf_op jit(solution)/shard_map/ppermute | solution.py:267
  44.6 7.3 %collective-permute-start.8 = (f32[2,8,1664]{2,1,0:T(8,128)S(1)}, f32[2,8,1664]{2,1,0:T(8,128)S(1)}, u32[]{:S(2)}, u32[]{:S(2)}) collective-permute-start(f32[2,8,1664]{2,1,0:T(8,128)S(1)} %get-tuple-element.84), channel_id=1, source_target_pairs={{0,2},{1,3},{2,0},{3,1},{4,6},{5,7},{6,4},{7,5},{8,10},{9,11},{10,... | collective-permute-start | bytes 319496 | tf_op jit(solution)/shard_map/ppermute | solution.py:267
  47.3 7.9 %collective-permute-start.9 = (f32[2,8,1664]{2,1,0:T(8,128)S(1)}, f32[2,8,1664]{2,1,0:T(8,128)S(1)}, u32[]{:S(2)}, u32[]{:S(2)}) collective-permute-start(f32[2,8,1664]{2,1,0:T(8,128)S(1)} %get-tuple-element.82), channel_id=1, source_target_pairs={{0,6},{1,7},{2,4},{3,5},{4,2},{5,3},{6,0},{7,1},{8,14},{9,15},{10,... | collective-permute-start | bytes 319496 | tf_op jit(solution)/shard_map/ppermute | solution.py:267
  49.8 10.3 %collective-permute-start.17 = (f32[2,8,1792]{2,1,0:T(8,128)S(1)}, f32[2,8,1792]{2,1,0:T(8,128)S(1)}, u32[]{:S(2)}, u32[]{:S(2)}) collective-permute-start(f32[2,8,1792]{2,1,0:T(8,128)S(1)} %get-tuple-element.74), channel_id=1, source_target_pairs={{0,8},{1,9},{2,10},{3,11},{4,12},{5,13},{6,14},{7,15},{8,0},{9,1},... | collective-permute-start | bytes 344072 | tf_op jit(solution)/shard_map/ppermute | solution.py:267
  51.9 6.3 %collective-permute-start.18 = (f32[2,8,1664]{2,1,0:T(8,128)S(1)}, f32[2,8,1664]{2,1,0:T(8,128)S(1)}, u32[]{:S(2)}, u32[]{:S(2)}) collective-permute-start(f32[2,8,1664]{2,1,0:T(8,128)S(1)} %get-tuple-element.80), channel_id=1, source_target_pairs={{0,2},{1,3},{2,0},{3,1},{4,6},{5,7},{6,4},{7,5},{8,10},{9,11},{10,... | collective-permute-start | bytes 319496 | tf_op jit(solution)/shard_map/ppermute | solution.py:267
  51.9 8.2 %collective-permute-start.19 = (f32[2,8,1664]{2,1,0:T(8,128)S(1)}, f32[2,8,1664]{2,1,0:T(8,128)S(1)}, u32[]{:S(2)}, u32[]{:S(2)}) collective-permute-start(f32[2,8,1664]{2,1,0:T(8,128)S(1)} %get-tuple-element.78), channel_id=1, source_target_pairs={{0,6},{1,7},{2,4},{3,5},{4,2},{5,3},{6,0},{7,1},{8,14},{9,15},{10,... | collective-permute-start | bytes 319496 | tf_op jit(solution)/shard_map/ppermute | solution.py:267
  56.5 6.5 %collective-permute-start.27 = (f32[32,640]{1,0:T(8,128)S(1)}, f32[32,640]{1,0:T(8,128)S(1)}, u32[]{:S(2)}, u32[]{:S(2)}) collective-permute-start(f32[32,640]{1,0:T(8,128)S(1)} %get-tuple-element.61), channel_id=1, source_target_pairs={{0,128},{16,144},{32,160},{48,176},{64,192},{80,208},{96,224},{112... | collective-permute-start | bytes 245768 | tf_op jit(solution)/shard_map/ppermute | solution.py:313
  57.3 7.7 %collective-permute-start.28 = (f32[32,640]{1,0:T(8,128)S(1)}, f32[32,640]{1,0:T(8,128)S(1)}, u32[]{:S(2)}, u32[]{:S(2)}) collective-permute-start(f32[32,640]{1,0:T(8,128)S(1)} %get-tuple-element.61), channel_id=1, source_target_pairs={{0,144},{16,128},{32,176},{48,160},{64,208},{80,192},{96,240},{112... | collective-permute-start | bytes 245768 | tf_op jit(solution)/shard_map/ppermute | solution.py:313
  58.2 6.8 %collective-permute-start.26 = (f32[32,640]{1,0:T(8,128)S(1)}, f32[32,640]{1,0:T(8,128)S(1)}, u32[]{:S(2)}, u32[]{:S(2)}) collective-permute-start(f32[32,640]{1,0:T(8,128)S(1)} %get-tuple-element.61), channel_id=1, source_target_pairs={{0,16},{16,0},{32,48},{48,32},{64,80},{80,64},{96,112},{112,96},{1... | collective-permute-start | bytes 245768 | tf_op jit(solution)/shard_map/ppermute | solution.py:313
  61.4 10.6 %collective-permute-start.21 = (f32[32,640]{1,0:T(8,128)S(1)}, f32[32,640]{1,0:T(8,128)S(1)}, u32[]{:S(2)}, u32[]{:S(2)}) collective-permute-start(f32[32,640]{1,0:T(8,128)S(1)} %get-tuple-element.60), channel_id=1, source_target_pairs={{0,128},{16,144},{32,160},{48,176},{64,192},{80,208},{96,224},{112... | collective-permute-start | bytes 245768 | tf_op jit(solution)/shard_map/ppermute | solution.py:313
  62.1 10.3 %collective-permute-start.22 = (f32[32,640]{1,0:T(8,128)S(1)}, f32[32,640]{1,0:T(8,128)S(1)}, u32[]{:S(2)}, u32[]{:S(2)}) collective-permute-start(f32[32,640]{1,0:T(8,128)S(1)} %get-tuple-element.60), channel_id=1, source_target_pairs={{0,144},{16,128},{32,176},{48,160},{64,208},{80,192},{96,240},{112... | collective-permute-start | bytes 245768 | tf_op jit(solution)/shard_map/ppermute | solution.py:313
  63.0 9.4 %collective-permute-start.20 = (f32[32,640]{1,0:T(8,128)S(1)}, f32[32,640]{1,0:T(8,128)S(1)}, u32[]{:S(2)}, u32[]{:S(2)}) collective-permute-start(f32[32,640]{1,0:T(8,128)S(1)} %get-tuple-element.60), channel_id=1, source_target_pairs={{0,16},{16,0},{32,48},{48,32},{64,80},{80,64},{96,112},{112,96},{1... | collective-permute-start | bytes 245768 | tf_op jit(solution)/shard_map/ppermute | solution.py:313
  65.0 12.7 %collective-permute-start.29 = (f32[32,640]{1,0:T(8,128)S(1)}, f32[32,640]{1,0:T(8,128)S(1)}, u32[]{:S(2)}, u32[]{:S(2)}) collective-permute-start(f32[32,640]{1,0:T(8,128)S(1)} %add_add_fusion.s0_ref), channel_id=1, source_target_pairs={{0,80},{16,64},{32,112},{48,96},{64,16},{80,0},{96,48},{112,32},{1... | collective-permute-start | bytes 245768 | tf_op jit(solution)/shard_map/ppermute | solution.py:315
  70.9 8.8 %collective-permute-start.30 = (f32[32,640]{1,0:T(8,128)S(1)}, f32[32,640]{1,0:T(8,128)S(1)}, u32[]{:S(2)}, u32[]{:S(2)}) collective-permute-start(f32[32,640]{1,0:T(8,128)S(1)} %add_add_fusion.s0_ref), channel_id=1, source_target_pairs={{0,112},{16,32},{32,16},{48,64},{64,48},{80,96},{96,80},{112,0},{1... | collective-permute-start | bytes 245768 | tf_op jit(solution)/shard_map/ppermute | solution.py:315
  71.9 7.8 %collective-permute-start.31 = (f32[32,640]{1,0:T(8,128)S(1)}, f32[32,640]{1,0:T(8,128)S(1)}, u32[]{:S(2)}, u32[]{:S(2)}) collective-permute-start(f32[32,640]{1,0:T(8,128)S(1)} %add_add_fusion.s0_ref), channel_id=1, source_target_pairs={{0,96},{16,48},{32,0},{48,80},{64,32},{80,112},{96,64},{112,16},{1... | collective-permute-start | bytes 245768 | tf_op jit(solution)/shard_map/ppermute | solution.py:315
  72.4 8.2 %collective-permute-start.23 = (f32[32,640]{1,0:T(8,128)S(1)}, f32[32,640]{1,0:T(8,128)S(1)}, u32[]{:S(2)}, u32[]{:S(2)}) collective-permute-start(f32[32,640]{1,0:T(8,128)S(1)} %add_add_fusion.1.s0_ref), channel_id=1, source_target_pairs={{0,80},{16,64},{32,112},{48,96},{64,16},{80,0},{96,48},{112,32},{1... | collective-permute-start | bytes 245768 | tf_op jit(solution)/shard_map/ppermute | solution.py:315
  76.6 5.1 %collective-permute-start.24 = (f32[32,640]{1,0:T(8,128)S(1)}, f32[32,640]{1,0:T(8,128)S(1)}, u32[]{:S(2)}, u32[]{:S(2)}) collective-permute-start(f32[32,640]{1,0:T(8,128)S(1)} %add_add_fusion.1.s0_ref), channel_id=1, source_target_pairs={{0,112},{16,32},{32,16},{48,64},{64,48},{80,96},{96,80},{112,0},{1... | collective-permute-start | bytes 245768 | tf_op jit(solution)/shard_map/ppermute | solution.py:315
  77.7 6.6 %collective-permute-start.25 = (f32[32,640]{1,0:T(8,128)S(1)}, f32[32,640]{1,0:T(8,128)S(1)}, u32[]{:S(2)}, u32[]{:S(2)}) collective-permute-start(f32[32,640]{1,0:T(8,128)S(1)} %add_add_fusion.1.s0_ref), channel_id=1, source_target_pairs={{0,96},{16,48},{32,0},{48,80},{64,32},{80,112},{96,64},{112,16},{1... | collective-permute-start | bytes 245768 | tf_op jit(solution)/shard_map/ppermute | solution.py:315
  (4 other events, 59.3 us)

commit v3 on v2

--- a/solution.py
+++ b/solution.py
@@ -9,10 +9,13 @@
 SPAN = 64
 BAND = 16
 LANES = 128
-VMEM_LIMIT = 12 * 2**20
+VMEM_LIMIT = 10 * 2**20
 EXACT = lax.Precision.HIGHEST
 CHUNKS = ((0, 2), (2, 2))
-ORDERS = ((1, 2, 0), (2, 0, 1), (0, 1, 2))
+PIECES = (
+    ((10, (0, 1, 2)), (10, (1, 2, 0)), (20, (2, 0, 1))),
+    ((20, (0, 1, 2)), (20, (1, 2, 0))),
+)
 
 
 def table128():
@@ -51,42 +54,46 @@
     return [(i, i ^ mask) for i in range(16)]
 
 
-def split_cores(grads, chips, core, first, count):
+def split_cores(grads, first, count):
     width = grads.shape[2]
-    chip_count = 8
-
-    def kernel(chips_ref, core_ref, grads_ref, other_ref, own_ref, held, sems):
-        def fetch(i):
-            start = pl.multiple_of(chips_ref[i] * 16, 16)
+    cube = [(dy, a, b) for dy in range(2) for a in range(2) for b in range(2)]
+
+    def kernel(grads_ref, other_ref, own_ref, held, sems):
+        me = lax.axis_index("fsdp")
+        core, x, y = me % 2, (me // 2) % 4, me // 8
+        across = {(0, 0): x, (0, 1): 3 - x, (1, 0): x + 1 - 2 * (x % 2), (1, 1): (x + 2) % 4}
+
+        def fetch(side, i):
+            dy, a, b = cube[i]
+            chip = (1 - y if dy else y) * 4 + across[a, b]
+            start = (chip * 2 + (core if side else 1 - core)) * 8
             return pltpu.make_async_copy(
-                grads_ref.at[pl.ds(first, count), pl.ds(start, 16)], held.at[i], sems.at[i]
+                grads_ref.at[pl.ds(first, count), pl.ds(pl.multiple_of(start, 8), 8)],
+                held.at[side, i],
+                sems.at[side, i],
             )
 
-        for i in range(chip_count):
-            fetch(i).start()
-        is_low = core_ref[0] == 0
-        for i in range(chip_count):
-            fetch(i).wait()
-            for layer in range(count):
-                both = held[i, layer].astype(jnp.float32)
-                own_ref[i, layer] = jnp.where(is_low, both[:8], both[8:])
-                other_ref[i, layer] = jnp.where(is_low, both[8:], both[:8])
-
-    out = jax.ShapeDtypeStruct((chip_count, count, 8, width), jnp.float32)
-    smem = pl.BlockSpec(memory_space=pltpu.SMEM)
-    return pl.pallas_call(
-        kernel,
-        in_specs=[smem, smem, pl.BlockSpec(memory_space=pltpu.HBM)],
+        for side in range(2):
+            for i in range(8):
+                fetch(side, i).start()
+        for side, out_ref in enumerate((other_ref, own_ref)):
+            for i in range(8):
+                fetch(side, i).wait()
+                for layer in range(count):
+                    out_ref[i, layer] = held[side, i, layer].astype(jnp.float32)
+
+    out = jax.ShapeDtypeStruct((8, count, 8, width), jnp.float32)
+    return pl.pallas_call(
+        kernel,
+        in_specs=[pl.BlockSpec(memory_space=pltpu.HBM)],
         out_shape=[out, out],
         scratch_shapes=[
-            pltpu.VMEM((chip_count, count, 16, width), grads.dtype),
-            pltpu.SemaphoreType.DMA((chip_count,)),
+            pltpu.VMEM((2, 8, count, 8, width), grads.dtype),
+            pltpu.SemaphoreType.DMA((2, 8)),
         ],
-        compiler_params=pltpu.CompilerParams(
-            vmem_limit_bytes=chip_count * count * width * 8 * 12 + 2**20
-        ),
+        compiler_params=pltpu.CompilerParams(vmem_limit_bytes=VMEM_LIMIT),
         name="split_cores",
-    )(chips, core, grads)
+    )(grads)
 
 
 def padded(count):
@@ -188,14 +195,14 @@
 
 
 def step_params(params, sums, band, table, before, replicas, first, count):
-    width = params.shape[2]
+    layers, _, width = params.shape
     rows = 8 * count
     blocks = band.shape[1]
+    pieces = 5
+    wide = width // pieces
 
     def kernel(params_ref, s0_ref, s1_ref, s2_ref, s3_ref, band_ref, table_ref, *rest):
-        out_ref, dense = rest[-2:]
-        if before is not None:
-            out_ref[:first] = rest[0][...]
+        out_ref, dense, held, sems = rest[-4:]
         index = lax.broadcasted_iota(jnp.int32, (SPAN, LANES), 0)
         for tile in range(blocks // LANES):
             lanes = slice(tile * LANES, (tile + 1) * LANES)
@@ -209,17 +216,39 @@
                     spread = jnp.where(hit, mean[row : row + 1], spread)
                 dense[h * SPAN : (h + 1) * SPAN, lanes] = spread
         update = inverse(dense[...], table_ref[...])
-        for t in range(width // LANES):
-            lanes = slice(t * LANES, (t + 1) * LANES)
-            old = params_ref[first : first + count, :, lanes].reshape(rows, LANES)
-            new = old - 0.5 * update[t * rows : (t + 1) * rows]
-            out_ref[first : first + count, :, lanes] = new.reshape(count, 8, LANES)
+        copies = []
+        for piece in range(pieces):
+            for t in range(piece * wide // LANES, (piece + 1) * wide // LANES):
+                lanes = slice(t * LANES, (t + 1) * LANES)
+                old = params_ref[first : first + count, :, lanes].reshape(rows, LANES)
+                new = old - 0.5 * update[t * rows : (t + 1) * rows]
+                held[:, :, lanes] = new.reshape(count, 8, LANES)
+            lanes = pl.ds(piece * wide, wide)
+            copies.append(
+                pltpu.make_async_copy(
+                    held.at[:, :, lanes],
+                    out_ref.at[pl.ds(first, count), :, lanes],
+                    sems.at[piece],
+                )
+            )
+            copies[-1].start()
+        for copy in copies:
+            copy.wait()
 
     extra = [] if before is None else [before]
-    return pl.pallas_call(
-        kernel,
-        out_shape=jax.ShapeDtypeStruct((first + count, 8, width), jnp.float32),
-        scratch_shapes=[pltpu.VMEM((LANES, blocks), jnp.float32)],
+    vmem = pl.BlockSpec(memory_space=pltpu.VMEM)
+    anywhere = pl.BlockSpec(memory_space=pl.ANY)
+    return pl.pallas_call(
+        kernel,
+        in_specs=[vmem] * 7 + [anywhere] * len(extra),
+        out_specs=anywhere,
+        out_shape=jax.ShapeDtypeStruct((layers, 8, width), jnp.float32),
+        scratch_shapes=[
+            pltpu.VMEM((LANES, blocks), jnp.float32),
+            pltpu.VMEM((count, 8, width), jnp.float32),
+            pltpu.SemaphoreType.DMA((pieces,)),
+        ],
+        input_output_aliases={7: 0} if extra else {},
         compiler_params=pltpu.CompilerParams(vmem_limit_bytes=VMEM_LIMIT),
         name="step_params",
     )(params, *sums, band, table, *extra)
@@ -257,14 +286,13 @@
     )(band)
 
 
-def halve(pieces, step):
+def halve(pieces, orders, step):
     keeps, recvs = [], []
-    for piece, order in zip(pieces, ORDERS):
-        dim = order[step]
-        axis = sorted(order[step:]).index(dim)
-        keeps.append(lax.index_in_dim(piece, 0, axis, keepdims=False))
-        send = lax.index_in_dim(piece, 1, axis, keepdims=False)
-        recvs.append(lax.ppermute(send, "fsdp", HALVES[dim]))
+    for piece, order in zip(pieces, orders):
+        axis = sorted(order[step:]).index(order[step])
+        keep, send = [lax.index_in_dim(piece, i, axis, keepdims=False) for i in range(2)]
+        keeps.append(keep)
+        recvs.append(lax.ppermute(send, "fsdp", HALVES[order[step]]))
     return keeps, list(lax.optimization_barrier(tuple(recvs)))
 
 
@@ -283,26 +311,23 @@
     moment = momentum[0]
     layers, _, width = params.shape
     replicas = lax.axis_size("rep")
-    me = lax.axis_index("fsdp").astype(jnp.int32)
-    core = (me % 2).reshape(1)
-    x, y = (me // 2) % 4, me // 8
-    chips = jnp.stack(
-        [(y ^ dy) * 4 + column for dy in range(2) for column in (x, 3 - x, x ^ 1, x ^ 2)]
-    )
-    tiles = width // LANES
-    cuts = [0, (tiles + 2) // 3 * LANES, ((tiles + 2) // 3 + (tiles + 1) // 3) * LANES, width]
     bands = band_rows(band.transpose(0, 1, 3, 2))
     source = pltpu.with_memory_space_constraint(grads, pltpu.HBM)
-    pieces = []
-    for first, count in CHUNKS:
-        other, own = split_cores(source, chips, core, first, count)
+    pieces, orders = [], []
+    for (first, count), parts in zip(CHUNKS, PIECES):
+        other, own = split_cores(source, first, count)
         got = lax.ppermute(other, "fsdp", CORE)
-        both = [
-            own[..., low:high] + got[..., low:high] for low, high in zip(cuts[:-1], cuts[1:])
-        ]
-        pieces.append([p.reshape(2, 2, 2, *p.shape[1:]) for p in both])
+        at = 0
+        both = []
+        for tiles, _ in parts:
+            lanes = slice(at, at + tiles * LANES)
+            part = own[..., lanes] + got[..., lanes]
+            both.append(part.reshape(2, 2, 2, *part.shape[1:]))
+            at += tiles * LANES
+        pieces.append(both)
+        orders.append([order for _, order in parts])
     for step in range(3):
-        halved = [halve(p, step) for p in pieces]
+        halved = [halve(p, o, step) for p, o in zip(pieces, orders)]
         if step < 2:
             pieces = [[k + r for k, r in zip(*h)] for h in halved]
     forwards = []

time: 86.3 us -> 83.4 us (0.966)
  starting transfers between devices: 50.9 us -> 43.4 us
  waiting for transfers between devices: 20.2 us -> 25 us
    ppermute x18 -> x15, starting transfers between devices: 30 us -> 22.5 us  [halve(): recvs.append(lax.ppermute(send, 'fsdp', HALVES[order[step]]))]
    ppermute x18 -> x15, waiting for transfers between devices: 14.6 us -> 19.8 us  [halve(): recvs.append(lax.ppermute(send, 'fsdp', HALVES[order[step]]))]
  transfers between devices with their start and end apart: 32 -> 29, of which waited for: 7 -> 11; matrix products, arithmetic and copies ran while one was open for 2% -> 2% of each run, Pallas kernels for 9% -> 10%
where the time goes in v3:
time: 83.4 us; the launch traced here: 83.2 us
  starting transfers between devices  43.4 us (52%)
  waiting for transfers between devices  25 us (30%)
  Pallas kernels  11.8 us (14%)
  other arithmetic  1.25 us (1%)
  between operations  1.11 us (1%)
    ppermute x15, starting transfers between devices, halve(): recvs.append(lax.ppermute(send, 'fsdp', HALVES[order[step]]))  22.5 us
    ppermute x15, waiting for transfers between devices, halve(): recvs.append(lax.ppermute(send, 'fsdp', HALVES[order[step]]))  19.8 us
    ppermute x6, starting transfers between devices, shards(): far = [lax.ppermute(four, 'rep', p) for p in (OPPOSITE, BESIDE, BEYOND)]  13.1 us
    ppermute x6, starting transfers between devices, shards(): near = [lax.ppermute(values, 'rep', rep_pairs(m)) for m in (1, 8, 9)]  7.15 us
    pallas_call x2, Pallas kernels, split_cores(): pl.pallas_call(kernel, in_specs=[pl.BlockSpec(memory_space=pltpu.HBM)], o...  3.95 us
    pallas_call x2, Pallas kernels, step_params(): pl.pallas_call(kernel, in_specs=[vmem] * 7 + [anywhere] * len(extra), out...  3.22 us
    ppermute x6, waiting for transfers between devices, shards(): far = [lax.ppermute(four, 'rep', p) for p in (OPPOSITE, BESIDE, BEYOND)]  2.86 us
    pallas_call x2, Pallas kernels, forward(): pl.pallas_call(kernel, out_shape=shapes, compiler_params=pltpu.CompilerPa...  2.54 us
  transfers between devices with their start and end apart: 29, of which 11 were waited for; matrix products, arithmetic and copies ran while one was open for 2% of the time, Pallas kernels for 10%

profile of v3, /device:TPU:32, one launch (start us, length us, event | category | flops | bytes accessed | tf_op | source)
XLA Modules:
  0.0 83.2 jit_solution(5897724742715516075)
XLA Ops:
  0.6 2.0 %split_cores.2 = (f32[8,2,8,5120]{3,2,1,0:T(8,128)S(1)}, f32[8,2,8,5120]{3,2,1,0:T(8,128)S(1)}) custom-call(bf16[4,128,5120]{2,1,0:T(8,128)(2,1)} %bitcast.88), custom_call_target="tpu_custom_call" | custom-call | tf_op jit(solution)/shard_map/split_cores/pallas_call | solution.py:86
  2.7 2.0 %split_cores.3 = (f32[8,2,8,5120]{3,2,1,0:T(8,128)S(1)}, f32[8,2,8,5120]{3,2,1,0:T(8,128)S(1)}) custom-call(bf16[4,128,5120]{2,1,0:T(8,128)(2,1)} %bitcast.89), custom_call_target="tpu_custom_call" | custom-call | tf_op jit(solution)/shard_map/split_cores/pallas_call | solution.py:86
  5.2 2.4 %collective-permute-done = f32[8,2,8,5120]{3,2,1,0:T(8,128)S(1)} collective-permute-done((f32[8,2,8,5120]{3,2,1,0:T(8,128)S(1)}, f32[8,2,8,5120]{3,2,1,0:T(8,128)S(1)}, u32[]{:S(2)}, u32[]{:S(2)}) %collective-permute-start) | collective-permute-done | bytes 2621472 | tf_op jit(solution)/shard_map/ppermute | solution.py:319
  7.9 3.3 %collective-permute-start.1 = (f32[2,2,2,8,1280]{4,3,2,1,0:T(8,128)S(1)}, f32[2,2,2,8,1280]{4,3,2,1,0:T(8,128)S(1)}, u32[]{:S(2)}, u32[]{:S(2)}) collective-permute-start(f32[2,2,2,8,1280]{4,3,2,1,0:T(8,128)S(1)} %bitcast.99), channel_id=1, source_target_pairs={{0,8},{1,9},{2,10},{3,11},{4,12},{5,13},{6,14},{7,15},{8,0},{9,1},... | collective-permute-start | bytes 983048 | tf_op jit(solution)/shard_map/ppermute | solution.py:295
  11.3 1.6 %collective-permute-start.2 = (f32[2,2,2,8,1280]{4,3,2,0,1:T(8,128)S(1)}, f32[2,2,2,8,1280]{4,3,2,0,1:T(8,128)S(1)}, u32[]{:S(2)}, u32[]{:S(2)}) collective-permute-start(f32[2,2,2,8,1280]{4,3,2,0,1:T(8,128)S(1)} %bitcast.100), channel_id=1, source_target_pairs={{0,2},{1,3},{2,0},{3,1},{4,6},{5,7},{6,4},{7,5},{8,10},{9,11},{10,... | collective-permute-start | bytes 983048 | tf_op jit(solution)/shard_map/ppermute | solution.py:295
  13.1 2.2 %collective-permute-start.3 = (f32[2,2,2,8,2560]{4,3,2,1,0:T(8,128)S(1)}, f32[2,2,2,8,2560]{4,3,2,1,0:T(8,128)S(1)}, u32[]{:S(2)}, u32[]{:S(2)}) collective-permute-start(f32[2,2,2,8,2560]{4,3,2,1,0:T(8,128)S(1)} %slice_bitcast_fusion.1), channel_id=1, source_target_pairs={{0,6},{1,7},{2,4},{3,5},{4,2},{5,3},{6,0},{7,1},{8,14},{9,15},{10,... | collective-permute-start | bytes 1966088 | tf_op jit(solution)/shard_map/ppermute | solution.py:295
  16.9 2.4 %collective-permute-done.1 = f32[2,2,2,8,1280]{4,3,2,1,0:T(8,128)S(1)} collective-permute-done((f32[2,2,2,8,1280]{4,3,2,1,0:T(8,128)S(1)}, f32[2,2,2,8,1280]{4,3,2,1,0:T(8,128)S(1)}, u32[]{:S(2)}, u32[]{:S(2)}) %collective-permute-start.1) | collective-permute-done | bytes 327712 | tf_op jit(solution)/shard_map/ppermute | solution.py:295
  19.3 2.7 %collective-permute-done.2 = f32[2,2,2,8,1280]{4,3,2,0,1:T(8,128)S(1)} collective-permute-done((f32[2,2,2,8,1280]{4,3,2,0,1:T(8,128)S(1)}, f32[2,2,2,8,1280]{4,3,2,0,1:T(8,128)S(1)}, u32[]{:S(2)}, u32[]{:S(2)}) %collective-permute-start.2) | collective-permute-done | bytes 327712 | tf_op jit(solution)/shard_map/ppermute | solution.py:295
  21.9 8.6 %collective-permute-done.3 = f32[2,2,2,8,2560]{4,3,2,1,0:T(8,128)S(1)} collective-permute-done((f32[2,2,2,8,2560]{4,3,2,1,0:T(8,128)S(1)}, f32[2,2,2,8,2560]{4,3,2,1,0:T(8,128)S(1)}, u32[]{:S(2)}, u32[]{:S(2)}) %collective-permute-start.3) | collective-permute-done | bytes 655392 | tf_op jit(solution)/shard_map/ppermute | solution.py:295
  30.8 2.2 %collective-permute-start.5 = (f32[2,2,8,1280]{3,2,1,0:T(8,128)S(1)}, f32[2,2,8,1280]{3,2,1,0:T(8,128)S(1)}, u32[]{:S(2)}, u32[]{:S(2)}) collective-permute-start(f32[2,2,8,1280]{3,2,1,0:T(8,128)S(1)} %slice_bitcast_fusion.15), channel_id=1, source_target_pairs={{0,6},{1,7},{2,4},{3,5},{4,2},{5,3},{6,0},{7,1},{8,14},{9,15},{10,... | collective-permute-start | bytes 491528 | tf_op jit(solution)/shard_map/ppermute | solution.py:295
  33.5 2.5 %collective-permute-done.12 = f32[2,2,2,8,2560]{4,3,2,0,1:T(8,128)S(1)} collective-permute-done((f32[2,2,2,8,2560]{4,3,2,0,1:T(8,128)S(1)}, f32[2,2,2,8,2560]{4,3,2,0,1:T(8,128)S(1)}, u32[]{:S(2)}, u32[]{:S(2)}) %collective-permute-start.12) | collective-permute-done | bytes 655392 | tf_op jit(solution)/shard_map/ppermute | solution.py:295
  36.1 1.6 %collective-permute-start.13 = (f32[2,2,8,2560]{3,2,1,0:T(8,128)S(1)}, f32[2,2,8,2560]{3,2,1,0:T(8,128)S(1)}, u32[]{:S(2)}, u32[]{:S(2)}) collective-permute-start(f32[2,2,8,2560]{3,2,1,0:T(8,128)S(1)} %slice_bitcast_fusion.4), channel_id=1, source_target_pairs={{0,2},{1,3},{2,0},{3,1},{4,6},{5,7},{6,4},{7,5},{8,10},{9,11},{10,... | collective-permute-start | bytes 983048 | tf_op jit(solution)/shard_map/ppermute | solution.py:295
  37.8 2.2 %collective-permute-start.14 = (f32[2,2,8,2560]{3,2,1,0:T(8,128)S(1)}, f32[2,2,8,2560]{3,2,1,0:T(8,128)S(1)}, u32[]{:S(2)}, u32[]{:S(2)}) collective-permute-start(f32[2,2,8,2560]{3,2,1,0:T(8,128)S(1)} %slice_bitcast_fusion.3), channel_id=1, source_target_pairs={{0,6},{1,7},{2,4},{3,5},{4,2},{5,3},{6,0},{7,1},{8,14},{9,15},{10,... | collective-permute-start | bytes 983048 | tf_op jit(solution)/shard_map/ppermute | solution.py:295
  40.0 2.7 %collective-permute-done.6 = f32[2,2,8,2560]{3,2,1,0:T(8,128)S(1)} collective-permute-done((f32[2,2,8,2560]{3,2,1,0:T(8,128)S(1)}, f32[2,2,8,2560]{3,2,1,0:T(8,128)S(1)}, u32[]{:S(2)}, u32[]{:S(2)}) %collective-permute-start.6) | collective-permute-done | bytes 327712 | tf_op jit(solution)/shard_map/ppermute | solution.py:295
  42.8 1.2 %collective-permute-start.7 = (f32[2,8,1280]{2,1,0:T(8,128)S(1)}, f32[2,8,1280]{2,1,0:T(8,128)S(1)}, u32[]{:S(2)}, u32[]{:S(2)}) collective-permute-start(f32[2,8,1280]{2,1,0:T(8,128)S(1)} %get-tuple-element.76), channel_id=1, source_target_pairs={{0,6},{1,7},{2,4},{3,5},{4,2},{5,3},{6,0},{7,1},{8,14},{9,15},{10,... | collective-permute-start | bytes 245768 | tf_op jit(solution)/shard_map/ppermute | solution.py:295
  44.1 2.5 %collective-permute-start.8 = (f32[2,8,1280]{2,1,0:T(8,128)S(1)}, f32[2,8,1280]{2,1,0:T(8,128)S(1)}, u32[]{:S(2)}, u32[]{:S(2)}) collective-permute-start(f32[2,8,1280]{2,1,0:T(8,128)S(1)} %get-tuple-element.74), channel_id=1, source_target_pairs={{0,8},{1,9},{2,10},{3,11},{4,12},{5,13},{6,14},{7,15},{8,0},{9,1},... | collective-permute-start | bytes 245768 | tf_op jit(solution)/shard_map/ppermute | solution.py:295
  47.3 2.2 %collective-permute-start.15 = (f32[2,8,2560]{2,1,0:T(8,128)S(1)}, f32[2,8,2560]{2,1,0:T(8,128)S(1)}, u32[]{:S(2)}, u32[]{:S(2)}) collective-permute-start(f32[2,8,2560]{2,1,0:T(8,128)S(1)} %get-tuple-element.70), channel_id=1, source_target_pairs={{0,6},{1,7},{2,4},{3,5},{4,2},{5,3},{6,0},{7,1},{8,14},{9,15},{10,... | collective-permute-start | bytes 491528 | tf_op jit(solution)/shard_map/ppermute | solution.py:295
  49.5 1.8 %collective-permute-start.16 = (f32[2,8,2560]{2,1,0:T(8,128)S(1)}, f32[2,8,2560]{2,1,0:T(8,128)S(1)}, u32[]{:S(2)}, u32[]{:S(2)}) collective-permute-start(f32[2,8,2560]{2,1,0:T(8,128)S(1)} %get-tuple-element.68), channel_id=1, source_target_pairs={{0,8},{1,9},{2,10},{3,11},{4,12},{5,13},{6,14},{7,15},{8,0},{9,1},... | collective-permute-start | bytes 491528 | tf_op jit(solution)/shard_map/ppermute | solution.py:295
  51.9 1.3 %forward_dct.2 = (f32[32,640]{1,0:T(8,128)S(1)}, f32[128,640]{1,0:T(8,128)S(1)}, f32[16,5120]{1,0:T(8,128)S(1)}) custom-call(f32[2,8,1280]{2,1,0:T(8,128)S(1)} %get-tuple-element.77.refs_0_, f32[2,8,1280]{2,1,0:T(8,128)S(1)} %get-tuple-element.75.refs_1_, f32[2,8,2560]{2,1,0:T(8,128)S(1)} %get-tuple-element.73.refs_2_, ...), custom_call_target="tpu_custom_call" | custom-call | tf_op jit(solution)/shard_map/forward_dct/pallas_call | solution.py:157
  55.0 1.8 %collective-permute-start.23 = (f32[32,640]{1,0:T(8,128)S(1)}, f32[32,640]{1,0:T(8,128)S(1)}, u32[]{:S(2)}, u32[]{:S(2)}) collective-permute-start(f32[32,640]{1,0:T(8,128)S(1)} %get-tuple-element.55), channel_id=1, source_target_pairs={{0,16},{16,0},{32,48},{48,32},{64,80},{80,64},{96,112},{112,96},{1... | collective-permute-start | bytes 245768 | tf_op jit(solution)/shard_map/ppermute | solution.py:338
  57.3 1.3 %forward_dct.3 = (f32[32,640]{1,0:T(8,128)S(1)}, f32[128,640]{1,0:T(8,128)S(1)}, f32[16,5120]{1,0:T(8,128)S(1)}) custom-call(f32[2,8,2560]{2,1,0:T(8,128)S(1)} %get-tuple-element.71.refs_0_, f32[2,8,2560]{2,1,0:T(8,128)S(1)} %get-tuple-element.69.refs_1_, f32[2,8,2560]{2,1,0:T(8,128)S(1)} %collective-permute-done.15.refs_2_, ...), custom_call_target="tpu_custom_call" | custom-call | tf_op jit(solution)/shard_map/forward_dct/pallas_call | solution.py:157
  59.3 1.0 %collective-permute-start.19 = (f32[32,640]{1,0:T(8,128)S(1)}, f32[32,640]{1,0:T(8,128)S(1)}, u32[]{:S(2)}, u32[]{:S(2)}) collective-permute-start(f32[32,640]{1,0:T(8,128)S(1)} %get-tuple-element.54), channel_id=1, source_target_pairs={{0,144},{16,128},{32,176},{48,160},{64,208},{80,192},{96,240},{112... | collective-permute-start | bytes 245768 | tf_op jit(solution)/shard_map/ppermute | solution.py:338
  60.2 1.9 %collective-permute-start.17 = (f32[32,640]{1,0:T(8,128)S(1)}, f32[32,640]{1,0:T(8,128)S(1)}, u32[]{:S(2)}, u32[]{:S(2)}) collective-permute-start(f32[32,640]{1,0:T(8,128)S(1)} %get-tuple-element.54), channel_id=1, source_target_pairs={{0,16},{16,0},{32,48},{48,32},{64,80},{80,64},{96,112},{112,96},{1... | collective-permute-start | bytes 245768 | tf_op jit(solution)/shard_map/ppermute | solution.py:338
  62.2 5.9 %collective-permute-start.26 = (f32[32,640]{1,0:T(8,128)S(1)}, f32[32,640]{1,0:T(8,128)S(1)}, u32[]{:S(2)}, u32[]{:S(2)}) collective-permute-start(f32[32,640]{1,0:T(8,128)S(1)} %add_add_fusion.s0_ref), channel_id=1, source_target_pairs={{0,80},{16,64},{32,112},{48,96},{64,16},{80,0},{96,48},{112,32},{1... | collective-permute-start | bytes 245768 | tf_op jit(solution)/shard_map/ppermute | solution.py:340
  68.1 1.0 %collective-permute-start.27 = (f32[32,640]{1,0:T(8,128)S(1)}, f32[32,640]{1,0:T(8,128)S(1)}, u32[]{:S(2)}, u32[]{:S(2)}) collective-permute-start(f32[32,640]{1,0:T(8,128)S(1)} %add_add_fusion.s0_ref), channel_id=1, source_target_pairs={{0,112},{16,32},{32,16},{48,64},{64,48},{80,96},{96,80},{112,0},{1... | collective-permute-start | bytes 245768 | tf_op jit(solution)/shard_map/ppermute | solution.py:340
  69.6 4.2 %collective-permute-start.20 = (f32[32,640]{1,0:T(8,128)S(1)}, f32[32,640]{1,0:T(8,128)S(1)}, u32[]{:S(2)}, u32[]{:S(2)}) collective-permute-start(f32[32,640]{1,0:T(8,128)S(1)} %add_add_fusion.1.s0_ref), channel_id=1, source_target_pairs={{0,80},{16,64},{32,112},{48,96},{64,16},{80,0},{96,48},{112,32},{1... | collective-permute-start | bytes 245768 | tf_op jit(solution)/shard_map/ppermute | solution.py:340
  73.8 1.0 %collective-permute-start.21 = (f32[32,640]{1,0:T(8,128)S(1)}, f32[32,640]{1,0:T(8,128)S(1)}, u32[]{:S(2)}, u32[]{:S(2)}) collective-permute-start(f32[32,640]{1,0:T(8,128)S(1)} %add_add_fusion.1.s0_ref), channel_id=1, source_target_pairs={{0,112},{16,32},{32,16},{48,64},{64,48},{80,96},{96,80},{112,0},{1... | collective-permute-start | bytes 245768 | tf_op jit(solution)/shard_map/ppermute | solution.py:340
  75.3 1.6 %residual.1 = f32[4,8,5120]{2,1,0:T(8,128)} custom-call(f32[16,5120]{1,0:T(8,128)S(1)} %get-tuple-element.41.refs_0_, f32[16,5120]{1,0:T(8,128)S(1)} %get-tuple-element.51.refs_1_, f32[128,640]{1,0:T(8,128)S(1)} %get-tuple-element.52.refs_2_, f32[128,640]{1,0:T(8,128)S(1)} %get-tuple-element.53.refs_3_, f32[128,128]{1,0:T(8,128)S(1)} %copy-done.2), custom_call_target="tpu_custom_call" | custom-call | tf_op jit(solution)/shard_map/residual/pallas_call | solution.py:189
  76.9 1.6 %step_params.2.rest_0_ = f32[4,8,5120]{2,1,0:T(8,128)} custom-call(f32[4,8,5120]{2,1,0:T(8,128)S(1)} %copy-done.1, f32[32,640]{1,0:T(8,128)S(1)} %add_add_fusion.s0_ref, f32[32,640]{1,0:T(8,128)S(1)} %collective-permute-done.26.s1_ref, f32[32,640]{1,0:T(8,128)S(1)} %collective-permute-done.27.s2_ref, f32[32,640]{1,0:T(8,128)S(1)} %collective-permute-done.28.s3_ref, ...), custom_call_target="tpu_custom_call" | custom-call | tf_op jit(solution)/shard_map/step_params/pallas_call | solution.py:241
  78.6 1.1 %collective-permute-done.21.s2_ref = f32[32,640]{1,0:T(8,128)S(1)} collective-permute-done((f32[32,640]{1,0:T(8,128)S(1)}, f32[32,640]{1,0:T(8,128)S(1)}, u32[]{:S(2)}, u32[]{:S(2)}) %collective-permute-start.21) | collective-permute-done | bytes 81952 | tf_op jit(solution)/shard_map/ppermute | solution.py:340
  79.7 1.8 %collective-permute-done.22.s3_ref = f32[32,640]{1,0:T(8,128)S(1)} collective-permute-done((f32[32,640]{1,0:T(8,128)S(1)}, f32[32,640]{1,0:T(8,128)S(1)}, u32[]{:S(2)}, u32[]{:S(2)}) %collective-permute-start.22) | collective-permute-done | bytes 81952 | tf_op jit(solution)/shard_map/ppermute | solution.py:340
  81.4 1.6 %step_params.3 = f32[4,8,5120]{2,1,0:T(8,128)} custom-call(f32[4,8,5120]{2,1,0:T(8,128)S(1)} %copy-done.1, f32[32,640]{1,0:T(8,128)S(1)} %add_add_fusion.1.s0_ref, f32[32,640]{1,0:T(8,128)S(1)} %collective-permute-done.20.s1_ref, f32[32,640]{1,0:T(8,128)S(1)} %collective-permute-done.21.s2_ref, ...), custom_call_target="tpu_custom_call", output_to_operand_aliasing={{}: (7, {})} | custom-call | tf_op jit(solution)/shard_map/step_params/pallas_call | solution.py:241
  (72 shorter events, 9.2 us)
Async XLA Ops:
  2.6 5.0 %collective-permute-start = (f32[8,2,8,5120]{3,2,1,0:T(8,128)S(1)}, f32[8,2,8,5120]{3,2,1,0:T(8,128)S(1)}, u32[]{:S(2)}, u32[]{:S(2)}) collective-permute-start(f32[8,2,8,5120]{3,2,1,0:T(8,128)S(1)} %get-tuple-element.30), channel_id=1, source_target_pairs={{0,1},{1,0},{2,3},{3,2},{4,5},{5,4},{6,7},{7,6},{8,9},{9,8},{10,11... | collective-permute-start | bytes 7864328 | tf_op jit(solution)/shard_map/ppermute | solution.py:319
  4.7 10.6 %collective-permute-start.10 = (f32[8,2,8,5120]{3,2,1,0:T(8,128)S(1)}, f32[8,2,8,5120]{3,2,1,0:T(8,128)S(1)}, u32[]{:S(2)}, u32[]{:S(2)}) collective-permute-start(f32[8,2,8,5120]{3,2,1,0:T(8,128)S(1)} %get-tuple-element.43), channel_id=1, source_target_pairs={{0,1},{1,0},{2,3},{3,2},{4,5},{5,4},{6,7},{7,6},{8,9},{9,8},{10,11... | collective-permute-start | bytes 7864328 | tf_op jit(solution)/shard_map/ppermute | solution.py:319
  7.9 11.4 %collective-permute-start.1 = (f32[2,2,2,8,1280]{4,3,2,1,0:T(8,128)S(1)}, f32[2,2,2,8,1280]{4,3,2,1,0:T(8,128)S(1)}, u32[]{:S(2)}, u32[]{:S(2)}) collective-permute-start(f32[2,2,2,8,1280]{4,3,2,1,0:T(8,128)S(1)} %bitcast.99), channel_id=1, source_target_pairs={{0,8},{1,9},{2,10},{3,11},{4,12},{5,13},{6,14},{7,15},{8,0},{9,1},... | collective-permute-start | bytes 983048 | tf_op jit(solution)/shard_map/ppermute | solution.py:295
  11.3 10.7 %collective-permute-start.2 = (f32[2,2,2,8,1280]{4,3,2,0,1:T(8,128)S(1)}, f32[2,2,2,8,1280]{4,3,2,0,1:T(8,128)S(1)}, u32[]{:S(2)}, u32[]{:S(2)}) collective-permute-start(f32[2,2,2,8,1280]{4,3,2,0,1:T(8,128)S(1)} %bitcast.100), channel_id=1, source_target_pairs={{0,2},{1,3},{2,0},{3,1},{4,6},{5,7},{6,4},{7,5},{8,10},{9,11},{10,... | collective-permute-start | bytes 983048 | tf_op jit(solution)/shard_map/ppermute | solution.py:295
  13.1 17.5 %collective-permute-start.3 = (f32[2,2,2,8,2560]{4,3,2,1,0:T(8,128)S(1)}, f32[2,2,2,8,2560]{4,3,2,1,0:T(8,128)S(1)}, u32[]{:S(2)}, u32[]{:S(2)}) collective-permute-start(f32[2,2,2,8,2560]{4,3,2,1,0:T(8,128)S(1)} %slice_bitcast_fusion.1), channel_id=1, source_target_pairs={{0,6},{1,7},{2,4},{3,5},{4,2},{5,3},{6,0},{7,1},{8,14},{9,15},{10,... | collective-permute-start | bytes 1966088 | tf_op jit(solution)/shard_map/ppermute | solution.py:295
  15.7 17.9 %collective-permute-start.11 = (f32[2,2,2,8,2560]{4,3,2,1,0:T(8,128)S(1)}, f32[2,2,2,8,2560]{4,3,2,1,0:T(8,128)S(1)}, u32[]{:S(2)}, u32[]{:S(2)}) collective-permute-start(f32[2,2,2,8,2560]{4,3,2,1,0:T(8,128)S(1)} %bitcast.96), channel_id=1, source_target_pairs={{0,8},{1,9},{2,10},{3,11},{4,12},{5,13},{6,14},{7,15},{8,0},{9,1},... | collective-permute-start | bytes 1966088 | tf_op jit(solution)/shard_map/ppermute | solution.py:295
  16.2 19.7 %collective-permute-start.12 = (f32[2,2,2,8,2560]{4,3,2,0,1:T(8,128)S(1)}, f32[2,2,2,8,2560]{4,3,2,0,1:T(8,128)S(1)}, u32[]{:S(2)}, u32[]{:S(2)}) collective-permute-start(f32[2,2,2,8,2560]{4,3,2,0,1:T(8,128)S(1)} %bitcast.97), channel_id=1, source_target_pairs={{0,2},{1,3},{2,0},{3,1},{4,6},{5,7},{6,4},{7,5},{8,10},{9,11},{10,... | collective-permute-start | bytes 1966088 | tf_op jit(solution)/shard_map/ppermute | solution.py:295
  30.6 9.4 %collective-permute-start.4 = (f32[2,2,8,1280]{3,2,1,0:T(8,128)S(1)}, f32[2,2,8,1280]{3,2,1,0:T(8,128)S(1)}, u32[]{:S(2)}, u32[]{:S(2)}) collective-permute-start(f32[2,2,8,1280]{3,2,1,0:T(8,128)S(1)} %slice_bitcast_fusion.16), channel_id=1, source_target_pairs={{0,2},{1,3},{2,0},{3,1},{4,6},{5,7},{6,4},{7,5},{8,10},{9,11},{10,... | collective-permute-start | bytes 491528 | tf_op jit(solution)/shard_map/ppermute | solution.py:295
  30.8 9.2 %collective-permute-start.5 = (f32[2,2,8,1280]{3,2,1,0:T(8,128)S(1)}, f32[2,2,8,1280]{3,2,1,0:T(8,128)S(1)}, u32[]{:S(2)}, u32[]{:S(2)}) collective-permute-start(f32[2,2,8,1280]{3,2,1,0:T(8,128)S(1)} %slice_bitcast_fusion.15), channel_id=1, source_target_pairs={{0,6},{1,7},{2,4},{3,5},{4,2},{5,3},{6,0},{7,1},{8,14},{9,15},{10,... | collective-permute-start | bytes 491528 | tf_op jit(solution)/shard_map/ppermute | solution.py:295
  33.1 9.6 %collective-permute-start.6 = (f32[2,2,8,2560]{3,2,1,0:T(8,128)S(1)}, f32[2,2,8,2560]{3,2,1,0:T(8,128)S(1)}, u32[]{:S(2)}, u32[]{:S(2)}) collective-permute-start(f32[2,2,8,2560]{3,2,1,0:T(8,128)S(1)} %slice_bitcast_fusion.7), channel_id=1, source_target_pairs={{0,8},{1,9},{2,10},{3,11},{4,12},{5,13},{6,14},{7,15},{8,0},{9,1},... | collective-permute-start | bytes 983048 | tf_op jit(solution)/shard_map/ppermute | solution.py:295
  36.1 10.7 %collective-permute-start.13 = (f32[2,2,8,2560]{3,2,1,0:T(8,128)S(1)}, f32[2,2,8,2560]{3,2,1,0:T(8,128)S(1)}, u32[]{:S(2)}, u32[]{:S(2)}) collective-permute-start(f32[2,2,8,2560]{3,2,1,0:T(8,128)S(1)} %slice_bitcast_fusion.4), channel_id=1, source_target_pairs={{0,2},{1,3},{2,0},{3,1},{4,6},{5,7},{6,4},{7,5},{8,10},{9,11},{10,... | collective-permute-start | bytes 983048 | tf_op jit(solution)/shard_map/ppermute | solution.py:295
  37.8 9.4 %collective-permute-start.14 = (f32[2,2,8,2560]{3,2,1,0:T(8,128)S(1)}, f32[2,2,8,2560]{3,2,1,0:T(8,128)S(1)}, u32[]{:S(2)}, u32[]{:S(2)}) collective-permute-start(f32[2,2,8,2560]{3,2,1,0:T(8,128)S(1)} %slice_bitcast_fusion.3), channel_id=1, source_target_pairs={{0,6},{1,7},{2,4},{3,5},{4,2},{5,3},{6,0},{7,1},{8,14},{9,15},{10,... | collective-permute-start | bytes 983048 | tf_op jit(solution)/shard_map/ppermute | solution.py:295
  42.8 9.0 %collective-permute-start.7 = (f32[2,8,1280]{2,1,0:T(8,128)S(1)}, f32[2,8,1280]{2,1,0:T(8,128)S(1)}, u32[]{:S(2)}, u32[]{:S(2)}) collective-permute-start(f32[2,8,1280]{2,1,0:T(8,128)S(1)} %get-tuple-element.76), channel_id=1, source_target_pairs={{0,6},{1,7},{2,4},{3,5},{4,2},{5,3},{6,0},{7,1},{8,14},{9,15},{10,... | collective-permute-start | bytes 245768 | tf_op jit(solution)/shard_map/ppermute | solution.py:295
  44.1 7.7 %collective-permute-start.8 = (f32[2,8,1280]{2,1,0:T(8,128)S(1)}, f32[2,8,1280]{2,1,0:T(8,128)S(1)}, u32[]{:S(2)}, u32[]{:S(2)}) collective-permute-start(f32[2,8,1280]{2,1,0:T(8,128)S(1)} %get-tuple-element.74), channel_id=1, source_target_pairs={{0,8},{1,9},{2,10},{3,11},{4,12},{5,13},{6,14},{7,15},{8,0},{9,1},... | collective-permute-start | bytes 245768 | tf_op jit(solution)/shard_map/ppermute | solution.py:295
  46.6 5.3 %copy-start = (f32[1,4,8,5120]{3,2,1,0:T(8,128)S(1)}, f32[1,4,8,5120]{3,2,1,0:T(8,128)}, u32[]{:S(2)}) copy-start(f32[1,4,8,5120]{3,2,1,0:T(8,128)} %param.6) | copy-start | bytes 1966084
  46.6 5.3 %copy-start.2 = (f32[128,128]{1,0:T(8,128)S(1)}, f32[128,128]{1,0:T(8,128)}, u32[]{:S(2)}) copy-start(f32[128,128]{1,0:T(8,128)} %constant.2.clone.refs_8_.refs_6_.refs_4_.table_ref) | copy-start | bytes 196612
  46.6 5.3 %collective-permute-start.9 = (f32[2,8,2560]{2,1,0:T(8,128)S(1)}, f32[2,8,2560]{2,1,0:T(8,128)S(1)}, u32[]{:S(2)}, u32[]{:S(2)}) collective-permute-start(f32[2,8,2560]{2,1,0:T(8,128)S(1)} %get-tuple-element.72), channel_id=1, source_target_pairs={{0,2},{1,3},{2,0},{3,1},{4,6},{5,7},{6,4},{7,5},{8,10},{9,11},{10,... | collective-permute-start | bytes 491528 | tf_op jit(solution)/shard_map/ppermute | solution.py:295
  47.3 9.5 %collective-permute-start.15 = (f32[2,8,2560]{2,1,0:T(8,128)S(1)}, f32[2,8,2560]{2,1,0:T(8,128)S(1)}, u32[]{:S(2)}, u32[]{:S(2)}) collective-permute-start(f32[2,8,2560]{2,1,0:T(8,128)S(1)} %get-tuple-element.70), channel_id=1, source_target_pairs={{0,6},{1,7},{2,4},{3,5},{4,2},{5,3},{6,0},{7,1},{8,14},{9,15},{10,... | collective-permute-start | bytes 491528 | tf_op jit(solution)/shard_map/ppermute | solution.py:295
  49.5 7.8 %collective-permute-start.16 = (f32[2,8,2560]{2,1,0:T(8,128)S(1)}, f32[2,8,2560]{2,1,0:T(8,128)S(1)}, u32[]{:S(2)}, u32[]{:S(2)}) collective-permute-start(f32[2,8,2560]{2,1,0:T(8,128)S(1)} %get-tuple-element.68), channel_id=1, source_target_pairs={{0,8},{1,9},{2,10},{3,11},{4,12},{5,13},{6,14},{7,15},{8,0},{9,1},... | collective-permute-start | bytes 491528 | tf_op jit(solution)/shard_map/ppermute | solution.py:295
  53.2 7.0 %collective-permute-start.24 = (f32[32,640]{1,0:T(8,128)S(1)}, f32[32,640]{1,0:T(8,128)S(1)}, u32[]{:S(2)}, u32[]{:S(2)}) collective-permute-start(f32[32,640]{1,0:T(8,128)S(1)} %get-tuple-element.55), channel_id=1, source_target_pairs={{0,128},{16,144},{32,160},{48,176},{64,192},{80,208},{96,224},{112... | collective-permute-start | bytes 245768 | tf_op jit(solution)/shard_map/ppermute | solution.py:338
  54.1 8.1 %collective-permute-start.25 = (f32[32,640]{1,0:T(8,128)S(1)}, f32[32,640]{1,0:T(8,128)S(1)}, u32[]{:S(2)}, u32[]{:S(2)}) collective-permute-start(f32[32,640]{1,0:T(8,128)S(1)} %get-tuple-element.55), channel_id=1, source_target_pairs={{0,144},{16,128},{32,176},{48,160},{64,208},{80,192},{96,240},{112... | collective-permute-start | bytes 245768 | tf_op jit(solution)/shard_map/ppermute | solution.py:338
  55.0 7.2 %collective-permute-start.23 = (f32[32,640]{1,0:T(8,128)S(1)}, f32[32,640]{1,0:T(8,128)S(1)}, u32[]{:S(2)}, u32[]{:S(2)}) collective-permute-start(f32[32,640]{1,0:T(8,128)S(1)} %get-tuple-element.55), channel_id=1, source_target_pairs={{0,16},{16,0},{32,48},{48,32},{64,80},{80,64},{96,112},{112,96},{1... | collective-permute-start | bytes 245768 | tf_op jit(solution)/shard_map/ppermute | solution.py:338
  58.6 10.6 %collective-permute-start.18 = (f32[32,640]{1,0:T(8,128)S(1)}, f32[32,640]{1,0:T(8,128)S(1)}, u32[]{:S(2)}, u32[]{:S(2)}) collective-permute-start(f32[32,640]{1,0:T(8,128)S(1)} %get-tuple-element.54), channel_id=1, source_target_pairs={{0,128},{16,144},{32,160},{48,176},{64,192},{80,208},{96,224},{112... | collective-permute-start | bytes 245768 | tf_op jit(solution)/shard_map/ppermute | solution.py:338
  59.3 10.3 %collective-permute-start.19 = (f32[32,640]{1,0:T(8,128)S(1)}, f32[32,640]{1,0:T(8,128)S(1)}, u32[]{:S(2)}, u32[]{:S(2)}) collective-permute-start(f32[32,640]{1,0:T(8,128)S(1)} %get-tuple-element.54), channel_id=1, source_target_pairs={{0,144},{16,128},{32,176},{48,160},{64,208},{80,192},{96,240},{112... | collective-permute-start | bytes 245768 | tf_op jit(solution)/shard_map/ppermute | solution.py:338
  60.2 9.4 %collective-permute-start.17 = (f32[32,640]{1,0:T(8,128)S(1)}, f32[32,640]{1,0:T(8,128)S(1)}, u32[]{:S(2)}, u32[]{:S(2)}) collective-permute-start(f32[32,640]{1,0:T(8,128)S(1)} %get-tuple-element.54), channel_id=1, source_target_pairs={{0,16},{16,0},{32,48},{48,32},{64,80},{80,64},{96,112},{112,96},{1... | collective-permute-start | bytes 245768 | tf_op jit(solution)/shard_map/ppermute | solution.py:338
  62.2 14.8 %copy-start.1 = (f32[4,8,5120]{2,1,0:T(8,128)S(1)}, f32[4,8,5120]{2,1,0:T(8,128)}, u32[]{:S(2)}) copy-start(f32[4,8,5120]{2,1,0:T(8,128)} %params_ref.3) | copy-start | bytes 1966084
  62.2 12.7 %collective-permute-start.26 = (f32[32,640]{1,0:T(8,128)S(1)}, f32[32,640]{1,0:T(8,128)S(1)}, u32[]{:S(2)}, u32[]{:S(2)}) collective-permute-start(f32[32,640]{1,0:T(8,128)S(1)} %add_add_fusion.s0_ref), channel_id=1, source_target_pairs={{0,80},{16,64},{32,112},{48,96},{64,16},{80,0},{96,48},{112,32},{1... | collective-permute-start | bytes 245768 | tf_op jit(solution)/shard_map/ppermute | solution.py:340
  68.1 8.8 %collective-permute-start.27 = (f32[32,640]{1,0:T(8,128)S(1)}, f32[32,640]{1,0:T(8,128)S(1)}, u32[]{:S(2)}, u32[]{:S(2)}) collective-permute-start(f32[32,640]{1,0:T(8,128)S(1)} %add_add_fusion.s0_ref), channel_id=1, source_target_pairs={{0,112},{16,32},{32,16},{48,64},{64,48},{80,96},{96,80},{112,0},{1... | collective-permute-start | bytes 245768 | tf_op jit(solution)/shard_map/ppermute | solution.py:340
  69.2 7.8 %collective-permute-start.28 = (f32[32,640]{1,0:T(8,128)S(1)}, f32[32,640]{1,0:T(8,128)S(1)}, u32[]{:S(2)}, u32[]{:S(2)}) collective-permute-start(f32[32,640]{1,0:T(8,128)S(1)} %add_add_fusion.s0_ref), channel_id=1, source_target_pairs={{0,96},{16,48},{32,0},{48,80},{64,32},{80,112},{96,64},{112,16},{1... | collective-permute-start | bytes 245768 | tf_op jit(solution)/shard_map/ppermute | solution.py:340
  69.6 8.9 %collective-permute-start.20 = (f32[32,640]{1,0:T(8,128)S(1)}, f32[32,640]{1,0:T(8,128)S(1)}, u32[]{:S(2)}, u32[]{:S(2)}) collective-permute-start(f32[32,640]{1,0:T(8,128)S(1)} %add_add_fusion.1.s0_ref), channel_id=1, source_target_pairs={{0,80},{16,64},{32,112},{48,96},{64,16},{80,0},{96,48},{112,32},{1... | collective-permute-start | bytes 245768 | tf_op jit(solution)/shard_map/ppermute | solution.py:340
  73.8 5.8 %collective-permute-start.21 = (f32[32,640]{1,0:T(8,128)S(1)}, f32[32,640]{1,0:T(8,128)S(1)}, u32[]{:S(2)}, u32[]{:S(2)}) collective-permute-start(f32[32,640]{1,0:T(8,128)S(1)} %add_add_fusion.1.s0_ref), channel_id=1, source_target_pairs={{0,112},{16,32},{32,16},{48,64},{64,48},{80,96},{96,80},{112,0},{1... | collective-permute-start | bytes 245768 | tf_op jit(solution)/shard_map/ppermute | solution.py:340
  74.9 6.6 %collective-permute-start.22 = (f32[32,640]{1,0:T(8,128)S(1)}, f32[32,640]{1,0:T(8,128)S(1)}, u32[]{:S(2)}, u32[]{:S(2)}) collective-permute-start(f32[32,640]{1,0:T(8,128)S(1)} %add_add_fusion.1.s0_ref), channel_id=1, source_target_pairs={{0,96},{16,48},{32,0},{48,80},{64,32},{80,112},{96,64},{112,16},{1... | collective-permute-start | bytes 245768 | tf_op jit(solution)/shard_map/ppermute | solution.py:340
  (1 other events, 4.7 us)

commit v4 on v3

--- a/solution.py
+++ b/solution.py
@@ -63,24 +63,24 @@
         core, x, y = me % 2, (me // 2) % 4, me // 8
         across = {(0, 0): x, (0, 1): 3 - x, (1, 0): x + 1 - 2 * (x % 2), (1, 1): (x + 2) % 4}
 
-        def fetch(side, i):
+        def fetch(i):
             dy, a, b = cube[i]
-            chip = (1 - y if dy else y) * 4 + across[a, b]
-            start = (chip * 2 + (core if side else 1 - core)) * 8
+            start = ((1 - y if dy else y) * 4 + across[a, b]) * 16
             return pltpu.make_async_copy(
-                grads_ref.at[pl.ds(first, count), pl.ds(pl.multiple_of(start, 8), 8)],
-                held.at[side, i],
-                sems.at[side, i],
+                grads_ref.at[pl.ds(first, count), pl.ds(pl.multiple_of(start, 16), 16)],
+                held.at[i],
+                sems.at[i],
             )
 
-        for side in range(2):
-            for i in range(8):
-                fetch(side, i).start()
-        for side, out_ref in enumerate((other_ref, own_ref)):
-            for i in range(8):
-                fetch(side, i).wait()
-                for layer in range(count):
-                    out_ref[i, layer] = held[side, i, layer].astype(jnp.float32)
+        for i in range(8):
+            fetch(i).start()
+        is_low = core == 0
+        for i in range(8):
+            fetch(i).wait()
+            for layer in range(count):
+                both = held[i, layer].astype(jnp.float32)
+                own_ref[i, layer] = jnp.where(is_low, both[:8], both[8:])
+                other_ref[i, layer] = jnp.where(is_low, both[8:], both[:8])
 
     out = jax.ShapeDtypeStruct((8, count, 8, width), jnp.float32)
     return pl.pallas_call(
@@ -88,8 +88,8 @@
         in_specs=[pl.BlockSpec(memory_space=pltpu.HBM)],
         out_shape=[out, out],
         scratch_shapes=[
-            pltpu.VMEM((2, 8, count, 8, width), grads.dtype),
-            pltpu.SemaphoreType.DMA((2, 8)),
+            pltpu.VMEM((8, count, 16, width), grads.dtype),
+            pltpu.SemaphoreType.DMA((8,)),
         ],
         compiler_params=pltpu.CompilerParams(vmem_limit_bytes=VMEM_LIMIT),
         name="split_cores",

time: 83.4 us -> 83.2 us (level)
  no operation moved by 1% of the time
where the time goes in v4:
time: 83.2 us; the launch traced here: 83.1 us
  starting transfers between devices  43.4 us (52%)
  waiting for transfers between devices  25.2 us (30%)
  Pallas kernels  11.5 us (14%)
  other arithmetic  1.25 us (2%)
  between operations  1.11 us (1%)
    ppermute x15, starting transfers between devices, halve(): recvs.append(lax.ppermute(send, 'fsdp', HALVES[order[step]]))  22.5 us
    ppermute x15, waiting for transfers between devices, halve(): recvs.append(lax.ppermute(send, 'fsdp', HALVES[order[step]]))  19.8 us
    ppermute x6, starting transfers between devices, shards(): far = [lax.ppermute(four, 'rep', p) for p in (OPPOSITE, BESIDE, BEYOND)]  13.1 us
    ppermute x6, starting transfers between devices, shards(): near = [lax.ppermute(values, 'rep', rep_pairs(m)) for m in (1, 8, 9)]  7.15 us
    pallas_call x2, Pallas kernels, split_cores(): pl.pallas_call(kernel, in_specs=[pl.BlockSpec(memory_space=pltpu.HBM)], o...  3.64 us
    pallas_call x2, Pallas kernels, step_params(): pl.pallas_call(kernel, in_specs=[vmem] * 7 + [anywhere] * len(extra), out...  3.21 us
    ppermute x6, waiting for transfers between devices, shards(): far = [lax.ppermute(four, 'rep', p) for p in (OPPOSITE, BESIDE, BEYOND)]  2.87 us
    pallas_call x2, Pallas kernels, forward(): pl.pallas_call(kernel, out_shape=shapes, compiler_params=pltpu.CompilerPa...  2.54 us
  transfers between devices with their start and end apart: 29, of which 11 were waited for; matrix products, arithmetic and copies ran while one was open for 2% of the time, Pallas kernels for 10%

profile of v4, /device:TPU:32, one launch (start us, length us, event | category | flops | bytes accessed | tf_op | source)
XLA Modules:
  0.0 83.1 jit_solution(13931748756870466068)
XLA Ops:
  0.6 1.8 %split_cores.2 = (f32[8,2,8,5120]{3,2,1,0:T(8,128)S(1)}, f32[8,2,8,5120]{3,2,1,0:T(8,128)S(1)}) custom-call(bf16[4,128,5120]{2,1,0:T(8,128)(2,1)} %bitcast.88), custom_call_target="tpu_custom_call" | custom-call | tf_op jit(solution)/shard_map/split_cores/pallas_call | solution.py:86
  2.6 1.8 %split_cores.3 = (f32[8,2,8,5120]{3,2,1,0:T(8,128)S(1)}, f32[8,2,8,5120]{3,2,1,0:T(8,128)S(1)}) custom-call(bf16[4,128,5120]{2,1,0:T(8,128)(2,1)} %bitcast.89), custom_call_target="tpu_custom_call" | custom-call | tf_op jit(solution)/shard_map/split_cores/pallas_call | solution.py:86
  4.9 2.5 %collective-permute-done = f32[8,2,8,5120]{3,2,1,0:T(8,128)S(1)} collective-permute-done((f32[8,2,8,5120]{3,2,1,0:T(8,128)S(1)}, f32[8,2,8,5120]{3,2,1,0:T(8,128)S(1)}, u32[]{:S(2)}, u32[]{:S(2)}) %collective-permute-start) | collective-permute-done | bytes 2621472 | tf_op jit(solution)/shard_map/ppermute | solution.py:319
  7.7 3.3 %collective-permute-start.1 = (f32[2,2,2,8,1280]{4,3,2,1,0:T(8,128)S(1)}, f32[2,2,2,8,1280]{4,3,2,1,0:T(8,128)S(1)}, u32[]{:S(2)}, u32[]{:S(2)}) collective-permute-start(f32[2,2,2,8,1280]{4,3,2,1,0:T(8,128)S(1)} %bitcast.99), channel_id=1, source_target_pairs={{0,8},{1,9},{2,10},{3,11},{4,12},{5,13},{6,14},{7,15},{8,0},{9,1},... | collective-permute-start | bytes 983048 | tf_op jit(solution)/shard_map/ppermute | solution.py:295
  11.1 1.6 %collective-permute-start.2 = (f32[2,2,2,8,1280]{4,3,2,0,1:T(8,128)S(1)}, f32[2,2,2,8,1280]{4,3,2,0,1:T(8,128)S(1)}, u32[]{:S(2)}, u32[]{:S(2)}) collective-permute-start(f32[2,2,2,8,1280]{4,3,2,0,1:T(8,128)S(1)} %bitcast.100), channel_id=1, source_target_pairs={{0,2},{1,3},{2,0},{3,1},{4,6},{5,7},{6,4},{7,5},{8,10},{9,11},{10,... | collective-permute-start | bytes 983048 | tf_op jit(solution)/shard_map/ppermute | solution.py:295
  12.9 2.2 %collective-permute-start.3 = (f32[2,2,2,8,2560]{4,3,2,1,0:T(8,128)S(1)}, f32[2,2,2,8,2560]{4,3,2,1,0:T(8,128)S(1)}, u32[]{:S(2)}, u32[]{:S(2)}) collective-permute-start(f32[2,2,2,8,2560]{4,3,2,1,0:T(8,128)S(1)} %slice_bitcast_fusion.1), channel_id=1, source_target_pairs={{0,6},{1,7},{2,4},{3,5},{4,2},{5,3},{6,0},{7,1},{8,14},{9,15},{10,... | collective-permute-start | bytes 1966088 | tf_op jit(solution)/shard_map/ppermute | solution.py:295
  16.8 2.4 %collective-permute-done.1 = f32[2,2,2,8,1280]{4,3,2,1,0:T(8,128)S(1)} collective-permute-done((f32[2,2,2,8,1280]{4,3,2,1,0:T(8,128)S(1)}, f32[2,2,2,8,1280]{4,3,2,1,0:T(8,128)S(1)}, u32[]{:S(2)}, u32[]{:S(2)}) %collective-permute-start.1) | collective-permute-done | bytes 327712 | tf_op jit(solution)/shard_map/ppermute | solution.py:295
  19.1 2.7 %collective-permute-done.2 = f32[2,2,2,8,1280]{4,3,2,0,1:T(8,128)S(1)} collective-permute-done((f32[2,2,2,8,1280]{4,3,2,0,1:T(8,128)S(1)}, f32[2,2,2,8,1280]{4,3,2,0,1:T(8,128)S(1)}, u32[]{:S(2)}, u32[]{:S(2)}) %collective-permute-start.2) | collective-permute-done | bytes 327712 | tf_op jit(solution)/shard_map/ppermute | solution.py:295
  21.8 8.6 %collective-permute-done.3 = f32[2,2,2,8,2560]{4,3,2,1,0:T(8,128)S(1)} collective-permute-done((f32[2,2,2,8,2560]{4,3,2,1,0:T(8,128)S(1)}, f32[2,2,2,8,2560]{4,3,2,1,0:T(8,128)S(1)}, u32[]{:S(2)}, u32[]{:S(2)}) %collective-permute-start.3) | collective-permute-done | bytes 655392 | tf_op jit(solution)/shard_map/ppermute | solution.py:295
  30.6 2.2 %collective-permute-start.5 = (f32[2,2,8,1280]{3,2,1,0:T(8,128)S(1)}, f32[2,2,8,1280]{3,2,1,0:T(8,128)S(1)}, u32[]{:S(2)}, u32[]{:S(2)}) collective-permute-start(f32[2,2,8,1280]{3,2,1,0:T(8,128)S(1)} %slice_bitcast_fusion.15), channel_id=1, source_target_pairs={{0,6},{1,7},{2,4},{3,5},{4,2},{5,3},{6,0},{7,1},{8,14},{9,15},{10,... | collective-permute-start | bytes 491528 | tf_op jit(solution)/shard_map/ppermute | solution.py:295
  33.4 2.5 %collective-permute-done.12 = f32[2,2,2,8,2560]{4,3,2,0,1:T(8,128)S(1)} collective-permute-done((f32[2,2,2,8,2560]{4,3,2,0,1:T(8,128)S(1)}, f32[2,2,2,8,2560]{4,3,2,0,1:T(8,128)S(1)}, u32[]{:S(2)}, u32[]{:S(2)}) %collective-permute-start.12) | collective-permute-done | bytes 655392 | tf_op jit(solution)/shard_map/ppermute | solution.py:295
  36.0 1.6 %collective-permute-start.13 = (f32[2,2,8,2560]{3,2,1,0:T(8,128)S(1)}, f32[2,2,8,2560]{3,2,1,0:T(8,128)S(1)}, u32[]{:S(2)}, u32[]{:S(2)}) collective-permute-start(f32[2,2,8,2560]{3,2,1,0:T(8,128)S(1)} %slice_bitcast_fusion.4), channel_id=1, source_target_pairs={{0,2},{1,3},{2,0},{3,1},{4,6},{5,7},{6,4},{7,5},{8,10},{9,11},{10,... | collective-permute-start | bytes 983048 | tf_op jit(solution)/shard_map/ppermute | solution.py:295
  37.7 2.2 %collective-permute-start.14 = (f32[2,2,8,2560]{3,2,1,0:T(8,128)S(1)}, f32[2,2,8,2560]{3,2,1,0:T(8,128)S(1)}, u32[]{:S(2)}, u32[]{:S(2)}) collective-permute-start(f32[2,2,8,2560]{3,2,1,0:T(8,128)S(1)} %slice_bitcast_fusion.3), channel_id=1, source_target_pairs={{0,6},{1,7},{2,4},{3,5},{4,2},{5,3},{6,0},{7,1},{8,14},{9,15},{10,... | collective-permute-start | bytes 983048 | tf_op jit(solution)/shard_map/ppermute | solution.py:295
  39.9 2.7 %collective-permute-done.6 = f32[2,2,8,2560]{3,2,1,0:T(8,128)S(1)} collective-permute-done((f32[2,2,8,2560]{3,2,1,0:T(8,128)S(1)}, f32[2,2,8,2560]{3,2,1,0:T(8,128)S(1)}, u32[]{:S(2)}, u32[]{:S(2)}) %collective-permute-start.6) | collective-permute-done | bytes 327712 | tf_op jit(solution)/shard_map/ppermute | solution.py:295
  42.7 1.2 %collective-permute-start.7 = (f32[2,8,1280]{2,1,0:T(8,128)S(1)}, f32[2,8,1280]{2,1,0:T(8,128)S(1)}, u32[]{:S(2)}, u32[]{:S(2)}) collective-permute-start(f32[2,8,1280]{2,1,0:T(8,128)S(1)} %get-tuple-element.76), channel_id=1, source_target_pairs={{0,6},{1,7},{2,4},{3,5},{4,2},{5,3},{6,0},{7,1},{8,14},{9,15},{10,... | collective-permute-start | bytes 245768 | tf_op jit(solution)/shard_map/ppermute | solution.py:295
  43.9 2.5 %collective-permute-start.8 = (f32[2,8,1280]{2,1,0:T(8,128)S(1)}, f32[2,8,1280]{2,1,0:T(8,128)S(1)}, u32[]{:S(2)}, u32[]{:S(2)}) collective-permute-start(f32[2,8,1280]{2,1,0:T(8,128)S(1)} %get-tuple-element.74), channel_id=1, source_target_pairs={{0,8},{1,9},{2,10},{3,11},{4,12},{5,13},{6,14},{7,15},{8,0},{9,1},... | collective-permute-start | bytes 245768 | tf_op jit(solution)/shard_map/ppermute | solution.py:295
  47.2 2.2 %collective-permute-start.15 = (f32[2,8,2560]{2,1,0:T(8,128)S(1)}, f32[2,8,2560]{2,1,0:T(8,128)S(1)}, u32[]{:S(2)}, u32[]{:S(2)}) collective-permute-start(f32[2,8,2560]{2,1,0:T(8,128)S(1)} %get-tuple-element.70), channel_id=1, source_target_pairs={{0,6},{1,7},{2,4},{3,5},{4,2},{5,3},{6,0},{7,1},{8,14},{9,15},{10,... | collective-permute-start | bytes 491528 | tf_op jit(solution)/shard_map/ppermute | solution.py:295
  49.4 1.8 %collective-permute-start.16 = (f32[2,8,2560]{2,1,0:T(8,128)S(1)}, f32[2,8,2560]{2,1,0:T(8,128)S(1)}, u32[]{:S(2)}, u32[]{:S(2)}) collective-permute-start(f32[2,8,2560]{2,1,0:T(8,128)S(1)} %get-tuple-element.68), channel_id=1, source_target_pairs={{0,8},{1,9},{2,10},{3,11},{4,12},{5,13},{6,14},{7,15},{8,0},{9,1},... | collective-permute-start | bytes 491528 | tf_op jit(solution)/shard_map/ppermute | solution.py:295
  51.8 1.3 %forward_dct.2 = (f32[32,640]{1,0:T(8,128)S(1)}, f32[128,640]{1,0:T(8,128)S(1)}, f32[16,5120]{1,0:T(8,128)S(1)}) custom-call(f32[2,8,1280]{2,1,0:T(8,128)S(1)} %get-tuple-element.77.refs_0_, f32[2,8,1280]{2,1,0:T(8,128)S(1)} %get-tuple-element.75.refs_1_, f32[2,8,2560]{2,1,0:T(8,128)S(1)} %get-tuple-element.73.refs_2_, ...), custom_call_target="tpu_custom_call" | custom-call | tf_op jit(solution)/shard_map/forward_dct/pallas_call | solution.py:157
  54.8 1.8 %collective-permute-start.23 = (f32[32,640]{1,0:T(8,128)S(1)}, f32[32,640]{1,0:T(8,128)S(1)}, u32[]{:S(2)}, u32[]{:S(2)}) collective-permute-start(f32[32,640]{1,0:T(8,128)S(1)} %get-tuple-element.55), channel_id=1, source_target_pairs={{0,16},{16,0},{32,48},{48,32},{64,80},{80,64},{96,112},{112,96},{1... | collective-permute-start | bytes 245768 | tf_op jit(solution)/shard_map/ppermute | solution.py:338
  57.1 1.3 %forward_dct.3 = (f32[32,640]{1,0:T(8,128)S(1)}, f32[128,640]{1,0:T(8,128)S(1)}, f32[16,5120]{1,0:T(8,128)S(1)}) custom-call(f32[2,8,2560]{2,1,0:T(8,128)S(1)} %get-tuple-element.71.refs_0_, f32[2,8,2560]{2,1,0:T(8,128)S(1)} %get-tuple-element.69.refs_1_, f32[2,8,2560]{2,1,0:T(8,128)S(1)} %collective-permute-done.15.refs_2_, ...), custom_call_target="tpu_custom_call" | custom-call | tf_op jit(solution)/shard_map/forward_dct/pallas_call | solution.py:157
  59.1 1.0 %collective-permute-start.19 = (f32[32,640]{1,0:T(8,128)S(1)}, f32[32,640]{1,0:T(8,128)S(1)}, u32[]{:S(2)}, u32[]{:S(2)}) collective-permute-start(f32[32,640]{1,0:T(8,128)S(1)} %get-tuple-element.54), channel_id=1, source_target_pairs={{0,144},{16,128},{32,176},{48,160},{64,208},{80,192},{96,240},{112... | collective-permute-start | bytes 245768 | tf_op jit(solution)/shard_map/ppermute | solution.py:338
  60.1 1.9 %collective-permute-start.17 = (f32[32,640]{1,0:T(8,128)S(1)}, f32[32,640]{1,0:T(8,128)S(1)}, u32[]{:S(2)}, u32[]{:S(2)}) collective-permute-start(f32[32,640]{1,0:T(8,128)S(1)} %get-tuple-element.54), channel_id=1, source_target_pairs={{0,16},{16,0},{32,48},{48,32},{64,80},{80,64},{96,112},{112,96},{1... | collective-permute-start | bytes 245768 | tf_op jit(solution)/shard_map/ppermute | solution.py:338
  62.0 5.9 %collective-permute-start.26 = (f32[32,640]{1,0:T(8,128)S(1)}, f32[32,640]{1,0:T(8,128)S(1)}, u32[]{:S(2)}, u32[]{:S(2)}) collective-permute-start(f32[32,640]{1,0:T(8,128)S(1)} %add_add_fusion.s0_ref), channel_id=1, source_target_pairs={{0,80},{16,64},{32,112},{48,96},{64,16},{80,0},{96,48},{112,32},{1... | collective-permute-start | bytes 245768 | tf_op jit(solution)/shard_map/ppermute | solution.py:340
  68.0 1.0 %collective-permute-start.27 = (f32[32,640]{1,0:T(8,128)S(1)}, f32[32,640]{1,0:T(8,128)S(1)}, u32[]{:S(2)}, u32[]{:S(2)}) collective-permute-start(f32[32,640]{1,0:T(8,128)S(1)} %add_add_fusion.s0_ref), channel_id=1, source_target_pairs={{0,112},{16,32},{32,16},{48,64},{64,48},{80,96},{96,80},{112,0},{1... | collective-permute-start | bytes 245768 | tf_op jit(solution)/shard_map/ppermute | solution.py:340
  69.5 4.2 %collective-permute-start.20 = (f32[32,640]{1,0:T(8,128)S(1)}, f32[32,640]{1,0:T(8,128)S(1)}, u32[]{:S(2)}, u32[]{:S(2)}) collective-permute-start(f32[32,640]{1,0:T(8,128)S(1)} %add_add_fusion.1.s0_ref), channel_id=1, source_target_pairs={{0,80},{16,64},{32,112},{48,96},{64,16},{80,0},{96,48},{112,32},{1... | collective-permute-start | bytes 245768 | tf_op jit(solution)/shard_map/ppermute | solution.py:340
  73.7 1.0 %collective-permute-start.21 = (f32[32,640]{1,0:T(8,128)S(1)}, f32[32,640]{1,0:T(8,128)S(1)}, u32[]{:S(2)}, u32[]{:S(2)}) collective-permute-start(f32[32,640]{1,0:T(8,128)S(1)} %add_add_fusion.1.s0_ref), channel_id=1, source_target_pairs={{0,112},{16,32},{32,16},{48,64},{64,48},{80,96},{96,80},{112,0},{1... | collective-permute-start | bytes 245768 | tf_op jit(solution)/shard_map/ppermute | solution.py:340
  75.2 1.6 %residual.1 = f32[4,8,5120]{2,1,0:T(8,128)} custom-call(f32[16,5120]{1,0:T(8,128)S(1)} %get-tuple-element.41.refs_0_, f32[16,5120]{1,0:T(8,128)S(1)} %get-tuple-element.51.refs_1_, f32[128,640]{1,0:T(8,128)S(1)} %get-tuple-element.52.refs_2_, f32[128,640]{1,0:T(8,128)S(1)} %get-tuple-element.53.refs_3_, f32[128,128]{1,0:T(8,128)S(1)} %copy-done.2), custom_call_target="tpu_custom_call" | custom-call | tf_op jit(solution)/shard_map/residual/pallas_call | solution.py:189
  76.8 1.6 %step_params.2.rest_0_ = f32[4,8,5120]{2,1,0:T(8,128)} custom-call(f32[4,8,5120]{2,1,0:T(8,128)S(1)} %copy-done.1, f32[32,640]{1,0:T(8,128)S(1)} %add_add_fusion.s0_ref, f32[32,640]{1,0:T(8,128)S(1)} %collective-permute-done.26.s1_ref, f32[32,640]{1,0:T(8,128)S(1)} %collective-permute-done.27.s2_ref, f32[32,640]{1,0:T(8,128)S(1)} %collective-permute-done.28.s3_ref, ...), custom_call_target="tpu_custom_call" | custom-call | tf_op jit(solution)/shard_map/step_params/pallas_call | solution.py:241
  78.4 1.1 %collective-permute-done.21.s2_ref = f32[32,640]{1,0:T(8,128)S(1)} collective-permute-done((f32[32,640]{1,0:T(8,128)S(1)}, f32[32,640]{1,0:T(8,128)S(1)}, u32[]{:S(2)}, u32[]{:S(2)}) %collective-permute-start.21) | collective-permute-done | bytes 81952 | tf_op jit(solution)/shard_map/ppermute | solution.py:340
  79.5 1.8 %collective-permute-done.22.s3_ref = f32[32,640]{1,0:T(8,128)S(1)} collective-permute-done((f32[32,640]{1,0:T(8,128)S(1)}, f32[32,640]{1,0:T(8,128)S(1)}, u32[]{:S(2)}, u32[]{:S(2)}) %collective-permute-start.22) | collective-permute-done | bytes 81952 | tf_op jit(solution)/shard_map/ppermute | solution.py:340
  81.3 1.6 %step_params.3 = f32[4,8,5120]{2,1,0:T(8,128)} custom-call(f32[4,8,5120]{2,1,0:T(8,128)S(1)} %copy-done.1, f32[32,640]{1,0:T(8,128)S(1)} %add_add_fusion.1.s0_ref, f32[32,640]{1,0:T(8,128)S(1)} %collective-permute-done.20.s1_ref, f32[32,640]{1,0:T(8,128)S(1)} %collective-permute-done.21.s2_ref, ...), custom_call_target="tpu_custom_call", output_to_operand_aliasing={{}: (7, {})} | custom-call | tf_op jit(solution)/shard_map/step_params/pallas_call | solution.py:241
  (72 shorter events, 9.2 us)
Async XLA Ops:
  2.5 5.0 %collective-permute-start = (f32[8,2,8,5120]{3,2,1,0:T(8,128)S(1)}, f32[8,2,8,5120]{3,2,1,0:T(8,128)S(1)}, u32[]{:S(2)}, u32[]{:S(2)}) collective-permute-start(f32[8,2,8,5120]{3,2,1,0:T(8,128)S(1)} %get-tuple-element.30), channel_id=1, source_target_pairs={{0,1},{1,0},{2,3},{3,2},{4,5},{5,4},{6,7},{7,6},{8,9},{9,8},{10,11... | collective-permute-start | bytes 7864328 | tf_op jit(solution)/shard_map/ppermute | solution.py:319
  4.4 10.7 %collective-permute-start.10 = (f32[8,2,8,5120]{3,2,1,0:T(8,128)S(1)}, f32[8,2,8,5120]{3,2,1,0:T(8,128)S(1)}, u32[]{:S(2)}, u32[]{:S(2)}) collective-permute-start(f32[8,2,8,5120]{3,2,1,0:T(8,128)S(1)} %get-tuple-element.43), channel_id=1, source_target_pairs={{0,1},{1,0},{2,3},{3,2},{4,5},{5,4},{6,7},{7,6},{8,9},{9,8},{10,11... | collective-permute-start | bytes 7864328 | tf_op jit(solution)/shard_map/ppermute | solution.py:319
  7.7 11.4 %collective-permute-start.1 = (f32[2,2,2,8,1280]{4,3,2,1,0:T(8,128)S(1)}, f32[2,2,2,8,1280]{4,3,2,1,0:T(8,128)S(1)}, u32[]{:S(2)}, u32[]{:S(2)}) collective-permute-start(f32[2,2,2,8,1280]{4,3,2,1,0:T(8,128)S(1)} %bitcast.99), channel_id=1, source_target_pairs={{0,8},{1,9},{2,10},{3,11},{4,12},{5,13},{6,14},{7,15},{8,0},{9,1},... | collective-permute-start | bytes 983048 | tf_op jit(solution)/shard_map/ppermute | solution.py:295
  11.1 10.7 %collective-permute-start.2 = (f32[2,2,2,8,1280]{4,3,2,0,1:T(8,128)S(1)}, f32[2,2,2,8,1280]{4,3,2,0,1:T(8,128)S(1)}, u32[]{:S(2)}, u32[]{:S(2)}) collective-permute-start(f32[2,2,2,8,1280]{4,3,2,0,1:T(8,128)S(1)} %bitcast.100), channel_id=1, source_target_pairs={{0,2},{1,3},{2,0},{3,1},{4,6},{5,7},{6,4},{7,5},{8,10},{9,11},{10,... | collective-permute-start | bytes 983048 | tf_op jit(solution)/shard_map/ppermute | solution.py:295
  12.9 17.5 %collective-permute-start.3 = (f32[2,2,2,8,2560]{4,3,2,1,0:T(8,128)S(1)}, f32[2,2,2,8,2560]{4,3,2,1,0:T(8,128)S(1)}, u32[]{:S(2)}, u32[]{:S(2)}) collective-permute-start(f32[2,2,2,8,2560]{4,3,2,1,0:T(8,128)S(1)} %slice_bitcast_fusion.1), channel_id=1, source_target_pairs={{0,6},{1,7},{2,4},{3,5},{4,2},{5,3},{6,0},{7,1},{8,14},{9,15},{10,... | collective-permute-start | bytes 1966088 | tf_op jit(solution)/shard_map/ppermute | solution.py:295
  15.5 17.9 %collective-permute-start.11 = (f32[2,2,2,8,2560]{4,3,2,1,0:T(8,128)S(1)}, f32[2,2,2,8,2560]{4,3,2,1,0:T(8,128)S(1)}, u32[]{:S(2)}, u32[]{:S(2)}) collective-permute-start(f32[2,2,2,8,2560]{4,3,2,1,0:T(8,128)S(1)} %bitcast.96), channel_id=1, source_target_pairs={{0,8},{1,9},{2,10},{3,11},{4,12},{5,13},{6,14},{7,15},{8,0},{9,1},... | collective-permute-start | bytes 1966088 | tf_op jit(solution)/shard_map/ppermute | solution.py:295
  16.1 19.7 %collective-permute-start.12 = (f32[2,2,2,8,2560]{4,3,2,0,1:T(8,128)S(1)}, f32[2,2,2,8,2560]{4,3,2,0,1:T(8,128)S(1)}, u32[]{:S(2)}, u32[]{:S(2)}) collective-permute-start(f32[2,2,2,8,2560]{4,3,2,0,1:T(8,128)S(1)} %bitcast.97), channel_id=1, source_target_pairs={{0,2},{1,3},{2,0},{3,1},{4,6},{5,7},{6,4},{7,5},{8,10},{9,11},{10,... | collective-permute-start | bytes 1966088 | tf_op jit(solution)/shard_map/ppermute | solution.py:295
  30.5 9.4 %collective-permute-start.4 = (f32[2,2,8,1280]{3,2,1,0:T(8,128)S(1)}, f32[2,2,8,1280]{3,2,1,0:T(8,128)S(1)}, u32[]{:S(2)}, u32[]{:S(2)}) collective-permute-start(f32[2,2,8,1280]{3,2,1,0:T(8,128)S(1)} %slice_bitcast_fusion.16), channel_id=1, source_target_pairs={{0,2},{1,3},{2,0},{3,1},{4,6},{5,7},{6,4},{7,5},{8,10},{9,11},{10,... | collective-permute-start | bytes 491528 | tf_op jit(solution)/shard_map/ppermute | solution.py:295
  30.6 9.2 %collective-permute-start.5 = (f32[2,2,8,1280]{3,2,1,0:T(8,128)S(1)}, f32[2,2,8,1280]{3,2,1,0:T(8,128)S(1)}, u32[]{:S(2)}, u32[]{:S(2)}) collective-permute-start(f32[2,2,8,1280]{3,2,1,0:T(8,128)S(1)} %slice_bitcast_fusion.15), channel_id=1, source_target_pairs={{0,6},{1,7},{2,4},{3,5},{4,2},{5,3},{6,0},{7,1},{8,14},{9,15},{10,... | collective-permute-start | bytes 491528 | tf_op jit(solution)/shard_map/ppermute | solution.py:295
  32.9 9.6 %collective-permute-start.6 = (f32[2,2,8,2560]{3,2,1,0:T(8,128)S(1)}, f32[2,2,8,2560]{3,2,1,0:T(8,128)S(1)}, u32[]{:S(2)}, u32[]{:S(2)}) collective-permute-start(f32[2,2,8,2560]{3,2,1,0:T(8,128)S(1)} %slice_bitcast_fusion.7), channel_id=1, source_target_pairs={{0,8},{1,9},{2,10},{3,11},{4,12},{5,13},{6,14},{7,15},{8,0},{9,1},... | collective-permute-start | bytes 983048 | tf_op jit(solution)/shard_map/ppermute | solution.py:295
  36.0 10.7 %collective-permute-start.13 = (f32[2,2,8,2560]{3,2,1,0:T(8,128)S(1)}, f32[2,2,8,2560]{3,2,1,0:T(8,128)S(1)}, u32[]{:S(2)}, u32[]{:S(2)}) collective-permute-start(f32[2,2,8,2560]{3,2,1,0:T(8,128)S(1)} %slice_bitcast_fusion.4), channel_id=1, source_target_pairs={{0,2},{1,3},{2,0},{3,1},{4,6},{5,7},{6,4},{7,5},{8,10},{9,11},{10,... | collective-permute-start | bytes 983048 | tf_op jit(solution)/shard_map/ppermute | solution.py:295
  37.7 9.4 %collective-permute-start.14 = (f32[2,2,8,2560]{3,2,1,0:T(8,128)S(1)}, f32[2,2,8,2560]{3,2,1,0:T(8,128)S(1)}, u32[]{:S(2)}, u32[]{:S(2)}) collective-permute-start(f32[2,2,8,2560]{3,2,1,0:T(8,128)S(1)} %slice_bitcast_fusion.3), channel_id=1, source_target_pairs={{0,6},{1,7},{2,4},{3,5},{4,2},{5,3},{6,0},{7,1},{8,14},{9,15},{10,... | collective-permute-start | bytes 983048 | tf_op jit(solution)/shard_map/ppermute | solution.py:295
  42.7 9.0 %collective-permute-start.7 = (f32[2,8,1280]{2,1,0:T(8,128)S(1)}, f32[2,8,1280]{2,1,0:T(8,128)S(1)}, u32[]{:S(2)}, u32[]{:S(2)}) collective-permute-start(f32[2,8,1280]{2,1,0:T(8,128)S(1)} %get-tuple-element.76), channel_id=1, source_target_pairs={{0,6},{1,7},{2,4},{3,5},{4,2},{5,3},{6,0},{7,1},{8,14},{9,15},{10,... | collective-permute-start | bytes 245768 | tf_op jit(solution)/shard_map/ppermute | solution.py:295
  43.9 7.7 %collective-permute-start.8 = (f32[2,8,1280]{2,1,0:T(8,128)S(1)}, f32[2,8,1280]{2,1,0:T(8,128)S(1)}, u32[]{:S(2)}, u32[]{:S(2)}) collective-permute-start(f32[2,8,1280]{2,1,0:T(8,128)S(1)} %get-tuple-element.74), channel_id=1, source_target_pairs={{0,8},{1,9},{2,10},{3,11},{4,12},{5,13},{6,14},{7,15},{8,0},{9,1},... | collective-permute-start | bytes 245768 | tf_op jit(solution)/shard_map/ppermute | solution.py:295
  46.4 5.3 %copy-start = (f32[1,4,8,5120]{3,2,1,0:T(8,128)S(1)}, f32[1,4,8,5120]{3,2,1,0:T(8,128)}, u32[]{:S(2)}) copy-start(f32[1,4,8,5120]{3,2,1,0:T(8,128)} %param.6) | copy-start | bytes 1966084
  46.4 5.3 %copy-start.2 = (f32[128,128]{1,0:T(8,128)S(1)}, f32[128,128]{1,0:T(8,128)}, u32[]{:S(2)}) copy-start(f32[128,128]{1,0:T(8,128)} %constant.2.clone.refs_8_.refs_6_.refs_4_.table_ref) | copy-start | bytes 196612
  46.4 5.3 %collective-permute-start.9 = (f32[2,8,2560]{2,1,0:T(8,128)S(1)}, f32[2,8,2560]{2,1,0:T(8,128)S(1)}, u32[]{:S(2)}, u32[]{:S(2)}) collective-permute-start(f32[2,8,2560]{2,1,0:T(8,128)S(1)} %get-tuple-element.72), channel_id=1, source_target_pairs={{0,2},{1,3},{2,0},{3,1},{4,6},{5,7},{6,4},{7,5},{8,10},{9,11},{10,... | collective-permute-start | bytes 491528 | tf_op jit(solution)/shard_map/ppermute | solution.py:295
  47.2 9.5 %collective-permute-start.15 = (f32[2,8,2560]{2,1,0:T(8,128)S(1)}, f32[2,8,2560]{2,1,0:T(8,128)S(1)}, u32[]{:S(2)}, u32[]{:S(2)}) collective-permute-start(f32[2,8,2560]{2,1,0:T(8,128)S(1)} %get-tuple-element.70), channel_id=1, source_target_pairs={{0,6},{1,7},{2,4},{3,5},{4,2},{5,3},{6,0},{7,1},{8,14},{9,15},{10,... | collective-permute-start | bytes 491528 | tf_op jit(solution)/shard_map/ppermute | solution.py:295
  49.4 7.8 %collective-permute-start.16 = (f32[2,8,2560]{2,1,0:T(8,128)S(1)}, f32[2,8,2560]{2,1,0:T(8,128)S(1)}, u32[]{:S(2)}, u32[]{:S(2)}) collective-permute-start(f32[2,8,2560]{2,1,0:T(8,128)S(1)} %get-tuple-element.68), channel_id=1, source_target_pairs={{0,8},{1,9},{2,10},{3,11},{4,12},{5,13},{6,14},{7,15},{8,0},{9,1},... | collective-permute-start | bytes 491528 | tf_op jit(solution)/shard_map/ppermute | solution.py:295
  53.0 7.0 %collective-permute-start.24 = (f32[32,640]{1,0:T(8,128)S(1)}, f32[32,640]{1,0:T(8,128)S(1)}, u32[]{:S(2)}, u32[]{:S(2)}) collective-permute-start(f32[32,640]{1,0:T(8,128)S(1)} %get-tuple-element.55), channel_id=1, source_target_pairs={{0,128},{16,144},{32,160},{48,176},{64,192},{80,208},{96,224},{112... | collective-permute-start | bytes 245768 | tf_op jit(solution)/shard_map/ppermute | solution.py:338
  53.9 8.1 %collective-permute-start.25 = (f32[32,640]{1,0:T(8,128)S(1)}, f32[32,640]{1,0:T(8,128)S(1)}, u32[]{:S(2)}, u32[]{:S(2)}) collective-permute-start(f32[32,640]{1,0:T(8,128)S(1)} %get-tuple-element.55), channel_id=1, source_target_pairs={{0,144},{16,128},{32,176},{48,160},{64,208},{80,192},{96,240},{112... | collective-permute-start | bytes 245768 | tf_op jit(solution)/shard_map/ppermute | solution.py:338
  54.8 7.2 %collective-permute-start.23 = (f32[32,640]{1,0:T(8,128)S(1)}, f32[32,640]{1,0:T(8,128)S(1)}, u32[]{:S(2)}, u32[]{:S(2)}) collective-permute-start(f32[32,640]{1,0:T(8,128)S(1)} %get-tuple-element.55), channel_id=1, source_target_pairs={{0,16},{16,0},{32,48},{48,32},{64,80},{80,64},{96,112},{112,96},{1... | collective-permute-start | bytes 245768 | tf_op jit(solution)/shard_map/ppermute | solution.py:338
  58.4 10.6 %collective-permute-start.18 = (f32[32,640]{1,0:T(8,128)S(1)}, f32[32,640]{1,0:T(8,128)S(1)}, u32[]{:S(2)}, u32[]{:S(2)}) collective-permute-start(f32[32,640]{1,0:T(8,128)S(1)} %get-tuple-element.54), channel_id=1, source_target_pairs={{0,128},{16,144},{32,160},{48,176},{64,192},{80,208},{96,224},{112... | collective-permute-start | bytes 245768 | tf_op jit(solution)/shard_map/ppermute | solution.py:338
  59.1 10.3 %collective-permute-start.19 = (f32[32,640]{1,0:T(8,128)S(1)}, f32[32,640]{1,0:T(8,128)S(1)}, u32[]{:S(2)}, u32[]{:S(2)}) collective-permute-start(f32[32,640]{1,0:T(8,128)S(1)} %get-tuple-element.54), channel_id=1, source_target_pairs={{0,144},{16,128},{32,176},{48,160},{64,208},{80,192},{96,240},{112... | collective-permute-start | bytes 245768 | tf_op jit(solution)/shard_map/ppermute | solution.py:338
  60.1 9.4 %collective-permute-start.17 = (f32[32,640]{1,0:T(8,128)S(1)}, f32[32,640]{1,0:T(8,128)S(1)}, u32[]{:S(2)}, u32[]{:S(2)}) collective-permute-start(f32[32,640]{1,0:T(8,128)S(1)} %get-tuple-element.54), channel_id=1, source_target_pairs={{0,16},{16,0},{32,48},{48,32},{64,80},{80,64},{96,112},{112,96},{1... | collective-permute-start | bytes 245768 | tf_op jit(solution)/shard_map/ppermute | solution.py:338
  62.0 14.8 %copy-start.1 = (f32[4,8,5120]{2,1,0:T(8,128)S(1)}, f32[4,8,5120]{2,1,0:T(8,128)}, u32[]{:S(2)}) copy-start(f32[4,8,5120]{2,1,0:T(8,128)} %params_ref.3) | copy-start | bytes 1966084
  62.0 12.7 %collective-permute-start.26 = (f32[32,640]{1,0:T(8,128)S(1)}, f32[32,640]{1,0:T(8,128)S(1)}, u32[]{:S(2)}, u32[]{:S(2)}) collective-permute-start(f32[32,640]{1,0:T(8,128)S(1)} %add_add_fusion.s0_ref), channel_id=1, source_target_pairs={{0,80},{16,64},{32,112},{48,96},{64,16},{80,0},{96,48},{112,32},{1... | collective-permute-start | bytes 245768 | tf_op jit(solution)/shard_map/ppermute | solution.py:340
  68.0 8.8 %collective-permute-start.27 = (f32[32,640]{1,0:T(8,128)S(1)}, f32[32,640]{1,0:T(8,128)S(1)}, u32[]{:S(2)}, u32[]{:S(2)}) collective-permute-start(f32[32,640]{1,0:T(8,128)S(1)} %add_add_fusion.s0_ref), channel_id=1, source_target_pairs={{0,112},{16,32},{32,16},{48,64},{64,48},{80,96},{96,80},{112,0},{1... | collective-permute-start | bytes 245768 | tf_op jit(solution)/shard_map/ppermute | solution.py:340
  69.0 7.8 %collective-permute-start.28 = (f32[32,640]{1,0:T(8,128)S(1)}, f32[32,640]{1,0:T(8,128)S(1)}, u32[]{:S(2)}, u32[]{:S(2)}) collective-permute-start(f32[32,640]{1,0:T(8,128)S(1)} %add_add_fusion.s0_ref), channel_id=1, source_target_pairs={{0,96},{16,48},{32,0},{48,80},{64,32},{80,112},{96,64},{112,16},{1... | collective-permute-start | bytes 245768 | tf_op jit(solution)/shard_map/ppermute | solution.py:340
  69.5 8.9 %collective-permute-start.20 = (f32[32,640]{1,0:T(8,128)S(1)}, f32[32,640]{1,0:T(8,128)S(1)}, u32[]{:S(2)}, u32[]{:S(2)}) collective-permute-start(f32[32,640]{1,0:T(8,128)S(1)} %add_add_fusion.1.s0_ref), channel_id=1, source_target_pairs={{0,80},{16,64},{32,112},{48,96},{64,16},{80,0},{96,48},{112,32},{1... | collective-permute-start | bytes 245768 | tf_op jit(solution)/shard_map/ppermute | solution.py:340
  73.7 5.8 %collective-permute-start.21 = (f32[32,640]{1,0:T(8,128)S(1)}, f32[32,640]{1,0:T(8,128)S(1)}, u32[]{:S(2)}, u32[]{:S(2)}) collective-permute-start(f32[32,640]{1,0:T(8,128)S(1)} %add_add_fusion.1.s0_ref), channel_id=1, source_target_pairs={{0,112},{16,32},{32,16},{48,64},{64,48},{80,96},{96,80},{112,0},{1... | collective-permute-start | bytes 245768 | tf_op jit(solution)/shard_map/ppermute | solution.py:340
  74.7 6.6 %collective-permute-start.22 = (f32[32,640]{1,0:T(8,128)S(1)}, f32[32,640]{1,0:T(8,128)S(1)}, u32[]{:S(2)}, u32[]{:S(2)}) collective-permute-start(f32[32,640]{1,0:T(8,128)S(1)} %add_add_fusion.1.s0_ref), channel_id=1, source_target_pairs={{0,96},{16,48},{32,0},{48,80},{64,32},{80,112},{96,64},{112,16},{1... | collective-permute-start | bytes 245768 | tf_op jit(solution)/shard_map/ppermute | solution.py:340
  (1 other events, 4.7 us)
